TPU v7x, 128 devices: a whole 4x4x4 slice. The times are simulated.
128 devices in a mesh: blk: 16 (over z_lo, x, core), narrow: 8 (over z_hi, y).
Axes of the slice: x: 4, y: 4, z: 4 (z_hi: 2, z_lo: 2; z = z_hi * 2 + z_lo), core: 2. Of those that a mesh axis runs over, the one named last changes fastest.
Arguments:
- queries: bfloat16 [512, 8192], P('blk'), may hold values from -181 to 181
- tree_key_cache: bfloat16 [64, 1024, 512], P('blk', 'narrow'), may hold values from -6.1 to 6.1
- tree_value_cache: bfloat16 [64, 1024, 512], P('blk', 'narrow'), may hold values from -8 to 8
- tree_mask: int32 [512, 64], P('blk'), may hold values from 0 to 1, as said below
- lengths: int32 [512], P('blk'), may hold values from 1 to 65536, as said below
- out_weight: bfloat16 [8192, 4096], P('blk', 'narrow'), may hold values from -0.0625 to 0.0625
- residual: bfloat16 [512, 4096], P('blk', 'narrow'), may hold values from -4 to 4
- norm_gain: float32 [4096], P('narrow'), may hold values from 0.1 to 1.9
- expert_ids: int32 [512, 8], P('blk'), may hold values from 0 to 63, all different within a row; in each aligned block of 32 rows (0 to 31, 32 to 63, ...) at most 6 rows name the same one
- gate_weights: float32 [512, 8], P('blk'), may hold values from 0.05 to 0.5
- gate_proj: bfloat16 [64, 4096, 1536], P('blk', 'narrow'), may hold values from -0.09375 to 0.09375
- up_proj: bfloat16 [64, 4096, 1536], P('blk', 'narrow'), may hold values from -0.09375 to 0.09375
- down_proj: bfloat16 [64, 1536, 4096], P('blk', None, 'narrow'), may hold values from -0.15625 to 0.15625
Outputs:
- mixed: bfloat16 [512, 4096], P('blk', 'narrow')
Inputs may be any that keep to these rules, and one draw needn't show every extreme that they name: `tree_mask`: block 0 is the root of a tree of 64 blocks in which every other block's parent has a smaller index; row b is 1 exactly on the path from the root to one block, branch b's deepest block. lengths[b] exceeds 1024 times the index of branch b's deepest block by 1 to 1024. `expert_ids`: the 8 entries of a row differ; among the 32 rows of one index of blk no expert is named more than 6 times.
All inputs are finite; a program needn't handle non-finite values.
Results may differ from a plain program's by a relative error of at most 0.025.
Values may be sent and summed in bfloat16 or wider, within the bound.
No kernel may reach another device: no remote copies, remote signals or barrier semaphores. Data moves between devices by JAX's collectives and lax.ppermute only.
A program may use at most 128 MiB of HBM per device.

v0:
```python
import jax
import jax.numpy as jnp
from jax import lax
from jax.sharding import PartitionSpec as P

D = 4096
QUERY_HEADS = 64
KEY_VALUE_HEADS = 4
HEAD_SIZE = 128
TOP = 8


NEGATIVE_FILLER = -1e30
EPSILON = 1e-06


def shifted(value, axis, by):
    length = lax.axis_size(axis)
    return lax.ppermute(value, axis, [(i, (i + by) % length) for i in range(length)])


def joined(value, axis, join):
    gathered = jax.tree.map(
        lambda a, kind: lax.all_gather(a.astype(kind), axis),
        value,
        jax.tree.map(lambda a: jnp.bfloat16 if a.dtype == jnp.float32 else a.dtype, value),
    )

    def take(source):
        return jax.tree.map(
            lambda a, own: lax.dynamic_index_in_dim(a, source, 0, False).astype(own.dtype),
            gathered,
            value,
        )

    return lax.fori_loop(
        1, lax.axis_size(axis), lambda source, state: join(state, take(source)), take(0)
    )


def combine(first_part, second_part):
    max_first, sum_first, acc_first = first_part
    max_second, sum_second, acc_second = second_part
    joint_max = jnp.maximum(max_first, max_second)
    scale_first = jnp.exp(max_first - joint_max)
    scale_second = jnp.exp(max_second - joint_max)
    joint_sum = sum_first * scale_first + sum_second * scale_second
    joint_acc = acc_first * scale_first[..., None] + acc_second * scale_second[..., None]
    return (joint_max, joint_sum, joint_acc)


def per_device(
    queries,
    tree_key_cache,
    tree_value_cache,
    tree_mask,
    lengths,
    out_weight,
    residual,
    norm_gain,
    expert_ids,
    gate_weights,
    gate_proj,
    up_proj,
    down_proj,
):
    count_of_rows = queries.shape[0]
    blocks_on_device = tree_key_cache.shape[0]
    block_token_span = tree_key_cache.shape[1]
    cycle_size = lax.axis_size("blk")
    narrow_size = lax.axis_size("narrow")
    my_cycle = lax.axis_index("blk")
    my_part = lax.axis_index("narrow")
    block_len = block_token_span * narrow_size
    heads_per_group = QUERY_HEADS // KEY_VALUE_HEADS
    query_head_rows = queries.reshape(count_of_rows, KEY_VALUE_HEADS, heads_per_group, HEAD_SIZE)
    score_scale = HEAD_SIZE ** (-0.5)
    local_tok = jnp.arange(blocks_on_device * block_token_span)
    tok_block = local_tok // block_token_span
    tok_offset = my_part * block_token_span + local_tok % block_token_span
    wo_rows = out_weight.shape[0]

    def absorb(run_state, key_portion, value_portion, source):
        block_ids = source * blocks_on_device + tok_block
        chosen = lax.dynamic_slice_in_dim(tree_mask, source * blocks_on_device, blocks_on_device, 1)
        readable = (jnp.repeat(chosen, block_token_span, axis=1) == 1) & (
            (block_ids * block_len + tok_offset)[None, :] < lengths[:, None]
        )
        live_mask = readable[:, None, None, :]
        flattened_keys = key_portion.reshape(
            blocks_on_device * block_token_span, KEY_VALUE_HEADS, HEAD_SIZE
        )
        flattened_values = value_portion.reshape(
            blocks_on_device * block_token_span, KEY_VALUE_HEADS, HEAD_SIZE
        )
        scores = (
            jnp.einsum(
                "rkgd,tkd->rkgt",
                query_head_rows,
                flattened_keys,
                preferred_element_type=jnp.float32,
            )
            * score_scale
        )
        scores = jnp.where(live_mask, scores, NEGATIVE_FILLER)
        run_max, run_sum, run_acc = run_state
        new_max = jnp.maximum(run_max, jnp.max(scores, axis=-1))
        weights = jnp.where(live_mask, jnp.exp(scores - new_max[..., None]), 0.0)
        rescale = jnp.exp(run_max - new_max)
        new_sum = run_sum * rescale + jnp.sum(weights, axis=-1)
        new_acc = run_acc * rescale[..., None] + jnp.einsum(
            "rkgt,tkd->rkgd",
            weights.astype(jnp.bfloat16),
            flattened_values,
            preferred_element_type=jnp.float32,
        )
        return (new_max, new_sum, new_acc)

    def take_piece(run_state, gathered, kv_piece, source):
        key_portion, value_portion, weight_piece = kv_piece
        run_state = absorb(run_state, key_portion, value_portion, source)
        gathered = lax.dynamic_update_slice_in_dim(gathered, weight_piece, source * wo_rows, 0)
        return (run_state, gathered)

    start_state = (
        jnp.full((count_of_rows, KEY_VALUE_HEADS, heads_per_group), NEGATIVE_FILLER, jnp.float32),
        jnp.zeros((count_of_rows, KEY_VALUE_HEADS, heads_per_group), jnp.float32),
        jnp.zeros((count_of_rows, KEY_VALUE_HEADS, heads_per_group, HEAD_SIZE), jnp.float32),
    )
    start_buffer = jnp.zeros((wo_rows * cycle_size, out_weight.shape[1]), jnp.bfloat16)
    own_piece = (tree_key_cache, tree_value_cache, out_weight)

    def one_turn(step_index, loop_carry):
        run_state, gathered, kv_piece = loop_carry
        run_state, gathered = take_piece(
            run_state, gathered, kv_piece, (my_cycle - step_index) % cycle_size
        )
        kv_piece = shifted((kv_piece[0], kv_piece[1], kv_piece[2]), "blk", 1)
        return (run_state, gathered, kv_piece)

    run_state, gathered, kv_piece = lax.fori_loop(
        0, cycle_size - 1, one_turn, (start_state, start_buffer, own_piece)
    )
    run_state, gathered = take_piece(
        run_state, gathered, kv_piece, (my_cycle - cycle_size + 1) % cycle_size
    )
    run_max, run_sum, run_acc = joined(run_state, "narrow", combine)
    attended = (
        (run_acc / run_sum[..., None])
        .reshape(count_of_rows, QUERY_HEADS * HEAD_SIZE)
        .astype(jnp.bfloat16)
    )
    projected = jnp.dot(attended, gathered, preferred_element_type=jnp.float32)
    hidden_b = (residual.astype(jnp.float32) + projected).astype(jnp.bfloat16)
    exp_dev = gate_proj.shape[0]
    n_experts = exp_dev * cycle_size
    capacity = max(2, 3 * count_of_rows * TOP // (2 * n_experts))
    flat_ids = expert_ids.reshape(-1)
    assign = flat_ids.shape[0]
    expert_hot = (flat_ids[:, None] == jnp.arange(n_experts)[None, :]).astype(jnp.int32)
    earlier = jnp.cumsum(expert_hot, axis=0) - expert_hot
    slot_of = jnp.sum(earlier * expert_hot, axis=1)
    target = flat_ids * capacity + slot_of
    placement = (jnp.arange(n_experts * capacity)[:, None] == target[None, :]).astype(jnp.bfloat16)
    owner_hot = (jnp.arange(assign)[:, None] // TOP == jnp.arange(count_of_rows)[None, :]).astype(
        jnp.bfloat16
    )
    select = jnp.dot(placement, owner_hot, preferred_element_type=jnp.float32).astype(jnp.bfloat16)
    outgoing = jnp.dot(select, hidden_b, preferred_element_type=jnp.float32).astype(jnp.bfloat16)
    outgoing = outgoing.reshape(cycle_size, exp_dev, capacity, hidden_b.shape[1])
    incoming = lax.all_to_all(outgoing, "blk", split_axis=0, concat_axis=2, tiled=True)[0]
    incoming_f = incoming.astype(jnp.float32)
    squares = jnp.sum(incoming_f * incoming_f, axis=-1)
    scaled = (incoming_f * norm_gain).astype(jnp.bfloat16)
    gate_part = jnp.einsum("esd,edf->esf", scaled, gate_proj, preferred_element_type=jnp.float32)
    up_part = jnp.einsum("esd,edf->esf", scaled, up_proj, preferred_element_type=jnp.float32)
    gate_sum, up_sum, square_sum = (
        lax.psum(gate_part.astype(jnp.bfloat16), "narrow").astype(jnp.float32),
        lax.psum(up_part.astype(jnp.bfloat16), "narrow").astype(jnp.float32),
        lax.psum(squares.astype(jnp.bfloat16), "narrow").astype(jnp.float32),
    )
    inv_rms = lax.rsqrt(square_sum / D + EPSILON)[..., None]
    activated = (jax.nn.silu(gate_sum * inv_rms) * (up_sum * inv_rms)).astype(jnp.bfloat16)
    expert_out = jnp.einsum(
        "esf,efd->esd", activated, down_proj, preferred_element_type=jnp.float32
    ).astype(jnp.bfloat16)
    expert_out = expert_out.reshape(exp_dev, cycle_size, capacity, expert_out.shape[2])
    returned = lax.all_to_all(expert_out, "blk", split_axis=1, concat_axis=0, tiled=True)
    returned = returned.reshape(n_experts * capacity, returned.shape[3])
    picked = returned[target].reshape(count_of_rows, TOP, returned.shape[1])
    mixed_in = jnp.sum(gate_weights[..., None] * picked.astype(jnp.float32), axis=1)
    return (hidden_b.astype(jnp.float32) + mixed_in).astype(jnp.bfloat16)


def solution(mesh):
    in_specs = (
        P("blk", None),
        P("blk", "narrow", None),
        P("blk", "narrow", None),
        P("blk", None),
        P("blk"),
        P("blk", "narrow"),
        P("blk", "narrow"),
        P("narrow"),
        P("blk", None),
        P("blk", None),
        P("blk", "narrow", None),
        P("blk", "narrow", None),
        P("blk", None, "narrow"),
    )
    out_specs = P("blk", "narrow")
    return jax.shard_map(
        per_device, mesh=mesh, in_specs=in_specs, out_specs=out_specs, check_vma=False
    )
```

profile of v0, /device:TPU:1, one launch (start us, length us, event | category | flops | bytes accessed | tf_op | source)
XLA Modules:
  0.0 622.4 jit_solution(5911888403788325652)
XLA Ops:
  6.5 1.9 copy.273
  15.4 3.8 broadcast_in_dim.124
  19.2 332.4 %while.48 = (s32[]{:T(128)}, f32[32,4,16]{0,2,1:T(8,128)S(1)}, f32[32,4,16]{0,2,1:T(8,128)S(1)}, f32[32,4,16,128]{3,2,0,1:T(8,128)}, bf16[8192,512]{1,0:T(8,128)...) while((s32[]{:T(128)}, f32[32,4,16]{0,2,1:T(8,128)S(1)}, ...), condition=%wide.region_3.4_spmd.clone, body=%wide.region_0.3_spmd.clone.sunk | while | flops 547145856 | bytes 29062564 | solution.py:141
  20.2 2.6 collective-permute-start
  34.1 3.5 fusion.111
  37.6 2.7 collective-permute-done.2
  41.3 2.5 collective-permute-start
  55.1 3.9 fusion.111
  58.9 2.3 collective-permute-done.2
  62.3 2.5 collective-permute-start
  76.1 3.9 fusion.111
  80.0 2.3 collective-permute-done.2
  83.3 2.5 collective-permute-start
  97.0 3.9 fusion.111
  100.9 2.3 collective-permute-done.2
  104.3 2.5 collective-permute-start
  116.2 1.9 constant_dynamic-update-slice_fusion.3
  118.1 3.9 fusion.111
  121.9 2.3 collective-permute-done.2
  125.3 2.5 collective-permute-start
  130.7 2.3 collective-permute-start.2
  139.7 3.9 fusion.111
  146.3 3.0 collective-permute-start
  152.2 3.9 collective-permute-start.2
  162.9 3.9 fusion.111
  167.8 4.6 collective-permute-start
  175.3 3.9 collective-permute-start.2
  185.9 3.9 fusion.111
  190.9 4.6 collective-permute-start
  198.4 3.9 collective-permute-start.2
  209.1 3.9 fusion.111
  214.0 4.5 collective-permute-start
  221.5 3.9 collective-permute-start.2
  232.1 3.9 fusion.111
  237.1 4.6 collective-permute-start
  244.6 3.9 collective-permute-start.2
  255.3 3.9 fusion.111
  260.2 4.6 collective-permute-start
  267.7 3.9 collective-permute-start.2
  278.3 3.9 fusion.111
  283.3 4.6 collective-permute-start
  290.8 3.9 collective-permute-start.2
  301.5 3.9 fusion.111
  306.4 4.6 collective-permute-start
  313.9 3.9 collective-permute-start.2
  324.5 3.9 fusion.111
  329.5 4.6 collective-permute-start
  337.0 3.9 collective-permute-start.2
  347.7 3.9 fusion.111
  354.1 2.4 fusion.33
  357.9 2.2 fusion.45
  360.5 29.4 %all-gather = bf16[256,4,16]{2,1,0:T(4,128)(2,1)S(1)} all-gather(bf16[32,4,16]{2,1,0:T(4,128)(2,1)S(1)} %copy.132), channel_id=2, replica_groups=mesh['blk'=16,'narrow'=8] {'narrow'}, dimensions={0}, use_global_device_ids=true | all-gather | bytes 36864 | tf_op jit(solution)/shard_map/all_gather | solution.py:24
  390.1 28.7 %all-gather.1 = bf16[256,4,16]{2,1,0:T(4,128)(2,1)S(1)} all-gather(bf16[32,4,16]{2,1,0:T(4,128)(2,1)S(1)} %copy.133), channel_id=3, replica_groups=mesh['blk'=16,'narrow'=8] {'narrow'}, dimensions={0}, use_global_device_ids=true | all-gather | bytes 36864 | tf_op jit(solution)/shard_map/all_gather | solution.py:24
  422.2 31.7 %all-gather.5.cloned.1.call-done = bf16[256,4,16,128]{3,0,2,1:T(8,128)(2,1)} async-done(((bf16[32,4,16,128]{3,0,2,1:T(8,128)(2,1)}), bf16[256,4,16,128]{3,0,2,1:T(8,128)(2,1)}) %all-gather.5.cloned.1.call-update) | async-done | bytes 4194320 | tf_op jit(solution)/shard_map/all_gather | solution.py:24
  455.7 16.3 %while.47 = (s32[]{:T(128)}, f32[32,4,16]{0,2,1:T(8,128)S(1)}, f32[32,4,16]{0,2,1:T(8,128)S(1)}, f32[32,4,16,128]{3,2,1,0:T(8,128)S(1)}, bf16[8,32,4,16]{1,3,2,0...) while((s32[]{:T(128)}, f32[32,4,16]{0,2,1:T(8,128)S(1)}, ...), condition=%wide.region_7.8_spmd, body=%wide.region_6.7_spmd.sunk | while | flops 1064965 | bytes 3776663 | solution.py:36
  472.4 4.7 fusion.50
  478.1 14.5 %all_to_all.24 = bf16[16,4,6,512]{3,1,2,0:T(4,128)(2,1)S(1)} all-to-all(bf16[16,4,6,512]{3,1,2,0:T(4,128)(2,1)S(1)} %copy.147), channel_id=1, replica_groups=mesh['blk'=16,'narrow'=8] {'blk'}, dimensions={0} | all-to-all | bytes 786432 | tf_op jit(solution)/shard_map/all_to_all | solution.py:171
  492.8 5.1 convolution_convert_fusion
  497.9 2.2 convolution_convert_fusion.1
  500.7 20.1 %psum.22 = bf16[4,96]{1,0:T(4,128)(2,1)S(1)} all-reduce(bf16[4,96]{1,0:T(4,128)(2,1)S(1)} %convert_element_type.197), channel_id=1, replica_groups=mesh['blk'=16,'narrow'=8] {'narrow'}, use_global_device_ids=true, to_apply=%region_13.14 | all-reduce | flops 384 | bytes 1536 | tf_op jit(solution)/shard_map/psum | solution.py:180
  520.8 69.0 %all-reduce.3.cloned.1.call-done = (bf16[4,96,1536]{2,1,0:T(8,128)(2,1)}, bf16[4,96,1536]{2,1,0:T(8,128)(2,1)}) async-done(((bf16[4,96,1536]{2,1,0:T(8,128)(2,1)}, bf16[4,96,1536]{2,1,0:T(8,128)(2,1)}), (bf16[4,96,1536]{2,1,0:T(8,128)(2,1)}, bf16[4,96,1536]{2,1,0:T(8,128)(2,1)})) %all-reduce.3.cloned.1.call-update) | async-done | bytes 2359312 | tf_op jit(solution)/shard_map/psum | solution.py:179
  589.8 4.7 convolution_convert_fusion.2
  595.6 9.4 %all-to-all-start.1 = ((bf16[4,16,6,512]{3,0,2,1:T(4,128)(2,1)}), bf16[4,16,6,512]{3,0,2,1:T(4,128)(2,1)S(1)}, u32[]{:S(2)}, u32[]{:S(2)}) async-start(bf16[4,16,6,512]{3,0,2,1:T(4,128)(2,1)} %bitcast.16), calls=%async_computation.1 | async-start | bytes 786432 | tf_op jit(solution)/shard_map/all_to_all | solution.py:188
  605.3 8.0 %all-to-all-done.1 = bf16[4,16,6,512]{3,0,2,1:T(4,128)(2,1)S(1)} async-done(((bf16[4,16,6,512]{3,0,2,1:T(4,128)(2,1)}), bf16[4,16,6,512]{3,0,2,1:T(4,128)(2,1)S(1)}, u32[]{:S(2)}, u32[]{:S(2)}) %all-to-all-start.1) | async-done | bytes 393248 | tf_op jit(solution)/shard_map/all_to_all | solution.py:188
  (419 shorter events, 205.5 us)
Async XLA Ops:
  6.5 8.8 %copy-start.1 = (s32[32,64]{1,0:T(8,128)S(1)}, s32[32,64]{1,0:T(8,128)}, u32[]{:S(2)}) copy-start(s32[32,64]{1,0:T(8,128)} %param.20) | copy-start | bytes 24580
  6.5 447.3 %all-gather.5.cloned.1.call-start = ((), (), s32[]{:S(2)}) async-start(), calls=%async_computation.2 | async-start | bytes 4718592 | tf_op jit(solution)/shard_map/all_gather | solution.py:24
  13.4 0.8 copy-start
  15.4 3.8 copy-start.4
  20.2 17.4 %collective-permute-start = (bf16[4,128,512]{2,1,0:T(8,128)(2,1)S(1)}, bf16[4,128,512]{2,1,0:T(8,128)(2,1)}, u32[]{:S(2)}, u32[]{:S(2)}) collective-permute-start(bf16[4,128,512]{2,1,0:T(8,128)(2,1)S(1)} %copy.244), channel_id=1, source_target_pairs={{0,8},{8,16},{16,24},{24,32},{32,40},{40,48},{48,56},{56,64},{64,7... | collective-permute-start | bytes 1572872 | tf_op jit(solution)/shard_map/while/body/eval_jaxpr/ppermute | solution.py:19
  23.9 13.8 %collective-permute-start.1 = (bf16[4,128,512]{2,1,0:T(8,128)(2,1)S(1)}, bf16[4,128,512]{2,1,0:T(8,128)(2,1)}, u32[]{:S(2)}, u32[]{:S(2)}) collective-permute-start(bf16[4,128,512]{2,1,0:T(8,128)(2,1)S(1)} %copy.245), channel_id=1, source_target_pairs={{0,8},{8,16},{16,24},{24,32},{32,40},{40,48},{48,56},{56,64},{64,7... | collective-permute-start | bytes 1572872 | tf_op jit(solution)/shard_map/while/body/eval_jaxpr/ppermute | solution.py:19
  25.7 14.6 %collective-permute-start.2 = (bf16[512,512]{1,0:T(8,128)(2,1)}, bf16[512,512]{1,0:T(8,128)(2,1)}, u32[]{:S(2)}, u32[]{:S(2)}) collective-permute-start(bf16[512,512]{1,0:T(8,128)(2,1)} %copy.246), channel_id=1, source_target_pairs={{0,8},{8,16},{16,24},{24,32},{32,40},{40,48},{48,56},{56,64},{64,7... | collective-permute-start | bytes 1572872 | tf_op jit(solution)/shard_map/while/body/eval_jaxpr/ppermute | solution.py:19
  41.3 17.6 %collective-permute-start = (bf16[4,128,512]{2,1,0:T(8,128)(2,1)S(1)}, bf16[4,128,512]{2,1,0:T(8,128)(2,1)}, u32[]{:S(2)}, u32[]{:S(2)}) collective-permute-start(bf16[4,128,512]{2,1,0:T(8,128)(2,1)S(1)} %copy.244), channel_id=1, source_target_pairs={{0,8},{8,16},{16,24},{24,32},{32,40},{40,48},{48,56},{56,64},{64,7... | collective-permute-start | bytes 1572872 | tf_op jit(solution)/shard_map/while/body/eval_jaxpr/ppermute | solution.py:19
  44.9 14.1 %collective-permute-start.1 = (bf16[4,128,512]{2,1,0:T(8,128)(2,1)S(1)}, bf16[4,128,512]{2,1,0:T(8,128)(2,1)}, u32[]{:S(2)}, u32[]{:S(2)}) collective-permute-start(bf16[4,128,512]{2,1,0:T(8,128)(2,1)S(1)} %copy.245), channel_id=1, source_target_pairs={{0,8},{8,16},{16,24},{24,32},{32,40},{40,48},{48,56},{56,64},{64,7... | collective-permute-start | bytes 1572872 | tf_op jit(solution)/shard_map/while/body/eval_jaxpr/ppermute | solution.py:19
  46.7 14.6 %collective-permute-start.2 = (bf16[512,512]{1,0:T(8,128)(2,1)}, bf16[512,512]{1,0:T(8,128)(2,1)}, u32[]{:S(2)}, u32[]{:S(2)}) collective-permute-start(bf16[512,512]{1,0:T(8,128)(2,1)} %copy.246), channel_id=1, source_target_pairs={{0,8},{8,16},{16,24},{24,32},{32,40},{40,48},{48,56},{56,64},{64,7... | collective-permute-start | bytes 1572872 | tf_op jit(solution)/shard_map/while/body/eval_jaxpr/ppermute | solution.py:19
  62.3 17.6 %collective-permute-start = (bf16[4,128,512]{2,1,0:T(8,128)(2,1)S(1)}, bf16[4,128,512]{2,1,0:T(8,128)(2,1)}, u32[]{:S(2)}, u32[]{:S(2)}) collective-permute-start(bf16[4,128,512]{2,1,0:T(8,128)(2,1)S(1)} %copy.244), channel_id=1, source_target_pairs={{0,8},{8,16},{16,24},{24,32},{32,40},{40,48},{48,56},{56,64},{64,7... | collective-permute-start | bytes 1572872 | tf_op jit(solution)/shard_map/while/body/eval_jaxpr/ppermute | solution.py:19
  65.9 14.1 %collective-permute-start.1 = (bf16[4,128,512]{2,1,0:T(8,128)(2,1)S(1)}, bf16[4,128,512]{2,1,0:T(8,128)(2,1)}, u32[]{:S(2)}, u32[]{:S(2)}) collective-permute-start(bf16[4,128,512]{2,1,0:T(8,128)(2,1)S(1)} %copy.245), channel_id=1, source_target_pairs={{0,8},{8,16},{16,24},{24,32},{32,40},{40,48},{48,56},{56,64},{64,7... | collective-permute-start | bytes 1572872 | tf_op jit(solution)/shard_map/while/body/eval_jaxpr/ppermute | solution.py:19
  67.7 14.6 %collective-permute-start.2 = (bf16[512,512]{1,0:T(8,128)(2,1)}, bf16[512,512]{1,0:T(8,128)(2,1)}, u32[]{:S(2)}, u32[]{:S(2)}) collective-permute-start(bf16[512,512]{1,0:T(8,128)(2,1)} %copy.246), channel_id=1, source_target_pairs={{0,8},{8,16},{16,24},{24,32},{32,40},{40,48},{48,56},{56,64},{64,7... | collective-permute-start | bytes 1572872 | tf_op jit(solution)/shard_map/while/body/eval_jaxpr/ppermute | solution.py:19
  83.3 17.6 %collective-permute-start = (bf16[4,128,512]{2,1,0:T(8,128)(2,1)S(1)}, bf16[4,128,512]{2,1,0:T(8,128)(2,1)}, u32[]{:S(2)}, u32[]{:S(2)}) collective-permute-start(bf16[4,128,512]{2,1,0:T(8,128)(2,1)S(1)} %copy.244), channel_id=1, source_target_pairs={{0,8},{8,16},{16,24},{24,32},{32,40},{40,48},{48,56},{56,64},{64,7... | collective-permute-start | bytes 1572872 | tf_op jit(solution)/shard_map/while/body/eval_jaxpr/ppermute | solution.py:19
  86.8 14.1 %collective-permute-start.1 = (bf16[4,128,512]{2,1,0:T(8,128)(2,1)S(1)}, bf16[4,128,512]{2,1,0:T(8,128)(2,1)}, u32[]{:S(2)}, u32[]{:S(2)}) collective-permute-start(bf16[4,128,512]{2,1,0:T(8,128)(2,1)S(1)} %copy.245), channel_id=1, source_target_pairs={{0,8},{8,16},{16,24},{24,32},{32,40},{40,48},{48,56},{56,64},{64,7... | collective-permute-start | bytes 1572872 | tf_op jit(solution)/shard_map/while/body/eval_jaxpr/ppermute | solution.py:19
  88.7 14.6 %collective-permute-start.2 = (bf16[512,512]{1,0:T(8,128)(2,1)}, bf16[512,512]{1,0:T(8,128)(2,1)}, u32[]{:S(2)}, u32[]{:S(2)}) collective-permute-start(bf16[512,512]{1,0:T(8,128)(2,1)} %copy.246), channel_id=1, source_target_pairs={{0,8},{8,16},{16,24},{24,32},{32,40},{40,48},{48,56},{56,64},{64,7... | collective-permute-start | bytes 1572872 | tf_op jit(solution)/shard_map/while/body/eval_jaxpr/ppermute | solution.py:19
  104.3 17.6 %collective-permute-start = (bf16[4,128,512]{2,1,0:T(8,128)(2,1)S(1)}, bf16[4,128,512]{2,1,0:T(8,128)(2,1)}, u32[]{:S(2)}, u32[]{:S(2)}) collective-permute-start(bf16[4,128,512]{2,1,0:T(8,128)(2,1)S(1)} %copy.244), channel_id=1, source_target_pairs={{0,8},{8,16},{16,24},{24,32},{32,40},{40,48},{48,56},{56,64},{64,7... | collective-permute-start | bytes 1572872 | tf_op jit(solution)/shard_map/while/body/eval_jaxpr/ppermute | solution.py:19
  107.8 14.1 %collective-permute-start.1 = (bf16[4,128,512]{2,1,0:T(8,128)(2,1)S(1)}, bf16[4,128,512]{2,1,0:T(8,128)(2,1)}, u32[]{:S(2)}, u32[]{:S(2)}) collective-permute-start(bf16[4,128,512]{2,1,0:T(8,128)(2,1)S(1)} %copy.245), channel_id=1, source_target_pairs={{0,8},{8,16},{16,24},{24,32},{32,40},{40,48},{48,56},{56,64},{64,7... | collective-permute-start | bytes 1572872 | tf_op jit(solution)/shard_map/while/body/eval_jaxpr/ppermute | solution.py:19
  109.7 14.6 %collective-permute-start.2 = (bf16[512,512]{1,0:T(8,128)(2,1)}, bf16[512,512]{1,0:T(8,128)(2,1)}, u32[]{:S(2)}, u32[]{:S(2)}) collective-permute-start(bf16[512,512]{1,0:T(8,128)(2,1)} %copy.246), channel_id=1, source_target_pairs={{0,8},{8,16},{16,24},{24,32},{32,40},{40,48},{48,56},{56,64},{64,7... | collective-permute-start | bytes 1572872 | tf_op jit(solution)/shard_map/while/body/eval_jaxpr/ppermute | solution.py:19
  125.3 18.3 %collective-permute-start = (bf16[4,128,512]{2,1,0:T(8,128)(2,1)S(1)}, bf16[4,128,512]{2,1,0:T(8,128)(2,1)}, u32[]{:S(2)}, u32[]{:S(2)}) collective-permute-start(bf16[4,128,512]{2,1,0:T(8,128)(2,1)S(1)} %copy.244), channel_id=1, source_target_pairs={{0,8},{8,16},{16,24},{24,32},{32,40},{40,48},{48,56},{56,64},{64,7... | collective-permute-start | bytes 1572872 | tf_op jit(solution)/shard_map/while/body/eval_jaxpr/ppermute | solution.py:19
  128.8 14.8 %collective-permute-start.1 = (bf16[4,128,512]{2,1,0:T(8,128)(2,1)S(1)}, bf16[4,128,512]{2,1,0:T(8,128)(2,1)}, u32[]{:S(2)}, u32[]{:S(2)}) collective-permute-start(bf16[4,128,512]{2,1,0:T(8,128)(2,1)S(1)} %copy.245), channel_id=1, source_target_pairs={{0,8},{8,16},{16,24},{24,32},{32,40},{40,48},{48,56},{56,64},{64,7... | collective-permute-start | bytes 1572872 | tf_op jit(solution)/shard_map/while/body/eval_jaxpr/ppermute | solution.py:19
  130.7 14.6 %collective-permute-start.2 = (bf16[512,512]{1,0:T(8,128)(2,1)}, bf16[512,512]{1,0:T(8,128)(2,1)}, u32[]{:S(2)}, u32[]{:S(2)}) collective-permute-start(bf16[512,512]{1,0:T(8,128)(2,1)} %copy.246), channel_id=1, source_target_pairs={{0,8},{8,16},{16,24},{24,32},{32,40},{40,48},{48,56},{56,64},{64,7... | collective-permute-start | bytes 1572872 | tf_op jit(solution)/shard_map/while/body/eval_jaxpr/ppermute | solution.py:19
  146.3 20.5 %collective-permute-start = (bf16[4,128,512]{2,1,0:T(8,128)(2,1)S(1)}, bf16[4,128,512]{2,1,0:T(8,128)(2,1)}, u32[]{:S(2)}, u32[]{:S(2)}) collective-permute-start(bf16[4,128,512]{2,1,0:T(8,128)(2,1)S(1)} %copy.244), channel_id=1, source_target_pairs={{0,8},{8,16},{16,24},{24,32},{32,40},{40,48},{48,56},{56,64},{64,7... | collective-permute-start | bytes 1572872 | tf_op jit(solution)/shard_map/while/body/eval_jaxpr/ppermute | solution.py:19
  150.4 16.4 %collective-permute-start.1 = (bf16[4,128,512]{2,1,0:T(8,128)(2,1)S(1)}, bf16[4,128,512]{2,1,0:T(8,128)(2,1)}, u32[]{:S(2)}, u32[]{:S(2)}) collective-permute-start(bf16[4,128,512]{2,1,0:T(8,128)(2,1)S(1)} %copy.245), channel_id=1, source_target_pairs={{0,8},{8,16},{16,24},{24,32},{32,40},{40,48},{48,56},{56,64},{64,7... | collective-permute-start | bytes 1572872 | tf_op jit(solution)/shard_map/while/body/eval_jaxpr/ppermute | solution.py:19
  152.2 14.6 %collective-permute-start.2 = (bf16[512,512]{1,0:T(8,128)(2,1)}, bf16[512,512]{1,0:T(8,128)(2,1)}, u32[]{:S(2)}, u32[]{:S(2)}) collective-permute-start(bf16[512,512]{1,0:T(8,128)(2,1)} %copy.246), channel_id=1, source_target_pairs={{0,8},{8,16},{16,24},{24,32},{32,40},{40,48},{48,56},{56,64},{64,7... | collective-permute-start | bytes 1572872 | tf_op jit(solution)/shard_map/while/body/eval_jaxpr/ppermute | solution.py:19
  167.8 22.0 %collective-permute-start = (bf16[4,128,512]{2,1,0:T(8,128)(2,1)S(1)}, bf16[4,128,512]{2,1,0:T(8,128)(2,1)}, u32[]{:S(2)}, u32[]{:S(2)}) collective-permute-start(bf16[4,128,512]{2,1,0:T(8,128)(2,1)S(1)} %copy.244), channel_id=1, source_target_pairs={{0,8},{8,16},{16,24},{24,32},{32,40},{40,48},{48,56},{56,64},{64,7... | collective-permute-start | bytes 1572872 | tf_op jit(solution)/shard_map/while/body/eval_jaxpr/ppermute | solution.py:19
  173.4 16.4 %collective-permute-start.1 = (bf16[4,128,512]{2,1,0:T(8,128)(2,1)S(1)}, bf16[4,128,512]{2,1,0:T(8,128)(2,1)}, u32[]{:S(2)}, u32[]{:S(2)}) collective-permute-start(bf16[4,128,512]{2,1,0:T(8,128)(2,1)S(1)} %copy.245), channel_id=1, source_target_pairs={{0,8},{8,16},{16,24},{24,32},{32,40},{40,48},{48,56},{56,64},{64,7... | collective-permute-start | bytes 1572872 | tf_op jit(solution)/shard_map/while/body/eval_jaxpr/ppermute | solution.py:19
  175.3 14.5 %collective-permute-start.2 = (bf16[512,512]{1,0:T(8,128)(2,1)}, bf16[512,512]{1,0:T(8,128)(2,1)}, u32[]{:S(2)}, u32[]{:S(2)}) collective-permute-start(bf16[512,512]{1,0:T(8,128)(2,1)} %copy.246), channel_id=1, source_target_pairs={{0,8},{8,16},{16,24},{24,32},{32,40},{40,48},{48,56},{56,64},{64,7... | collective-permute-start | bytes 1572872 | tf_op jit(solution)/shard_map/while/body/eval_jaxpr/ppermute | solution.py:19
  190.9 22.1 %collective-permute-start = (bf16[4,128,512]{2,1,0:T(8,128)(2,1)S(1)}, bf16[4,128,512]{2,1,0:T(8,128)(2,1)}, u32[]{:S(2)}, u32[]{:S(2)}) collective-permute-start(bf16[4,128,512]{2,1,0:T(8,128)(2,1)S(1)} %copy.244), channel_id=1, source_target_pairs={{0,8},{8,16},{16,24},{24,32},{32,40},{40,48},{48,56},{56,64},{64,7... | collective-permute-start | bytes 1572872 | tf_op jit(solution)/shard_map/while/body/eval_jaxpr/ppermute | solution.py:19
  196.5 16.4 %collective-permute-start.1 = (bf16[4,128,512]{2,1,0:T(8,128)(2,1)S(1)}, bf16[4,128,512]{2,1,0:T(8,128)(2,1)}, u32[]{:S(2)}, u32[]{:S(2)}) collective-permute-start(bf16[4,128,512]{2,1,0:T(8,128)(2,1)S(1)} %copy.245), channel_id=1, source_target_pairs={{0,8},{8,16},{16,24},{24,32},{32,40},{40,48},{48,56},{56,64},{64,7... | collective-permute-start | bytes 1572872 | tf_op jit(solution)/shard_map/while/body/eval_jaxpr/ppermute | solution.py:19
  198.4 14.6 %collective-permute-start.2 = (bf16[512,512]{1,0:T(8,128)(2,1)}, bf16[512,512]{1,0:T(8,128)(2,1)}, u32[]{:S(2)}, u32[]{:S(2)}) collective-permute-start(bf16[512,512]{1,0:T(8,128)(2,1)} %copy.246), channel_id=1, source_target_pairs={{0,8},{8,16},{16,24},{24,32},{32,40},{40,48},{48,56},{56,64},{64,7... | collective-permute-start | bytes 1572872 | tf_op jit(solution)/shard_map/while/body/eval_jaxpr/ppermute | solution.py:19
  214.0 22.0 %collective-permute-start = (bf16[4,128,512]{2,1,0:T(8,128)(2,1)S(1)}, bf16[4,128,512]{2,1,0:T(8,128)(2,1)}, u32[]{:S(2)}, u32[]{:S(2)}) collective-permute-start(bf16[4,128,512]{2,1,0:T(8,128)(2,1)S(1)} %copy.244), channel_id=1, source_target_pairs={{0,8},{8,16},{16,24},{24,32},{32,40},{40,48},{48,56},{56,64},{64,7... | collective-permute-start | bytes 1572872 | tf_op jit(solution)/shard_map/while/body/eval_jaxpr/ppermute | solution.py:19
  219.6 16.4 %collective-permute-start.1 = (bf16[4,128,512]{2,1,0:T(8,128)(2,1)S(1)}, bf16[4,128,512]{2,1,0:T(8,128)(2,1)}, u32[]{:S(2)}, u32[]{:S(2)}) collective-permute-start(bf16[4,128,512]{2,1,0:T(8,128)(2,1)S(1)} %copy.245), channel_id=1, source_target_pairs={{0,8},{8,16},{16,24},{24,32},{32,40},{40,48},{48,56},{56,64},{64,7... | collective-permute-start | bytes 1572872 | tf_op jit(solution)/shard_map/while/body/eval_jaxpr/ppermute | solution.py:19
  221.5 14.5 %collective-permute-start.2 = (bf16[512,512]{1,0:T(8,128)(2,1)}, bf16[512,512]{1,0:T(8,128)(2,1)}, u32[]{:S(2)}, u32[]{:S(2)}) collective-permute-start(bf16[512,512]{1,0:T(8,128)(2,1)} %copy.246), channel_id=1, source_target_pairs={{0,8},{8,16},{16,24},{24,32},{32,40},{40,48},{48,56},{56,64},{64,7... | collective-permute-start | bytes 1572872 | tf_op jit(solution)/shard_map/while/body/eval_jaxpr/ppermute | solution.py:19
  237.1 22.1 %collective-permute-start = (bf16[4,128,512]{2,1,0:T(8,128)(2,1)S(1)}, bf16[4,128,512]{2,1,0:T(8,128)(2,1)}, u32[]{:S(2)}, u32[]{:S(2)}) collective-permute-start(bf16[4,128,512]{2,1,0:T(8,128)(2,1)S(1)} %copy.244), channel_id=1, source_target_pairs={{0,8},{8,16},{16,24},{24,32},{32,40},{40,48},{48,56},{56,64},{64,7... | collective-permute-start | bytes 1572872 | tf_op jit(solution)/shard_map/while/body/eval_jaxpr/ppermute | solution.py:19
  242.8 16.4 %collective-permute-start.1 = (bf16[4,128,512]{2,1,0:T(8,128)(2,1)S(1)}, bf16[4,128,512]{2,1,0:T(8,128)(2,1)}, u32[]{:S(2)}, u32[]{:S(2)}) collective-permute-start(bf16[4,128,512]{2,1,0:T(8,128)(2,1)S(1)} %copy.245), channel_id=1, source_target_pairs={{0,8},{8,16},{16,24},{24,32},{32,40},{40,48},{48,56},{56,64},{64,7... | collective-permute-start | bytes 1572872 | tf_op jit(solution)/shard_map/while/body/eval_jaxpr/ppermute | solution.py:19
  244.6 14.6 %collective-permute-start.2 = (bf16[512,512]{1,0:T(8,128)(2,1)}, bf16[512,512]{1,0:T(8,128)(2,1)}, u32[]{:S(2)}, u32[]{:S(2)}) collective-permute-start(bf16[512,512]{1,0:T(8,128)(2,1)} %copy.246), channel_id=1, source_target_pairs={{0,8},{8,16},{16,24},{24,32},{32,40},{40,48},{48,56},{56,64},{64,7... | collective-permute-start | bytes 1572872 | tf_op jit(solution)/shard_map/while/body/eval_jaxpr/ppermute | solution.py:19
  260.2 22.0 %collective-permute-start = (bf16[4,128,512]{2,1,0:T(8,128)(2,1)S(1)}, bf16[4,128,512]{2,1,0:T(8,128)(2,1)}, u32[]{:S(2)}, u32[]{:S(2)}) collective-permute-start(bf16[4,128,512]{2,1,0:T(8,128)(2,1)S(1)} %copy.244), channel_id=1, source_target_pairs={{0,8},{8,16},{16,24},{24,32},{32,40},{40,48},{48,56},{56,64},{64,7... | collective-permute-start | bytes 1572872 | tf_op jit(solution)/shard_map/while/body/eval_jaxpr/ppermute | solution.py:19
  265.8 16.4 %collective-permute-start.1 = (bf16[4,128,512]{2,1,0:T(8,128)(2,1)S(1)}, bf16[4,128,512]{2,1,0:T(8,128)(2,1)}, u32[]{:S(2)}, u32[]{:S(2)}) collective-permute-start(bf16[4,128,512]{2,1,0:T(8,128)(2,1)S(1)} %copy.245), channel_id=1, source_target_pairs={{0,8},{8,16},{16,24},{24,32},{32,40},{40,48},{48,56},{56,64},{64,7... | collective-permute-start | bytes 1572872 | tf_op jit(solution)/shard_map/while/body/eval_jaxpr/ppermute | solution.py:19
  267.7 14.5 %collective-permute-start.2 = (bf16[512,512]{1,0:T(8,128)(2,1)}, bf16[512,512]{1,0:T(8,128)(2,1)}, u32[]{:S(2)}, u32[]{:S(2)}) collective-permute-start(bf16[512,512]{1,0:T(8,128)(2,1)} %copy.246), channel_id=1, source_target_pairs={{0,8},{8,16},{16,24},{24,32},{32,40},{40,48},{48,56},{56,64},{64,7... | collective-permute-start | bytes 1572872 | tf_op jit(solution)/shard_map/while/body/eval_jaxpr/ppermute | solution.py:19
  283.3 22.1 %collective-permute-start = (bf16[4,128,512]{2,1,0:T(8,128)(2,1)S(1)}, bf16[4,128,512]{2,1,0:T(8,128)(2,1)}, u32[]{:S(2)}, u32[]{:S(2)}) collective-permute-start(bf16[4,128,512]{2,1,0:T(8,128)(2,1)S(1)} %copy.244), channel_id=1, source_target_pairs={{0,8},{8,16},{16,24},{24,32},{32,40},{40,48},{48,56},{56,64},{64,7... | collective-permute-start | bytes 1572872 | tf_op jit(solution)/shard_map/while/body/eval_jaxpr/ppermute | solution.py:19
  288.9 16.4 %collective-permute-start.1 = (bf16[4,128,512]{2,1,0:T(8,128)(2,1)S(1)}, bf16[4,128,512]{2,1,0:T(8,128)(2,1)}, u32[]{:S(2)}, u32[]{:S(2)}) collective-permute-start(bf16[4,128,512]{2,1,0:T(8,128)(2,1)S(1)} %copy.245), channel_id=1, source_target_pairs={{0,8},{8,16},{16,24},{24,32},{32,40},{40,48},{48,56},{56,64},{64,7... | collective-permute-start | bytes 1572872 | tf_op jit(solution)/shard_map/while/body/eval_jaxpr/ppermute | solution.py:19
  290.8 14.6 %collective-permute-start.2 = (bf16[512,512]{1,0:T(8,128)(2,1)}, bf16[512,512]{1,0:T(8,128)(2,1)}, u32[]{:S(2)}, u32[]{:S(2)}) collective-permute-start(bf16[512,512]{1,0:T(8,128)(2,1)} %copy.246), channel_id=1, source_target_pairs={{0,8},{8,16},{16,24},{24,32},{32,40},{40,48},{48,56},{56,64},{64,7... | collective-permute-start | bytes 1572872 | tf_op jit(solution)/shard_map/while/body/eval_jaxpr/ppermute | solution.py:19
  306.4 22.0 %collective-permute-start = (bf16[4,128,512]{2,1,0:T(8,128)(2,1)S(1)}, bf16[4,128,512]{2,1,0:T(8,128)(2,1)}, u32[]{:S(2)}, u32[]{:S(2)}) collective-permute-start(bf16[4,128,512]{2,1,0:T(8,128)(2,1)S(1)} %copy.244), channel_id=1, source_target_pairs={{0,8},{8,16},{16,24},{24,32},{32,40},{40,48},{48,56},{56,64},{64,7... | collective-permute-start | bytes 1572872 | tf_op jit(solution)/shard_map/while/body/eval_jaxpr/ppermute | solution.py:19
  312.0 16.4 %collective-permute-start.1 = (bf16[4,128,512]{2,1,0:T(8,128)(2,1)S(1)}, bf16[4,128,512]{2,1,0:T(8,128)(2,1)}, u32[]{:S(2)}, u32[]{:S(2)}) collective-permute-start(bf16[4,128,512]{2,1,0:T(8,128)(2,1)S(1)} %copy.245), channel_id=1, source_target_pairs={{0,8},{8,16},{16,24},{24,32},{32,40},{40,48},{48,56},{56,64},{64,7... | collective-permute-start | bytes 1572872 | tf_op jit(solution)/shard_map/while/body/eval_jaxpr/ppermute | solution.py:19
  313.9 14.5 %collective-permute-start.2 = (bf16[512,512]{1,0:T(8,128)(2,1)}, bf16[512,512]{1,0:T(8,128)(2,1)}, u32[]{:S(2)}, u32[]{:S(2)}) collective-permute-start(bf16[512,512]{1,0:T(8,128)(2,1)} %copy.246), channel_id=1, source_target_pairs={{0,8},{8,16},{16,24},{24,32},{32,40},{40,48},{48,56},{56,64},{64,7... | collective-permute-start | bytes 1572872 | tf_op jit(solution)/shard_map/while/body/eval_jaxpr/ppermute | solution.py:19
  329.5 22.1 %collective-permute-start = (bf16[4,128,512]{2,1,0:T(8,128)(2,1)S(1)}, bf16[4,128,512]{2,1,0:T(8,128)(2,1)}, u32[]{:S(2)}, u32[]{:S(2)}) collective-permute-start(bf16[4,128,512]{2,1,0:T(8,128)(2,1)S(1)} %copy.244), channel_id=1, source_target_pairs={{0,8},{8,16},{16,24},{24,32},{32,40},{40,48},{48,56},{56,64},{64,7... | collective-permute-start | bytes 1572872 | tf_op jit(solution)/shard_map/while/body/eval_jaxpr/ppermute | solution.py:19
  335.2 16.4 %collective-permute-start.1 = (bf16[4,128,512]{2,1,0:T(8,128)(2,1)S(1)}, bf16[4,128,512]{2,1,0:T(8,128)(2,1)}, u32[]{:S(2)}, u32[]{:S(2)}) collective-permute-start(bf16[4,128,512]{2,1,0:T(8,128)(2,1)S(1)} %copy.245), channel_id=1, source_target_pairs={{0,8},{8,16},{16,24},{24,32},{32,40},{40,48},{48,56},{56,64},{64,7... | collective-permute-start | bytes 1572872 | tf_op jit(solution)/shard_map/while/body/eval_jaxpr/ppermute | solution.py:19
  337.0 14.6 %collective-permute-start.2 = (bf16[512,512]{1,0:T(8,128)(2,1)}, bf16[512,512]{1,0:T(8,128)(2,1)}, u32[]{:S(2)}, u32[]{:S(2)}) collective-permute-start(bf16[512,512]{1,0:T(8,128)(2,1)} %copy.246), channel_id=1, source_target_pairs={{0,8},{8,16},{16,24},{24,32},{32,40},{40,48},{48,56},{56,64},{64,7... | collective-permute-start | bytes 1572872 | tf_op jit(solution)/shard_map/while/body/eval_jaxpr/ppermute | solution.py:19
  354.1 3.7 copy-start.7
  357.9 2.3 copy-start.5
  360.1 229.7 %all-reduce.3.cloned.1.call-start = ((), (), s32[]{:S(2)}) async-start(), calls=%async_computation.3 | async-start | bytes 4718592 | tf_op jit(solution)/shard_map/psum | solution.py:179
  455.6 16.7 %copy-start.3 = (bf16[32,512]{1,0:T(8,128)(2,1)S(1)}, bf16[32,512]{1,0:T(8,128)(2,1)}, u32[]{:S(2)}) copy-start(bf16[32,512]{1,0:T(8,128)(2,1)} %param.23) | copy-start | bytes 98308
  477.1 15.6 %copy-start.2 = (f32[512]{0:T(512)S(1)}, f32[512]{0:T(512)}, u32[]{:S(2)}) copy-start(f32[512]{0:T(512)} %param.24) | copy-start | bytes 6148
  477.7 20.2 %slice-start = ((s8[6291456]{0:T(1024)(128)(4,1)}), s8[2097152]{0:T(1024)(128)(4,1)S(1)}, s32[]{:S(2)}) async-start(s8[6291456]{0:T(1024)(128)(4,1)} %bitcast.138), calls=%async_computation.4 | async-start | bytes 4194304
  492.8 5.1 slice-start.1
  589.8 15.4 %copy-start.6 = (f32[32,8]{0,1:T(8,128)S(1)}, f32[32,8]{0,1:T(8,128)}, u32[]{:S(2)}) copy-start(f32[32,8]{0,1:T(8,128)} %param.26) | copy-start | bytes 3076
  595.6 17.7 %all-to-all-start.1 = ((bf16[4,16,6,512]{3,0,2,1:T(4,128)(2,1)}), bf16[4,16,6,512]{3,0,2,1:T(4,128)(2,1)S(1)}, u32[]{:S(2)}, u32[]{:S(2)}) async-start(bf16[4,16,6,512]{3,0,2,1:T(4,128)(2,1)} %bitcast.16), calls=%async_computation.1 | async-start | bytes 786432 | tf_op jit(solution)/shard_map/all_to_all | solution.py:188
Sparse Core Ops, SparseCore 0:
  360.2 93.5 all-gather.4
  500.2 89.5 all-reduce.2
where the time goes:
time: 627 us; the launch traced here: 622 us
  local copies, waits for them, and re-layouts  137 us (22%)
  waiting for transfers between devices  123 us (20%)
  starting transfers between devices  110 us (18%)
  matrix products  108 us (17%)
  blocking collectives  92.6 us (15%)
  other arithmetic  37.4 us (6%)
  between operations  13.7 us (2%)
    ppermute x45, starting transfers between devices, shifted(): lax.ppermute(value, axis, [(i, (i + by) % length) for i in range(length)])  100 us
    psum x1, waiting for transfers between devices, per_device(): lax.psum(up_part.astype(jnp.bfloat16), 'narrow').astype(jnp.float32)  69 us
    dot_general x16, matrix products, absorb(): jnp.einsum('rkgt,tkd->rkgd', weights.astype(jnp.bfloat16), flattened_valu...  60 us
    while x60, local copies, waits for them, and re-layouts  59.3 us
    all_gather x2, blocking collectives, joined(): lax.all_gather(a.astype(kind), axis)  58.1 us
    all_gather x1, waiting for transfers between devices, joined(): lax.all_gather(a.astype(kind), axis)  31.7 us
    dot_general x16, matrix products, absorb(): jnp.einsum('rkgd,tkd->rkgt', query_head_rows, flattened_keys, preferred_e...  30.3 us
    dynamic_update_slice x16, local copies, waits for them, and re-layouts, take_piece(): lax.dynamic_update_slice_in_dim(gathered, weight_piece, source * wo_rows, 0)  30.2 us
  transfers between devices with their start and end apart: 48, of which 9 were waited for; matrix products, arithmetic and copies ran while one was open for 33% of the time, Pallas kernels for 0%

commit v1 on v0

v1 whole, which is shorter than its diff:
```python
import functools

import jax
import jax.numpy as jnp
from jax import lax
from jax.experimental import pallas as pl
from jax.experimental.pallas import tpu as pltpu
from jax.sharding import PartitionSpec as P

D = 4096
QUERY_HEADS = 64
KEY_VALUE_HEADS = 4
HEAD_SIZE = 128
FF = 1536
TOP = 8
CAP = 6
BLOCK_TOKENS = 1024
TREE_BLOCKS = 64
NEGATIVE_FILLER = -1e30
EPSILON = 1e-06
SCORE_SCALE = HEAD_SIZE ** (-0.5)
LOG2E = 1.4426950408889634
LANES = 128
VMEM_LIMIT = 56 * 1024 * 1024


def params(*semantics):
    return pltpu.CompilerParams(dimension_semantics=semantics, vmem_limit_bytes=VMEM_LIMIT)


def split_bf16(value):
    high = value.astype(jnp.bfloat16)
    rest = value - high.astype(jnp.float32)
    mid = rest.astype(jnp.bfloat16)
    low = (rest - mid.astype(jnp.float32)).astype(jnp.bfloat16)
    return high, mid, low


def gather_by_exchange(value, axis):
    length = lax.axis_size(axis)
    spread = jnp.broadcast_to(value[None], (length,) + value.shape)
    return lax.all_to_all(spread, axis, 0, 0)


def attention_kernel(heads, blocks, q_ref, lim_ref, kv_ref, out_ref, kt_ref, v_ref, s_ref):
    rows = q_ref.shape[0]
    parts = kv_ref.shape[0]

    @pl.when(pl.program_id(0) == 0)
    def _():
        lane = lax.broadcasted_iota(jnp.int32, (BLOCK_TOKENS, HEAD_SIZE), 1)
        ones = jnp.where(lane == 0, 1.0, 0.0).astype(jnp.bfloat16)
        for i in range(blocks):
            span = pl.ds(i * BLOCK_TOKENS, BLOCK_TOKENS)
            keys = kv_ref[:, 0, i].reshape(BLOCK_TOKENS, HEAD_SIZE)
            kt_ref[:, span] = keys.T
            v_ref[span, :HEAD_SIZE] = kv_ref[:, 1, i].reshape(BLOCK_TOKENS, HEAD_SIZE)
            v_ref[span, HEAD_SIZE:] = ones

    token = lax.broadcasted_iota(jnp.int32, (rows, BLOCK_TOKENS), 1)
    lane_row = lax.broadcasted_iota(jnp.int32, (rows, LANES), 1)

    def one_head(h, info):
        cols = pl.ds(pl.multiple_of(h * HEAD_SIZE, HEAD_SIZE), HEAD_SIZE)
        q = q_ref[:, cols]
        top = jnp.full((rows, 1), -1e29, jnp.float32)
        for i in range(blocks):
            span = pl.ds(i * BLOCK_TOKENS, BLOCK_TOKENS)
            s = jnp.dot(q, kt_ref[:, span], preferred_element_type=jnp.float32)
            s = jnp.where(token < lim_ref[:, i : i + 1], s, NEGATIVE_FILLER)
            s_ref[:, span] = s
            top = jnp.maximum(top, jnp.max(s, axis=1, keepdims=True))
        acc = jnp.zeros((rows, 2 * HEAD_SIZE), jnp.float32)
        for i in range(blocks):
            span = pl.ds(i * BLOCK_TOKENS, BLOCK_TOKENS)
            p = jnp.exp2((s_ref[:, span] - top) * (SCORE_SCALE * LOG2E)).astype(jnp.bfloat16)
            acc = acc + jnp.dot(p, v_ref[span, :], preferred_element_type=jnp.float32)
        total = acc[:, HEAD_SIZE : HEAD_SIZE + 1]
        some = total > 0
        safe = jnp.where(some, total, 1.0)
        out_ref[:, cols] = (acc[:, :HEAD_SIZE] / safe).astype(jnp.bfloat16)
        lse = jnp.where(some, top * SCORE_SCALE + jnp.log(safe), NEGATIVE_FILLER)
        return jnp.where(lane_row == h, lse, info)

    info = lax.fori_loop(0, heads, one_head, jnp.zeros((rows, LANES), jnp.float32))
    high, mid, low = split_bf16(info[:, :heads])
    base = heads * HEAD_SIZE
    out_ref[:, base:] = jnp.zeros((rows, LANES), jnp.bfloat16)
    out_ref[:, base : base + heads] = high
    out_ref[:, base + heads : base + 2 * heads] = mid
    out_ref[:, base + 2 * heads : base + 3 * heads] = low


def attention(queries, limits, kv):
    total_rows, width = queries.shape
    heads = width // HEAD_SIZE
    blocks = kv.shape[2]
    rows = 256
    tokens = blocks * BLOCK_TOKENS
    return pl.pallas_call(
        functools.partial(attention_kernel, heads, blocks),
        grid=(total_rows // rows,),
        in_specs=[
            pl.BlockSpec((rows, width), lambda r: (r, 0)),
            pl.BlockSpec((rows, blocks), lambda r: (r, 0)),
            pl.BlockSpec(kv.shape, lambda r: (0, 0, 0, 0, 0)),
        ],
        out_specs=pl.BlockSpec((rows, width + LANES), lambda r: (r, 0)),
        out_shape=jax.ShapeDtypeStruct((total_rows, width + LANES), jnp.bfloat16),
        scratch_shapes=[
            pltpu.VMEM((HEAD_SIZE, tokens), jnp.bfloat16),
            pltpu.VMEM((tokens, 2 * HEAD_SIZE), jnp.bfloat16),
            pltpu.VMEM((rows, tokens), jnp.float32),
        ],
        compiler_params=params("arbitrary"),
        cost_estimate=pl.CostEstimate(
            flops=6 * total_rows * heads * tokens * HEAD_SIZE,
            bytes_accessed=6 << 20,
            transcendentals=total_rows * heads * tokens,
        ),
        name="attention",
    )(queries, limits, kv)


def combine_kernel(heads, x_ref, out_ref):
    base = heads * HEAD_SIZE
    info = x_ref[:, :, base:].astype(jnp.float32)
    half = out_ref.shape[2] // HEAD_SIZE
    for h in range(heads):
        lse = info[:, :, h : h + 1] + info[:, :, heads + h : heads + h + 1]
        lse = lse + info[:, :, 2 * heads + h : 2 * heads + h + 1]
        scale = jnp.exp(lse - jnp.max(lse, axis=0, keepdims=True))
        cols = slice(h * HEAD_SIZE, (h + 1) * HEAD_SIZE)
        acc = jnp.sum(x_ref[:, :, cols].astype(jnp.float32) * scale, axis=0)
        acc = acc / jnp.sum(scale, axis=0)
        at = (h % half) * HEAD_SIZE
        out_ref[h // half, :, at : at + HEAD_SIZE] = acc.astype(jnp.bfloat16)


def combine(parts, heads):
    count, rows, _ = parts.shape
    return pl.pallas_call(
        functools.partial(combine_kernel, heads),
        out_shape=jax.ShapeDtypeStruct((2, rows, heads * HEAD_SIZE // 2), jnp.bfloat16),
        compiler_params=params(),
        name="combine",
    )(parts)


def gate_up_kernel(tiles, x_ref, perm_ref, gain_ref, gate_ref, up_ref, out_ref, scaled_ref):
    f = pl.program_id(1)
    width = gate_ref.shape[1]

    @pl.when(f == 0)
    def _():
        rows = jnp.dot(perm_ref[...], x_ref[...], preferred_element_type=jnp.float32)
        scaled_ref[...] = (rows * gain_ref[...]).astype(jnp.bfloat16)
        squares = jnp.sum(rows * rows, axis=1, keepdims=True)
        high, mid, _ = split_bf16(squares)
        lane = lax.broadcasted_iota(jnp.int32, (rows.shape[0], LANES), 1)
        pad = jnp.where(lane == 0, high.astype(jnp.float32), 0.0)
        pad = jnp.where(lane == 1, mid.astype(jnp.float32), pad)
        out_ref[:, 2 * tiles * width :] = pad.astype(jnp.bfloat16)

    scaled = scaled_ref[...]
    at = pl.multiple_of(f * width, LANES)
    out_ref[:, pl.ds(at, width)] = jnp.dot(
        scaled, gate_ref[...], preferred_element_type=jnp.float32
    ).astype(jnp.bfloat16)
    out_ref[:, pl.ds(tiles * width + at, width)] = jnp.dot(
        scaled, up_ref[...], preferred_element_type=jnp.float32
    ).astype(jnp.bfloat16)


def gate_up(x, perm, gain, gate_proj, up_proj):
    experts, depth, ff = gate_proj.shape
    slots = x.shape[0]
    rows = slots // experts
    tiles = 3
    width = ff // tiles
    weight_spec = pl.BlockSpec((None, depth, width), lambda e, f: (e, 0, f))
    return pl.pallas_call(
        functools.partial(gate_up_kernel, tiles),
        grid=(experts, tiles),
        in_specs=[
            pl.BlockSpec((slots, depth), lambda e, f: (0, 0)),
            pl.BlockSpec((rows, slots), lambda e, f: (e, 0)),
            pl.BlockSpec((1, depth), lambda e, f: (0, 0)),
            weight_spec,
            weight_spec,
        ],
        out_specs=pl.BlockSpec((rows, 2 * ff + LANES), lambda e, f: (e, 0)),
        out_shape=jax.ShapeDtypeStruct((slots, 2 * ff + LANES), jnp.bfloat16),
        scratch_shapes=[pltpu.VMEM((rows, depth), jnp.bfloat16)],
        compiler_params=params("arbitrary", "arbitrary"),
        cost_estimate=pl.CostEstimate(
            flops=4 * slots * depth * ff,
            bytes_accessed=4 * experts * depth * ff + 8 * slots * ff,
            transcendentals=0,
        ),
        name="gate_up",
    )(x, perm, gain, gate_proj, up_proj)


def activate_kernel(x_ref, out_ref):
    ff = out_ref.shape[1]
    rows = out_ref.shape[0]
    parts = x_ref.shape[0]
    squares = jnp.zeros((rows, 1), jnp.float32)
    for part in range(parts):
        pad = x_ref[part, :, 2 * ff :].astype(jnp.float32)
        squares = squares + pad[:, 0:1] + pad[:, 1:2]
    inv_rms = lax.rsqrt(squares / D + EPSILON)
    step = 256
    for at in range(0, ff, step):
        gate = jnp.zeros((rows, step), jnp.float32)
        up = jnp.zeros((rows, step), jnp.float32)
        for part in range(parts):
            gate = gate + x_ref[part, :, at : at + step].astype(jnp.float32)
            up = up + x_ref[part, :, ff + at : ff + at + step].astype(jnp.float32)
        gate = gate * inv_rms
        up = up * inv_rms
        out_ref[:, at : at + step] = (gate / (1.0 + jnp.exp(-gate)) * up).astype(jnp.bfloat16)


def activate(parts):
    _, rows, width = parts.shape
    return pl.pallas_call(
        activate_kernel,
        out_shape=jax.ShapeDtypeStruct((rows, (width - LANES) // 2), jnp.bfloat16),
        compiler_params=params(),
        name="activate",
    )(parts)


def down_kernel(act_ref, perm_ref, down_ref, out_ref, acc_ref):
    e = pl.program_id(0)
    piece = jnp.dot(act_ref[...], down_ref[...], preferred_element_type=jnp.float32)
    piece = jnp.dot(
        perm_ref[...].T, piece.astype(jnp.bfloat16), preferred_element_type=jnp.float32
    )

    @pl.when(e == 0)
    def _():
        acc_ref[...] = piece

    @pl.when(e > 0)
    def _():
        acc_ref[...] += piece

    @pl.when(e == pl.num_programs(0) - 1)
    def _():
        out_ref[...] = acc_ref[...].astype(jnp.bfloat16)


def down(act, perm, down_proj):
    experts, ff, width = down_proj.shape
    slots = act.shape[0]
    rows = slots // experts
    return pl.pallas_call(
        down_kernel,
        grid=(experts,),
        in_specs=[
            pl.BlockSpec((rows, ff), lambda e: (e, 0)),
            pl.BlockSpec((rows, slots), lambda e: (e, 0)),
            pl.BlockSpec((None, ff, width), lambda e: (e, 0, 0)),
        ],
        out_specs=pl.BlockSpec((slots, width), lambda e: (0, 0)),
        out_shape=jax.ShapeDtypeStruct((slots, width), jnp.bfloat16),
        scratch_shapes=[pltpu.VMEM((slots, width), jnp.float32)],
        compiler_params=params("arbitrary"),
        cost_estimate=pl.CostEstimate(
            flops=2 * slots * ff * width,
            bytes_accessed=2 * experts * ff * width,
            transcendentals=0,
        ),
        name="down",
    )(act, perm, down_proj)


def per_device(
    queries,
    tree_key_cache,
    tree_value_cache,
    tree_mask,
    lengths,
    out_weight,
    residual,
    norm_gain,
    expert_ids,
    gate_weights,
    gate_proj,
    up_proj,
    down_proj,
):
    rows = queries.shape[0]
    blocks, part_tokens = tree_key_cache.shape[:2]
    n_blk = lax.axis_size("blk")
    n_narrow = lax.axis_size("narrow")
    my_blk = lax.axis_index("blk")
    my_part = lax.axis_index("narrow")
    heads = QUERY_HEADS // n_narrow
    sharing = n_narrow // KEY_VALUE_HEADS

    first = jnp.arange(TREE_BLOCKS) * BLOCK_TOKENS
    bound = jnp.clip(lengths[:, None] - first[None, :], 0, BLOCK_TOKENS)
    bound = jnp.where(tree_mask == 1, bound, 0)
    own_q = lax.dynamic_slice_in_dim(queries, my_part * heads * HEAD_SIZE, heads * HEAD_SIZE, 1)
    q_out = jnp.concatenate(
        [own_q, (bound // 32).astype(jnp.bfloat16), (bound % 32).astype(jnp.bfloat16)], axis=1
    )
    q_all = lax.all_gather(q_out, "blk", tiled=True)

    kv = jnp.stack([tree_key_cache, tree_value_cache])
    kv = kv.reshape(2, blocks, part_tokens, KEY_VALUE_HEADS, HEAD_SIZE)
    kv = jnp.repeat(kv.transpose(3, 0, 1, 2, 4), sharing, axis=0)
    kv = lax.all_to_all(kv, "narrow", 0, 0)

    width = heads * HEAD_SIZE
    bounds = (q_all[:, width : width + TREE_BLOCKS].astype(jnp.int32) * 32) + q_all[
        :, width + TREE_BLOCKS :
    ].astype(jnp.int32)
    limits = lax.dynamic_slice_in_dim(bounds, my_blk * blocks, blocks, 1)
    partial = attention(q_all[:, :width], limits, kv)
    partial = lax.all_to_all(partial.reshape(n_blk, rows, width + LANES), "blk", 0, 0)
    attended = combine(partial, heads)
    attended = gather_by_exchange(attended, "narrow")
    attended = attended.reshape(n_blk, rows, QUERY_HEADS * HEAD_SIZE // n_blk)
    attended = lax.all_to_all(attended, "blk", 0, 0)
    projected = jnp.dot(
        attended.reshape(n_blk * rows, -1), out_weight, preferred_element_type=jnp.float32
    ).astype(jnp.bfloat16)
    projected = lax.all_to_all(projected.reshape(n_blk, rows, -1), "blk", 0, 0)
    projected = jnp.sum(projected.astype(jnp.float32), axis=0)
    hidden_b = (residual.astype(jnp.float32) + projected).astype(jnp.bfloat16)

    exp_dev = gate_proj.shape[0]
    n_experts = exp_dev * n_blk
    flat_ids = expert_ids.reshape(-1)
    expert_hot = (flat_ids[:, None] == jnp.arange(n_experts)[None, :]).astype(jnp.int32)
    earlier = jnp.cumsum(expert_hot, axis=0) - expert_hot
    slot_of = jnp.sum(earlier * expert_hot, axis=1)
    target = (flat_ids * CAP + slot_of).reshape(rows, TOP)
    slots = n_experts * CAP
    at_slot = target[:, :, None] == jnp.arange(slots)[None, None, :]
    select = jnp.any(at_slot, axis=1).astype(jnp.bfloat16)
    mixing = jnp.sum(jnp.where(at_slot, gate_weights[:, :, None], 0.0), axis=1)
    outgoing = lax.dot_general(
        select, hidden_b, (((0,), (0,)), ((), ())), preferred_element_type=jnp.float32
    ).astype(jnp.bfloat16)
    incoming = lax.all_to_all(outgoing.reshape(n_blk, exp_dev * CAP, -1), "blk", 0, 0)

    place = jnp.arange(slots)
    expert, rest = place // (n_blk * CAP), place % (n_blk * CAP)
    order = (rest // CAP) * (exp_dev * CAP) + expert * CAP + rest % CAP
    perm = (order[:, None] == place[None, :]).astype(jnp.bfloat16)

    parts = gate_up(
        incoming.reshape(slots, -1), perm, norm_gain.reshape(1, -1), gate_proj, up_proj
    )
    parts = lax.all_to_all(parts.reshape(n_narrow, slots // n_narrow, -1), "narrow", 0, 0)
    activated = gather_by_exchange(activate(parts), "narrow").reshape(slots, -1)
    expert_out = down(activated, perm, down_proj)
    returned = lax.all_to_all(expert_out.reshape(n_blk, exp_dev * CAP, -1), "blk", 0, 0)
    returned = returned.reshape(slots, -1)
    mix_high = lax.reduce_precision(mixing, 8, 7)
    mix_low = mixing - mix_high
    mixed_in = jnp.dot(
        mix_high.astype(jnp.bfloat16), returned, preferred_element_type=jnp.float32
    ) + jnp.dot(mix_low.astype(jnp.bfloat16), returned, preferred_element_type=jnp.float32)
    return (hidden_b.astype(jnp.float32) + mixed_in).astype(jnp.bfloat16)


def solution(mesh):
    in_specs = (
        P("blk", None),
        P("blk", "narrow", None),
        P("blk", "narrow", None),
        P("blk", None),
        P("blk"),
        P("blk", "narrow"),
        P("blk", "narrow"),
        P("narrow"),
        P("blk", None),
        P("blk", None),
        P("blk", "narrow", None),
        P("blk", "narrow", None),
        P("blk", None, "narrow"),
    )
    out_specs = P("blk", "narrow")
    return jax.shard_map(
        per_device, mesh=mesh, in_specs=in_specs, out_specs=out_specs, check_vma=False
    )
```

time: 627 us -> 306 us (0.49)
  local copies, waits for them, and re-layouts: 137 us -> 13.9 us
  matrix products: 108 us -> 3.26 us
  starting transfers between devices: 110 us -> 30 us
  Pallas kernels: 0 us -> 71.5 us
  waiting for transfers between devices: 123 us -> 73 us
  other arithmetic: 37.4 us -> 5.33 us
    dot_general x37 -> x4, matrix products: 108 us -> 3.26 us  [the longest x1 1.22 us: per_device(): jnp.dot(attended.reshape(n_blk * rows, -1), out_weight, preferred_element...]
    ppermute x45 -> x0, starting transfers between devices: 100 us -> none  [shifted(): lax.ppermute(value, axis, [(i, (i + by) % length) for i in range(length)])]
    all_to_all x1 -> x4, blocking collectives: 14.5 us -> 93.8 us  [the longest x2 36.4 us: gather_by_exchange(): return lax.all_to_all(spread, axis, 0, 0)]
    pallas_call x0 -> x5, Pallas kernels: none -> 71.5 us  [the longest x1 47.6 us: attention(): pl.pallas_call(functools.partial(attention_kernel, heads, blocks), grid=(...]
    psum x1 -> x0, waiting for transfers between devices: 69 us -> none  [per_device(): lax.psum(up_part.astype(jnp.bfloat16), 'narrow').astype(jnp.float32)]
    while x66 -> x0, local copies, waits for them, and re-layouts: 60.5 us -> none
    all_gather x2 -> x0, blocking collectives: 58.1 us -> none  [joined(): lax.all_gather(a.astype(kind), axis)]
    dynamic_update_slice x16 -> x0, local copies, waits for them, and re-layouts: 30.2 us -> none  [take_piece(): lax.dynamic_update_slice_in_dim(gathered, weight_piece, source * wo_rows, 0)]
  transfers between devices with their start and end apart: 48 -> 6, of which waited for: 9 -> 5; matrix products, arithmetic and copies ran while one was open for 33% -> 4% of each run, Pallas kernels for 0% -> 0%
where the time goes in v1:
time: 306 us; the launch traced here: 304 us
  blocking collectives  93.8 us (31%)
  waiting for transfers between devices  73 us (24%)
  Pallas kernels  71.5 us (23%)
  starting transfers between devices  30 us (10%)
  local copies, waits for them, and re-layouts  13.9 us (5%)
  between operations  13.5 us (4%)
  other arithmetic  5.33 us (2%)
  matrix products  3.26 us (1%)
    pallas_call x1, Pallas kernels, attention(): pl.pallas_call(functools.partial(attention_kernel, heads, blocks), grid=(...  47.6 us
    all_gather x1, waiting for transfers between devices, per_device(): q_all = lax.all_gather(q_out, 'blk', tiled=True)  39.1 us
    all_to_all x2, blocking collectives, gather_by_exchange(): return lax.all_to_all(spread, axis, 0, 0)  36.4 us
    all_to_all x1, blocking collectives, per_device(): lax.all_to_all(parts.reshape(n_narrow, slots // n_narrow, -1), 'narrow',...  35.5 us
    all_to_all x1, blocking collectives, per_device(): lax.all_to_all(partial.reshape(n_blk, rows, width + LANES), 'blk', 0, 0)  21.9 us
    pallas_call x1, Pallas kernels, gate_up(): pl.pallas_call(functools.partial(gate_up_kernel, tiles), grid=(experts, t...  12.2 us
    all_to_all x1, waiting for transfers between devices, per_device(): projected = lax.all_to_all(projected.reshape(n_blk, rows, -1), 'blk', 0, 0)  9.26 us
    all_to_all x1, waiting for transfers between devices, per_device(): attended = lax.all_to_all(attended, 'blk', 0, 0)  9.17 us
  transfers between devices with their start and end apart: 6, of which 5 were waited for; matrix products, arithmetic and copies ran while one was open for 4% of the time, Pallas kernels for 0%

profile of v1, /device:TPU:1, one launch (start us, length us, event | category | flops | bytes accessed | tf_op | source)
XLA Modules:
  0.0 304.3 jit_solution(2064466385388692776)
XLA Ops:
  6.5 0.0 copy-start
  6.5 0.0 all-gather.2.cloned.1.call-start
  6.5 0.9 fusion.12
  7.4 0.7 fusion.11
  8.2 0.9 constant_dynamic-slice_fusion
  9.0 0.7 concatenate.4
  9.7 0.0 all-gather.2.cloned.1.call-update
  9.8 1.2 stack.10
  10.9 1.2 stack.9
  12.1 0.7 maximum_bitcast_fusion
  12.9 0.2 copy.23
  13.1 1.9 broadcast_in_dim.20
  15.0 8.3 %all-to-all-start = ((bf16[8,2,4,128,128]{4,3,2,1,0:T(8,128)(2,1)}), bf16[8,2,4,128,128]{4,3,2,1,0:T(8,128)(2,1)S(1)}, u32[]{:S(2)}, u32[]{:S(2)}) async-start(bf16[8,2,4,128,128]{4,3,2,1,0:T(8,128)(2,1)} %bitcast.1), calls=%async_computation | async-start | bytes 4194304 | tf_op jit(solution)/shard_map/all_to_all | solution.py:317
  23.3 39.1 %all-gather.2.cloned.1.call-done = bf16[512,1152]{1,0:T(8,128)(2,1)} async-done(((bf16[32,1152]{1,0:T(8,128)(2,1)}), bf16[512,1152]{1,0:T(8,128)(2,1)}) %all-gather.2.cloned.1.call-update) | async-done | bytes 1179664 | tf_op jit(solution)/shard_map/all_gather | solution.py:312
  62.4 2.3 slice.20.q_ref
  64.7 1.1 fusion.27
  65.7 0.9 convert_add_fusion.lim_ref
  66.6 0.0 all-to-all-done.kv_ref
  66.6 0.0 copy-start.1
  66.6 1.3 copy-done.1
  67.9 47.6 %attention.1 = bf16[512,1152]{1,0:T(8,128)(2,1)} custom-call(bf16[512,1024]{1,0:T(8,128)(2,1)} %slice.20.q_ref, s32[512,4]{1,0:T(8,128)} %convert_add_fusion.lim_ref, bf16[8,2,4,128,128]{4,3,2,1,0:T(8,128)(2,1)} %copy-done.1), custom_call_target="tpu_custom_call" | custom-call | flops 12884901888 | bytes 6291456 | tf_op jit(solution)/shard_map/attention/pallas_call | solution.py:100
  115.5 21.9 %all_to_all.45.x_ref = bf16[16,32,1152]{2,1,0:T(8,128)(2,1)} all-to-all(bf16[16,32,1152]{2,1,0:T(8,128)(2,1)} %bitcast.45), channel_id=1, replica_groups=mesh['blk'=16,'narrow'=8] {'blk'}, dimensions={0} | all-to-all | bytes 2359296 | tf_op jit(solution)/shard_map/all_to_all | solution.py:325
  137.4 0.0 copy-start.4
  137.4 2.8 combine.1
  140.2 0.9 broadcast_in_dim.21
  141.1 16.9 %all_to_all.46 = bf16[8,2,32,512]{3,2,1,0:T(8,128)(2,1)} all-to-all(bf16[8,2,32,512]{3,2,1,0:T(8,128)(2,1)S(1)} %broadcast_in_dim.21), channel_id=1, replica_groups=mesh['blk'=16,'narrow'=8] {'narrow'}, dimensions={0} | all-to-all | bytes 1048576 | tf_op jit(solution)/shard_map/all_to_all | solution.py:42
  158.0 5.2 %all-to-all-start.3 = ((bf16[16,32,512]{2,1,0:T(8,128)(2,1)}), bf16[16,32,512]{2,1,0:T(8,128)(2,1)S(1)}, u32[]{:S(2)}, u32[]{:S(2)}) async-start(bf16[16,32,512]{2,1,0:T(8,128)(2,1)} %bitcast.3), calls=%async_computation.3 | async-start | bytes 1048576 | tf_op jit(solution)/shard_map/all_to_all | solution.py:329
  163.1 0.0 copy-done.4
  163.2 0.0 copy-start.3
  163.2 0.1 copy.24
  163.2 0.1 eq.74
  163.3 0.6 reduce-window.6
  164.0 9.2 %all-to-all-done.3 = bf16[16,32,512]{2,1,0:T(8,128)(2,1)S(1)} async-done(((bf16[16,32,512]{2,1,0:T(8,128)(2,1)}), bf16[16,32,512]{2,1,0:T(8,128)(2,1)S(1)}, u32[]{:S(2)}, u32[]{:S(2)}) %all-to-all-start.3) | async-done | bytes 524320 | tf_op jit(solution)/shard_map/all_to_all | solution.py:329
  173.1 0.0 copy-done
  173.1 1.2 convolution_convert_fusion
  174.4 4.4 %all-to-all-start.4 = ((bf16[16,32,512]{2,1,0:T(8,128)(2,1)}), bf16[16,32,512]{2,1,0:T(8,128)(2,1)S(1)}, u32[]{:S(2)}, u32[]{:S(2)}) async-start(bf16[16,32,512]{2,1,0:T(8,128)(2,1)} %bitcast.5), calls=%async_computation.4 | async-start | bytes 1048576 | tf_op jit(solution)/shard_map/all_to_all | solution.py:333
  178.8 0.2 slice_reduce_fusion
  179.0 0.1 eq.70
  179.1 0.1 fusion.6
  179.2 0.1 reduce_sum.31
  179.3 0.2 fusion.3
  179.5 9.3 %all-to-all-done.4 = bf16[16,32,512]{2,1,0:T(8,128)(2,1)S(1)} async-done(((bf16[16,32,512]{2,1,0:T(8,128)(2,1)}), bf16[16,32,512]{2,1,0:T(8,128)(2,1)S(1)}, u32[]{:S(2)}, u32[]{:S(2)}) %all-to-all-start.4) | async-done | bytes 524320 | tf_op jit(solution)/shard_map/all_to_all | solution.py:333
  188.8 0.1 convert_reduce_fusion
  188.8 0.0 copy-done.3
  188.8 1.1 convolution_convert_fusion.1
  189.9 4.4 %all-to-all-start.5 = ((bf16[16,24,512]{2,1,0:T(8,128)(2,1)}), bf16[16,24,512]{2,1,0:T(8,128)(2,1)S(1)}, u32[]{:S(2)}, u32[]{:S(2)}) async-start(bf16[16,24,512]{2,1,0:T(8,128)(2,1)} %bitcast.7), calls=%async_computation.5 | async-start | bytes 786432 | tf_op jit(solution)/shard_map/all_to_all | solution.py:351
  194.3 0.9 fusion.2.perm_ref
  195.2 7.5 %all-to-all-done.5 = bf16[16,24,512]{2,1,0:T(8,128)(2,1)S(1)} async-done(((bf16[16,24,512]{2,1,0:T(8,128)(2,1)}), bf16[16,24,512]{2,1,0:T(8,128)(2,1)S(1)}, u32[]{:S(2)}, u32[]{:S(2)}) %all-to-all-start.5) | async-done | bytes 393248 | tf_op jit(solution)/shard_map/all_to_all | solution.py:351
  202.7 0.0 copy-start.2
  202.7 0.7 copy-done.2
  203.4 12.2 %gate_up.1 = bf16[384,3200]{1,0:T(8,128)(2,1)} custom-call(bf16[384,512]{1,0:T(8,128)(2,1)} %bitcast.44, bf16[384,384]{1,0:T(8,128)(2,1)} %fusion.2.perm_ref, f32[1,512]{1,0:T(1,128)} %bitcast.46, bf16[4,512,1536]{2,1,0:T(8,128)(2,1)} %gate_ref.1, bf16[4,512,1536]{2,1,0:T(8,128)(2,1)} %up_ref.1), custom_call_target="tpu_custom_call" | custom-call | flops 1207959552 | bytes 17301504 | tf_op jit(solution)/shard_map/gate_up/pallas_call | solution.py:182
  215.6 35.5 %all_to_all.47.x_ref = bf16[8,48,3200]{2,1,0:T(8,128)(2,1)} all-to-all(bf16[8,48,3200]{2,1,0:T(8,128)(2,1)} %bitcast.38), channel_id=1, replica_groups=mesh['blk'=16,'narrow'=8] {'narrow'}, dimensions={0} | all-to-all | bytes 4915200 | tf_op jit(solution)/shard_map/all_to_all | solution.py:361
  251.2 2.8 activate.1
  254.0 1.0 broadcast_in_dim.24
  255.0 19.4 %all_to_all.48 = bf16[8,48,1536]{2,1,0:T(8,128)(2,1)} all-to-all(bf16[8,48,1536]{2,1,0:T(8,128)(2,1)S(1)} %broadcast_in_dim.24), channel_id=1, replica_groups=mesh['blk'=16,'narrow'=8] {'narrow'}, dimensions={0} | all-to-all | bytes 2359296 | tf_op jit(solution)/shard_map/all_to_all | solution.py:42
  274.4 0.0 copy-start.5
  274.4 6.1 %down.1 = bf16[384,512]{1,0:T(8,128)(2,1)} custom-call(bf16[384,1536]{1,0:T(8,128)(2,1)} %bitcast.39, bf16[384,384]{1,0:T(8,128)(2,1)} %fusion.2.perm_ref, bf16[4,1536,512]{2,1,0:T(8,128)(2,1)} %down_ref.1), custom_call_target="tpu_custom_call" | custom-call | flops 603979776 | bytes 6291456 | tf_op jit(solution)/shard_map/down/pallas_call | solution.py:260
  280.5 7.7 %all-to-all-start.8 = ((bf16[16,24,512]{2,1,0:T(8,128)(2,1)}), bf16[16,24,512]{2,1,0:T(8,128)(2,1)S(1)}, u32[]{:S(2)}, u32[]{:S(2)}) async-start(bf16[16,24,512]{2,1,0:T(8,128)(2,1)} %bitcast.43), calls=%async_computation.8 | async-start | bytes 786432 | tf_op jit(solution)/shard_map/all_to_all | solution.py:364
  288.2 0.0 copy-done.5
  288.2 0.1 copy.28
  288.3 0.2 select_reduce_fusion
  288.5 8.0 %all-to-all-done.8 = bf16[16,24,512]{2,1,0:T(8,128)(2,1)S(1)} async-done(((bf16[16,24,512]{2,1,0:T(8,128)(2,1)}), bf16[16,24,512]{2,1,0:T(8,128)(2,1)S(1)}, u32[]{:S(2)}, u32[]{:S(2)}) %all-to-all-start.8) | async-done | bytes 393248 | tf_op jit(solution)/shard_map/all_to_all | solution.py:364
  296.5 0.2 fusion.10
  296.6 0.8 fusion.1
  (6 shorter events, 0.1 us)
Async XLA Ops:
  6.5 166.6 %copy-start = (bf16[512,512]{1,0:T(8,128)(2,1)S(1)}, bf16[512,512]{1,0:T(8,128)(2,1)}, u32[]{:S(2)}) copy-start(bf16[512,512]{1,0:T(8,128)(2,1)} %param.18) | copy-start | bytes 1572868
  6.5 55.9 %all-gather.2.cloned.1.call-start = ((), (), s32[]{:S(2)}) async-start(), calls=%async_computation.9 | async-start | bytes 1253376 | tf_op jit(solution)/shard_map/all_gather | solution.py:312
  15.0 51.6 %all-to-all-start = ((bf16[8,2,4,128,128]{4,3,2,1,0:T(8,128)(2,1)}), bf16[8,2,4,128,128]{4,3,2,1,0:T(8,128)(2,1)S(1)}, u32[]{:S(2)}, u32[]{:S(2)}) async-start(bf16[8,2,4,128,128]{4,3,2,1,0:T(8,128)(2,1)} %bitcast.1), calls=%async_computation | async-start | bytes 4194304 | tf_op jit(solution)/shard_map/all_to_all | solution.py:317
  66.6 1.3 copy-start.1
  137.4 25.8 %copy-start.4 = (s32[32,8]{0,1:T(8,128)S(1)}, s32[32,8]{0,1:T(8,128)}, u32[]{:S(2)}) copy-start(s32[32,8]{0,1:T(8,128)} %param.21) | copy-start | bytes 3076
  158.0 15.1 %all-to-all-start.3 = ((bf16[16,32,512]{2,1,0:T(8,128)(2,1)}), bf16[16,32,512]{2,1,0:T(8,128)(2,1)S(1)}, u32[]{:S(2)}, u32[]{:S(2)}) async-start(bf16[16,32,512]{2,1,0:T(8,128)(2,1)} %bitcast.3), calls=%async_computation.3 | async-start | bytes 1048576 | tf_op jit(solution)/shard_map/all_to_all | solution.py:329
  163.2 25.7 %copy-start.3 = (bf16[32,512]{1,0:T(8,128)(2,1)S(1)}, bf16[32,512]{1,0:T(8,128)(2,1)}, u32[]{:S(2)}) copy-start(bf16[32,512]{1,0:T(8,128)(2,1)} %param.19) | copy-start | bytes 98308
  174.4 14.4 %all-to-all-start.4 = ((bf16[16,32,512]{2,1,0:T(8,128)(2,1)}), bf16[16,32,512]{2,1,0:T(8,128)(2,1)S(1)}, u32[]{:S(2)}, u32[]{:S(2)}) async-start(bf16[16,32,512]{2,1,0:T(8,128)(2,1)} %bitcast.5), calls=%async_computation.4 | async-start | bytes 1048576 | tf_op jit(solution)/shard_map/all_to_all | solution.py:333
  189.9 12.8 %all-to-all-start.5 = ((bf16[16,24,512]{2,1,0:T(8,128)(2,1)}), bf16[16,24,512]{2,1,0:T(8,128)(2,1)S(1)}, u32[]{:S(2)}, u32[]{:S(2)}) async-start(bf16[16,24,512]{2,1,0:T(8,128)(2,1)} %bitcast.7), calls=%async_computation.5 | async-start | bytes 786432 | tf_op jit(solution)/shard_map/all_to_all | solution.py:351
  202.7 0.7 copy-start.2
  274.4 13.8 %copy-start.5 = (f32[32,8]{0,1:T(8,128)S(1)}, f32[32,8]{0,1:T(8,128)}, u32[]{:S(2)}) copy-start(f32[32,8]{0,1:T(8,128)} %param.22) | copy-start | bytes 3076
  280.5 16.0 %all-to-all-start.8 = ((bf16[16,24,512]{2,1,0:T(8,128)(2,1)}), bf16[16,24,512]{2,1,0:T(8,128)(2,1)S(1)}, u32[]{:S(2)}, u32[]{:S(2)}) async-start(bf16[16,24,512]{2,1,0:T(8,128)(2,1)} %bitcast.43), calls=%async_computation.8 | async-start | bytes 786432 | tf_op jit(solution)/shard_map/all_to_all | solution.py:364
Sparse Core Ops, SparseCore 0:
  9.9 52.4 all-gather.1

commit v2 on v1

v2 whole, which is shorter than its diff:
```python
import functools

import jax
import jax.numpy as jnp
from jax import lax
from jax.experimental import pallas as pl
from jax.experimental.pallas import tpu as pltpu
from jax.sharding import Mesh
from jax.sharding import PartitionSpec as P

D = 4096
QUERY_HEADS = 64
KEY_VALUE_HEADS = 4
HEAD_SIZE = 128
FF = 1536
TOP = 8
CAP = 6
BLOCK_TOKENS = 1024
TREE_BLOCKS = 64
NEGATIVE_FILLER = -1e30
EPSILON = 1e-06
SCORE_SCALE = HEAD_SIZE ** (-0.5)
LOG2E = 1.4426950408889634
LANES = 128
BLK = ("zl", "x", "core")
NARROW = ("zh", "yh", "yl")
VMEM_LIMIT = 32 * 1024 * 1024
SMALL_LIMIT = 12 * 1024 * 1024


def params(limit):
    return pltpu.CompilerParams(vmem_limit_bytes=limit)


def split_bf16(value):
    high = value.astype(jnp.bfloat16)
    rest = value - high.astype(jnp.float32)
    mid = rest.astype(jnp.bfloat16)
    low = (rest - mid.astype(jnp.float32)).astype(jnp.bfloat16)
    return high, mid, low


def gather_by_exchange(value, axis):
    length = lax.axis_size(axis)
    spread = jnp.broadcast_to(value[None], (length,) + value.shape)
    return lax.all_to_all(spread, axis, 0, 0)


def attention_kernel(start, heads, *refs):
    info_ref = refs[0]
    q_refs = refs[1:9]
    kv_refs = refs[9:17]
    out_ref, q_ref, k_ref, vt_ref, lim_ref, s_ref = refs[17:]
    rows = q_ref.shape[0]
    base = q_refs[0].shape[1] - LANES
    chip, core, my_yh = info_ref[0], info_ref[1], info_ref[2]
    sources = len(kv_refs) // 2
    blocks = kv_refs[0].shape[1]
    span = sources * LANES
    step = rows // len(q_refs)

    for i, ref in enumerate(q_refs):
        q_ref[i * step : (i + 1) * step, :] = ref[...]
    extra = q_ref[:, base:].astype(jnp.float32).T
    lim_ref[...] = extra
    length = extra[TREE_BLOCKS : TREE_BLOCKS + 1] * 256.0 + extra[TREE_BLOCKS + 1 : TREE_BLOCKS + 2]
    chip_blocks = 2 * blocks
    first = pl.multiple_of(chip * chip_blocks, chip_blocks)
    mask = lim_ref[pl.ds(first, chip_blocks), :]
    block_id = lax.broadcasted_iota(jnp.int32, (chip_blocks, rows), 0) + first
    bound = length - (block_id * BLOCK_TOKENS).astype(jnp.float32)
    bound = jnp.where(mask > 0.5, bound, 0.0)
    lim_ref[0:chip_blocks, :] = bound
    sub = lax.broadcasted_iota(jnp.int32, (16, blocks * 2 * span), 0)
    vt_ref[HEAD_SIZE:, :] = jnp.where(sub == 0, 1.0, 0.0).astype(jnp.bfloat16)
    for side in range(2):
        for i in range(blocks):
            for s in range(sources):
                at = (side * blocks + i) * span + s * LANES
                ref = kv_refs[side * sources + s]
                k_ref[at : at + LANES, :] = ref[0, i]
                vt_ref[:HEAD_SIZE, at : at + LANES] = ref[1, i].T

    token = lax.broadcasted_iota(jnp.int32, (LANES, 1), 0) + my_yh * (2 * LANES)
    token = [(token + info_ref[4 + s] * LANES).astype(jnp.float32) for s in range(sources)]
    token = jnp.concatenate(token, axis=0)
    sub_row = lax.broadcasted_iota(jnp.int32, (8, rows), 0)

    def one_head(h, info):
        cols = pl.ds(pl.multiple_of(h * HEAD_SIZE, HEAD_SIZE), HEAD_SIZE)
        q_cols = pl.ds(pl.multiple_of((start + h) * HEAD_SIZE, HEAD_SIZE), HEAD_SIZE)
        qt = q_ref[:, q_cols].T
        top = jnp.full((1, rows), -1e29, jnp.float32)
        for i in range(2 * blocks):
            at = slice(i * span, (i + 1) * span)
            side = core if i < blocks else 1 - core
            lim = lim_ref[pl.ds(side * blocks + i % blocks, 1), :]
            s = jnp.dot(k_ref[at, :], qt, preferred_element_type=jnp.float32)
            s = jnp.where(token < lim, s, NEGATIVE_FILLER)
            s_ref[at, :] = s
            top = jnp.maximum(top, jnp.max(s, axis=0, keepdims=True))
        acc = jnp.zeros((HEAD_SIZE + 16, rows), jnp.float32)
        for i in range(2 * blocks):
            at = slice(i * span, (i + 1) * span)
            p = jnp.exp2((s_ref[at, :] - top) * (SCORE_SCALE * LOG2E)).astype(jnp.bfloat16)
            acc = acc + jnp.dot(vt_ref[:, at], p, preferred_element_type=jnp.float32)
        total = acc[HEAD_SIZE : HEAD_SIZE + 1]
        some = total > 0
        safe = jnp.where(some, total, 1.0)
        result = (acc[:HEAD_SIZE] / safe).astype(jnp.bfloat16).T
        group = rows // 16
        for i in range(16):
            row = pl.multiple_of(info_ref[8 + i] * group, group)
            out_ref[pl.ds(row, group), cols] = result[i * group : (i + 1) * group]
        lse = jnp.where(some, top * SCORE_SCALE + jnp.log(safe), NEGATIVE_FILLER)
        return jnp.where(sub_row == h, lse, info)

    info = lax.fori_loop(0, heads, one_head, jnp.zeros((8, rows), jnp.float32))
    high, mid, low = split_bf16(info)
    pieces = [piece.astype(jnp.float32) for piece in (high, mid, low)]
    pieces.append(jnp.zeros((LANES - 24, rows), jnp.float32))
    result = jnp.concatenate(pieces, axis=0).T.astype(jnp.bfloat16)
    group = rows // 16
    for i in range(16):
        row = pl.multiple_of(info_ref[8 + i] * group, group)
        out_ref[pl.ds(row, group), heads * HEAD_SIZE :] = result[i * group : (i + 1) * group]


def attention(info, queries, kv, start, heads):
    step, width = queries[0].shape
    rows = step * len(queries)
    out_width = heads * HEAD_SIZE + LANES
    blocks = kv[0].shape[1]
    tokens = len(kv) * blocks * LANES
    vmem = pl.BlockSpec(memory_space=pltpu.VMEM)
    return pl.pallas_call(
        functools.partial(attention_kernel, start, heads),
        in_specs=[pl.BlockSpec(memory_space=pltpu.SMEM)] + [vmem] * (len(queries) + len(kv)),
        out_specs=vmem,
        out_shape=jax.ShapeDtypeStruct((rows, out_width), jnp.bfloat16),
        scratch_shapes=[
            pltpu.VMEM((rows, width), jnp.bfloat16),
            pltpu.VMEM((tokens, HEAD_SIZE), jnp.bfloat16),
            pltpu.VMEM((HEAD_SIZE + 16, tokens), jnp.bfloat16),
            pltpu.VMEM((LANES, rows), jnp.float32),
            pltpu.VMEM((tokens, rows), jnp.float32),
        ],
        compiler_params=params(limit=VMEM_LIMIT),
        cost_estimate=pl.CostEstimate(
            flops=6 * rows * heads * tokens * HEAD_SIZE,
            bytes_accessed=6 << 20,
            transcendentals=rows * heads * tokens,
        ),
        name="attention",
    )(info, *queries, *kv)


def combine_kernel(heads, x_ref, out_ref):
    base = heads * HEAD_SIZE
    info = x_ref[:, :, base:].astype(jnp.float32)
    for h in range(heads):
        lse = info[:, :, h : h + 1] + info[:, :, 8 + h : 9 + h]
        lse = lse + info[:, :, 16 + h : 17 + h]
        scale = jnp.exp(lse - jnp.max(lse, axis=0, keepdims=True))
        cols = slice(h * HEAD_SIZE, (h + 1) * HEAD_SIZE)
        acc = jnp.sum(x_ref[:, :, cols].astype(jnp.float32) * scale, axis=0)
        out_ref[:, cols] = (acc / jnp.sum(scale, axis=0)).astype(jnp.bfloat16)


def combine(parts, heads):
    _, rows, _ = parts.shape
    return pl.pallas_call(
        functools.partial(combine_kernel, heads),
        out_shape=jax.ShapeDtypeStruct((rows, heads * HEAD_SIZE), jnp.bfloat16),
        compiler_params=params(limit=SMALL_LIMIT),
        cost_estimate=pl.CostEstimate(
            flops=4 * parts.size, bytes_accessed=2 * parts.size, transcendentals=0
        ),
        name="combine",
    )(parts)


def gate_up_kernel(x_ref, perm_ref, gain_ref, gate_ref, up_ref, out_ref):
    experts, _, width = gate_ref.shape
    count = x_ref.shape[0] // experts
    for e in range(experts):
        at = slice(e * count, (e + 1) * count)
        rows = jnp.dot(perm_ref[at, :], x_ref[...], preferred_element_type=jnp.float32)
        scaled = (rows * gain_ref[...]).astype(jnp.bfloat16)
        squares = jnp.sum(rows * rows, axis=1, keepdims=True)
        high, mid, _ = split_bf16(squares)
        lane = lax.broadcasted_iota(jnp.int32, (count, LANES), 1)
        pad = jnp.where(lane == 0, high.astype(jnp.float32), 0.0)
        pad = jnp.where(lane == 1, mid.astype(jnp.float32), pad)
        out_ref[at, 2 * width :] = pad.astype(jnp.bfloat16)
        out_ref[at, :width] = jnp.dot(
            scaled, gate_ref[e], preferred_element_type=jnp.float32
        ).astype(jnp.bfloat16)
        out_ref[at, width : 2 * width] = jnp.dot(
            scaled, up_ref[e], preferred_element_type=jnp.float32
        ).astype(jnp.bfloat16)


def gate_up(x, perm, gain, gate_proj, up_proj):
    experts, depth, ff = gate_proj.shape
    slots = x.shape[0]
    vmem = pl.BlockSpec(memory_space=pltpu.VMEM)
    return pl.pallas_call(
        gate_up_kernel,
        in_specs=[vmem] * 5,
        out_specs=vmem,
        out_shape=jax.ShapeDtypeStruct((slots, 2 * ff + LANES), jnp.bfloat16),
        compiler_params=params(limit=SMALL_LIMIT),
        cost_estimate=pl.CostEstimate(
            flops=4 * slots * depth * ff,
            bytes_accessed=4 * experts * depth * ff + 4 * slots * ff,
            transcendentals=0,
        ),
        name="gate_up",
    )(x, perm, gain, gate_proj, up_proj)


def activate_kernel(x_ref, out_ref):
    ff = out_ref.shape[1]
    rows = out_ref.shape[0]
    parts = x_ref.shape[0]
    squares = jnp.zeros((rows, 1), jnp.float32)
    for part in range(parts):
        pad = x_ref[part, :, 2 * ff :].astype(jnp.float32)
        squares = squares + pad[:, 0:1] + pad[:, 1:2]
    inv_rms = lax.rsqrt(squares / D + EPSILON)
    step = 256
    for at in range(0, ff, step):
        gate = jnp.zeros((rows, step), jnp.float32)
        up = jnp.zeros((rows, step), jnp.float32)
        for part in range(parts):
            gate = gate + x_ref[part, :, at : at + step].astype(jnp.float32)
            up = up + x_ref[part, :, ff + at : ff + at + step].astype(jnp.float32)
        gate = gate * inv_rms
        up = up * inv_rms
        out_ref[:, at : at + step] = (gate / (1.0 + jnp.exp(-gate)) * up).astype(jnp.bfloat16)


def activate(parts):
    _, rows, width = parts.shape
    return pl.pallas_call(
        activate_kernel,
        out_shape=jax.ShapeDtypeStruct((rows, (width - LANES) // 2), jnp.bfloat16),
        compiler_params=params(limit=SMALL_LIMIT),
        name="activate",
    )(parts)


def down_kernel(act_ref, back_ref, down_ref, out_ref, all_ref):
    experts = down_ref.shape[0]
    count = act_ref.shape[0] // experts
    for e in range(experts):
        at = slice(e * count, (e + 1) * count)
        all_ref[at, :] = jnp.dot(
            act_ref[at, :], down_ref[e], preferred_element_type=jnp.float32
        ).astype(jnp.bfloat16)
    out_ref[...] = jnp.dot(
        back_ref[...], all_ref[...], preferred_element_type=jnp.float32
    ).astype(jnp.bfloat16)


def down(act, back, down_proj):
    experts, ff, width = down_proj.shape
    slots = act.shape[0]
    vmem = pl.BlockSpec(memory_space=pltpu.VMEM)
    return pl.pallas_call(
        down_kernel,
        in_specs=[vmem] * 3,
        out_specs=vmem,
        out_shape=jax.ShapeDtypeStruct((slots, width), jnp.bfloat16),
        scratch_shapes=[pltpu.VMEM((slots, width), jnp.bfloat16)],
        compiler_params=params(limit=SMALL_LIMIT),
        cost_estimate=pl.CostEstimate(
            flops=2 * slots * ff * width,
            bytes_accessed=2 * experts * ff * width,
            transcendentals=0,
        ),
        name="down",
    )(act, back, down_proj)


def per_device(
    queries,
    tree_key_cache,
    tree_value_cache,
    tree_mask,
    lengths,
    out_weight,
    residual,
    norm_gain,
    expert_ids,
    gate_weights,
    gate_proj,
    up_proj,
    down_proj,
):
    rows = queries.shape[0]
    blocks, part_tokens = tree_key_cache.shape[:2]
    n_blk = lax.axis_size(BLK)
    n_narrow = lax.axis_size(NARROW)
    zl, x, core = (lax.axis_index(name) for name in BLK)
    zh, yh, yl = (lax.axis_index(name) for name in NARROW)
    kv_head = zh * 2 + yl
    heads = QUERY_HEADS // n_narrow
    width = heads * HEAD_SIZE
    swap = [(0, 1), (1, 0)]
    size_x = lax.axis_size("x")

    kv = jnp.stack([tree_key_cache, tree_value_cache])
    kv = kv.reshape(2, blocks, part_tokens, KEY_VALUE_HEADS, HEAD_SIZE).transpose(3, 0, 1, 2, 4)
    own_kv = [lax.dynamic_index_in_dim(kv, kv_head, 0, False)]
    for step in range(1, KEY_VALUE_HEADS):
        piece = lax.dynamic_index_in_dim(kv, kv_head ^ step, 0, False)
        pairs = [(i, i ^ step) for i in range(KEY_VALUE_HEADS)]
        own_kv.append(lax.ppermute(piece, ("zh", "yl"), pairs))
    kv = own_kv + [lax.ppermute(piece, "core", swap) for piece in own_kv]

    both = lax.dynamic_slice_in_dim(queries, kv_head * 2 * width, 2 * width, 1)
    extra = jnp.concatenate(
        [
            tree_mask.astype(jnp.bfloat16),
            (lengths // 256).astype(jnp.bfloat16)[:, None],
            (lengths % 256).astype(jnp.bfloat16)[:, None],
            jnp.zeros((rows, LANES - TREE_BLOCKS - 2), jnp.bfloat16),
        ],
        axis=1,
    )
    own_q = lax.dynamic_slice_in_dim(both, core * width, width, 1)
    other_q = lax.dynamic_slice_in_dim(both, (1 - core) * width, width, 1)
    own_q = jnp.concatenate([own_q, extra], axis=1)
    other_q = lax.ppermute(jnp.concatenate([other_q, extra], axis=1), "core", swap)
    pair = jnp.concatenate([own_q, other_q], axis=0)
    all_q, groups = [], []
    for dx in range(size_x):
        for dz in range(2):
            pairs = [
                (z * size_x + i, (z ^ dz) * size_x + (i + dx) % size_x)
                for z in range(2)
                for i in range(size_x)
            ]
            all_q.append(lax.ppermute(pair, ("zl", "x"), pairs) if dx + dz else pair)
            origin = (zl ^ dz) * size_x + (x - dx) % size_x
            groups += [origin * 2 + core, origin * 2 + (1 - core)]
    sources = [((kv_head ^ s) // 2) * 4 + (kv_head ^ s) % 2 for s in range(KEY_VALUE_HEADS)]
    zero = jnp.int32(0)
    info = [zl * size_x + x, core, yh, zero] + sources + groups
    info = jnp.stack([value.astype(jnp.int32) for value in info])
    group_axes = ("zl", "x", "yh")
    attended = []
    for half in range(2):
        partial = attention(info, all_q, kv, half * (heads // 2), heads // 2)
        partial = lax.all_to_all(partial.reshape(n_blk, rows, -1), group_axes, 0, 0)
        attended.append(combine(partial, heads // 2))

    mine = jnp.where(core == 0, attended[0], attended[1])
    other = jnp.where(core == 0, attended[1], attended[0])
    other = lax.ppermute(other, "core", swap)
    first = jnp.where(core == 0, mine, other)
    second = jnp.where(core == 0, other, mine)
    attended = jnp.stack([first, second])
    gathered = jnp.zeros((KEY_VALUE_HEADS,) + attended.shape, attended.dtype)
    gathered = lax.dynamic_update_index_in_dim(gathered, attended, kv_head, 0)
    for step in range(1, KEY_VALUE_HEADS):
        pairs = [(i, i ^ step) for i in range(KEY_VALUE_HEADS)]
        piece = lax.ppermute(attended, ("zh", "yl"), pairs)
        gathered = lax.dynamic_update_index_in_dim(gathered, piece, kv_head ^ step, 0)
    gathered = gathered.reshape(n_blk // 2, 1, rows, -1)
    gathered = jnp.broadcast_to(gathered, (n_blk // 2, 2) + gathered.shape[2:])
    gathered = lax.all_to_all(gathered.reshape((n_blk,) + gathered.shape[2:]), group_axes, 0, 0)
    projected = jnp.dot(
        gathered.reshape(n_blk * rows, -1), out_weight, preferred_element_type=jnp.float32
    )
    projected = projected.reshape(n_blk // 2, 2, rows, -1)
    mine = lax.dynamic_index_in_dim(projected, core, 1, False)
    other = lax.dynamic_index_in_dim(projected, 1 - core, 1, False).astype(jnp.bfloat16)
    projected = (mine + lax.ppermute(other, "core", swap).astype(jnp.float32)).astype(jnp.bfloat16)
    projected = lax.all_to_all(projected, ("zl", "x"), 0, 0)
    projected = jnp.sum(projected.astype(jnp.float32), axis=0)
    hidden_b = (residual.astype(jnp.float32) + projected).astype(jnp.bfloat16)

    exp_dev = gate_proj.shape[0]
    n_experts = exp_dev * n_blk
    flat_ids = expert_ids.reshape(-1)
    expert_hot = (flat_ids[:, None] == jnp.arange(n_experts)[None, :]).astype(jnp.int32)
    earlier = jnp.cumsum(expert_hot, axis=0) - expert_hot
    slot_of = jnp.sum(earlier * expert_hot, axis=1)
    target = (flat_ids * CAP + slot_of).reshape(rows, TOP)
    slots = n_experts * CAP
    at_slot = target[:, :, None] == jnp.arange(slots)[None, None, :]
    select = jnp.any(at_slot, axis=1).astype(jnp.bfloat16)
    mixing = jnp.sum(jnp.where(at_slot, gate_weights[:, :, None], 0.0), axis=1)
    outgoing = lax.dot_general(
        select, hidden_b, (((0,), (0,)), ((), ())), preferred_element_type=jnp.float32
    ).astype(jnp.bfloat16)
    incoming = lax.all_to_all(outgoing.reshape(n_blk, exp_dev * CAP, -1), BLK, 0, 0)

    place = jnp.arange(slots)
    expert, rest = place // (n_blk * CAP), place % (n_blk * CAP)
    order = (rest // CAP) * (exp_dev * CAP) + expert * CAP + rest % CAP
    perm = (order[:, None] == place[None, :]).astype(jnp.bfloat16)

    back = (place[:, None] == order[None, :]).astype(jnp.bfloat16)
    sums = gate_up(
        incoming.reshape(slots, -1), perm, norm_gain.reshape(1, -1), gate_proj, up_proj
    )
    sums = lax.all_to_all(sums.reshape(n_narrow, slots // n_narrow, -1), NARROW, 0, 0)
    activated = gather_by_exchange(activate(sums), NARROW).reshape(slots, -1)
    expert_out = down(activated, back, down_proj)
    returned = lax.all_to_all(expert_out.reshape(n_blk, exp_dev * CAP, -1), BLK, 0, 0)
    returned = returned.reshape(slots, -1)
    mix_high = lax.reduce_precision(mixing, 8, 7)
    mix_low = mixing - mix_high
    mixed_in = jnp.dot(
        mix_high.astype(jnp.bfloat16), returned, preferred_element_type=jnp.float32
    ) + jnp.dot(mix_low.astype(jnp.bfloat16), returned, preferred_element_type=jnp.float32)
    return (hidden_b.astype(jnp.float32) + mixed_in).astype(jnp.bfloat16)


def solution(mesh):
    shape = (2, 4, 2, 2, 2, 2)
    fine = Mesh(mesh.devices.reshape(shape), BLK + NARROW)
    in_specs = (
        P(BLK, None),
        P(BLK, NARROW, None),
        P(BLK, NARROW, None),
        P(BLK, None),
        P(BLK),
        P(BLK, NARROW),
        P(BLK, NARROW),
        P(NARROW),
        P(BLK, None),
        P(BLK, None),
        P(BLK, NARROW, None),
        P(BLK, NARROW, None),
        P(BLK, None, NARROW),
    )
    out_specs = P(BLK, NARROW)
    return jax.shard_map(
        per_device, mesh=fine, in_specs=in_specs, out_specs=out_specs, check_vma=False
    )
```

time: 306 us -> 248 us (0.81)
  blocking collectives: 93.8 us -> 52.8 us
  starting transfers between devices: 30 us -> 69.5 us
  Pallas kernels: 71.5 us -> 38.7 us
  waiting for transfers between devices: 73 us -> 57.1 us
  between operations: 13.5 us -> 0.4 us
  local copies, waits for them, and re-layouts: 13.9 us -> 21.8 us
    all_gather x1 -> x0, waiting for transfers between devices: 39.1 us -> none  [per_device(): q_all = lax.all_gather(q_out, 'blk', tiled=True)]
    ppermute x0 -> x20, starting transfers between devices: none -> 35.4 us  [the longest x7 12.3 us: per_device(): all_q.append(lax.ppermute(pair, ('zl', 'x'), pairs) if dx + dz else pair)]
    pallas_call x3 -> x4, Pallas kernels: 65.9 us -> 37.2 us  [the longest x2 32.3 us: attention(): pl.pallas_call(functools.partial(attention_kernel, start, heads), in_spec...]
    all_to_all x2 -> x1, blocking collectives: 57.4 us -> 34.7 us  [per_device(): lax.all_to_all(sums.reshape(n_narrow, slots // n_narrow, -1), NARROW, 0, 0)]
    all_to_all x2 -> x1, blocking collectives: 36.4 us -> 18.1 us  [gather_by_exchange(): return lax.all_to_all(spread, axis, 0, 0)]
    ppermute x0 -> x20, waiting for transfers between devices: none -> 15 us  [the longest x7 8.14 us: per_device(): all_q.append(lax.ppermute(pair, ('zl', 'x'), pairs) if dx + dz else pair)]
    unnamed x14 -> x49, local copies, waits for them, and re-layouts: 2.26 us -> 17.2 us
    all_to_all x5 -> x6, waiting for transfers between devices: 33.9 us -> 42.1 us  [the longest x2 9.66 us: per_device(): partial = lax.all_to_all(partial.reshape(n_blk, rows, -1), group_axes, 0, 0)]
  transfers between devices with their start and end apart: 6 -> 26, of which waited for: 5 -> 12; matrix products, arithmetic and copies ran while one was open for 4% -> 2% of each run, Pallas kernels for 0% -> 7%
where the time goes in v2:
time: 248 us; the launch traced here: 246 us
  starting transfers between devices  69.5 us (28%)
  waiting for transfers between devices  57.1 us (23%)
  blocking collectives  52.8 us (21%)
  Pallas kernels  38.7 us (16%)
  local copies, waits for them, and re-layouts  21.8 us (9%)
  other arithmetic  3.69 us (1%)
  matrix products  2.49 us (1%)
    all_to_all x1, blocking collectives, per_device(): lax.all_to_all(sums.reshape(n_narrow, slots // n_narrow, -1), NARROW, 0, 0)  34.7 us
    pallas_call x2, Pallas kernels, attention(): pl.pallas_call(functools.partial(attention_kernel, start, heads), in_spec...  32.3 us
    all_to_all x1, blocking collectives, gather_by_exchange(): return lax.all_to_all(spread, axis, 0, 0)  18.1 us
    unnamed x49, local copies, waits for them, and re-layouts  17.2 us
    all_to_all x2, starting transfers between devices, per_device(): partial = lax.all_to_all(partial.reshape(n_blk, rows, -1), group_axes, 0, 0)  14.6 us
    ppermute x7, starting transfers between devices, per_device(): all_q.append(lax.ppermute(pair, ('zl', 'x'), pairs) if dx + dz else pair)  12.3 us
    all_to_all x2, waiting for transfers between devices, per_device(): partial = lax.all_to_all(partial.reshape(n_blk, rows, -1), group_axes, 0, 0)  9.66 us
    all_to_all x1, waiting for transfers between devices, per_device(): lax.all_to_all(gathered.reshape((n_blk,) + gathered.shape[2:]), group_axe...  9.11 us
  transfers between devices with their start and end apart: 26, of which 12 were waited for; matrix products, arithmetic and copies ran while one was open for 2% of the time, Pallas kernels for 7%

profile of v2, /device:TPU:1, one launch (start us, length us, event | category | flops | bytes accessed | tf_op | source)
XLA Modules:
  0.0 246.4 jit_solution(16315101971079163416)
XLA Ops:
  0.0 0.8 fusion.28
  1.0 0.7 convert_element_type.60
  1.7 1.1 constant_dynamic-slice_fusion.1
  2.9 1.5 collective-permute-start
  4.4 1.2 stack.114
  5.9 1.8 collective-permute-start.1
  7.9 1.3 collective-permute-start.2
  9.2 1.0 collective-permute-start.3
  10.2 1.4 collective-permute-start.8
  11.6 3.3 %collective-permute-start.9 = (bf16[2,4,128,128]{3,2,1,0:T(8,128)(2,1)S(1)}, bf16[2,4,128,128]{3,2,1,0:T(8,128)(2,1)S(1)}, u32[]{:S(2)}, u32[]{:S(2)}) collective-permute-start(bf16[2,4,128,128]{3,2,1,0:T(8,128)(2,1)S(1)} %get-tuple-element.6), channel_id=1, source_target_pairs={{0,4},{1,5},{4,0},{5,1},{2,6},{3,7},{6,2},{7,3},{8,12},{9,13},{12,... | collective-permute-start | bytes 786440 | tf_op jit(solution)/shard_map/ppermute | solution.py:320
  15.0 1.1 collective-permute-start.10
  16.1 2.7 %collective-permute-start.4 = (bf16[64,1152]{1,0:T(8,128)(2,1)S(1)}, bf16[64,1152]{1,0:T(8,128)(2,1)S(1)}, u32[]{:S(2)}, u32[]{:S(2)}) collective-permute-start(bf16[64,1152]{1,0:T(8,128)(2,1)S(1)} %pad_maximum_fusion.refs_1_), channel_id=1, source_target_pairs={{0,32},{16,48},{32,0},{48,16},{64,96},{80,112},{96,64},{112,80},{1... | collective-permute-start | bytes 442376 | tf_op jit(solution)/shard_map/ppermute | solution.py:346
  18.9 1.1 collective-permute-start.5
  19.9 2.0 collective-permute-done.4.refs_5_
  21.9 2.5 %collective-permute-start.6 = (bf16[64,1152]{1,0:T(8,128)(2,1)S(1)}, bf16[64,1152]{1,0:T(8,128)(2,1)S(1)}, u32[]{:S(2)}, u32[]{:S(2)}) collective-permute-start(bf16[64,1152]{1,0:T(8,128)(2,1)S(1)} %pad_maximum_fusion.refs_1_), channel_id=1, source_target_pairs={{0,48},{16,0},{32,16},{48,32},{64,112},{80,64},{96,80},{112,96},{1... | collective-permute-start | bytes 442376 | tf_op jit(solution)/shard_map/ppermute | solution.py:346
  24.4 2.3 collective-permute-done.5.refs_6_
  26.6 0.7 copy-done.13
  27.3 2.3 collective-permute-start.11
  29.6 2.9 %collective-permute-done.9.refs_11_ = bf16[2,4,128,128]{3,2,1,0:T(8,128)(2,1)S(1)} collective-permute-done((bf16[2,4,128,128]{3,2,1,0:T(8,128)(2,1)S(1)}, bf16[2,4,128,128]{3,2,1,0:T(8,128)(2,1)S(1)}, u32[]{:S(2)}, u32[]{:S(2)}) %collective-permute-start.9) | collective-permute-done | bytes 262176 | tf_op jit(solution)/shard_map/ppermute | solution.py:320
  32.5 1.7 collective-permute-start.13
  34.2 0.6 copy-done.16
  34.8 1.9 collective-permute-start.7
  36.9 3.9 %collective-permute-done.7.refs_8_ = bf16[64,1152]{1,0:T(8,128)(2,1)} collective-permute-done((bf16[64,1152]{1,0:T(8,128)(2,1)S(1)}, bf16[64,1152]{1,0:T(8,128)(2,1)}, u32[]{:S(2)}, u32[]{:S(2)}) %collective-permute-start.7) | collective-permute-done | bytes 147488 | tf_op jit(solution)/shard_map/ppermute | solution.py:346
  40.8 0.9 copy-done.14
  41.7 0.9 copy-done.17
  42.6 16.1 %attention.2 = bf16[512,640]{1,0:T(8,128)(2,1)} custom-call(s32[24]{0:T(128)S(1)} %stack.113.refs_0_, bf16[64,1152]{1,0:T(8,128)(2,1)S(1)} %pad_maximum_fusion.refs_1_, bf16[64,1152]{1,0:T(8,128)(2,1)S(1)} %collective-permute-done.1.refs_2_, bf16[64,1152]{1,0:T(8,128)(2,1)S(1)} %collective-permute-done.2.refs_3_, ...), custom_call_target="tpu_custom_call" | custom-call | flops 6442450944 | bytes 6291456 | tf_op jit(solution)/shard_map/attention/pallas_call | solution.py:136
  58.7 7.0 %all-to-all-start = ((bf16[16,32,640]{2,1,0:T(8,128)(2,1)}), bf16[16,32,640]{2,1,0:T(8,128)(2,1)S(1)}, u32[]{:S(2)}, u32[]{:S(2)}) async-start(bf16[16,32,640]{2,1,0:T(8,128)(2,1)} %bitcast.29), calls=%async_computation | async-start | bytes 1310720 | tf_op jit(solution)/shard_map/all_to_all | solution.py:357
  65.8 0.9 copy-done.6
  66.7 0.9 copy-done.8
  67.6 0.9 copy-done.10
  68.5 0.9 copy-done.12
  69.4 0.9 copy-done.15
  70.3 0.9 copy-done.18
  71.2 16.2 %attention.3 = bf16[512,640]{1,0:T(8,128)(2,1)} custom-call(s32[24]{0:T(128)S(1)} %stack.113.refs_0_, bf16[64,1152]{1,0:T(8,128)(2,1)S(1)} %pad_maximum_fusion.refs_1_, bf16[64,1152]{1,0:T(8,128)(2,1)S(1)} %copy-done.6, bf16[64,1152]{1,0:T(8,128)(2,1)S(1)} %copy-done.8, bf16[64,1152]{1,0:T(8,128)(2,1)S(1)} %copy-done.10, bf16[64,1152]{1,0:T(8,128)(2,1)S(1)} %copy-done.12, ...), custom_call_target="tpu_custom_call" | custom-call | flops 6442450944 | bytes 6291456 | tf_op jit(solution)/shard_map/attention/pallas_call | solution.py:136
  87.4 7.5 %all-to-all-start.1 = ((bf16[16,32,640]{2,1,0:T(8,128)(2,1)}), bf16[16,32,640]{2,1,0:T(8,128)(2,1)S(1)}, u32[]{:S(2)}, u32[]{:S(2)}) async-start(bf16[16,32,640]{2,1,0:T(8,128)(2,1)} %bitcast.30), calls=%async_computation.1 | async-start | bytes 1310720 | tf_op jit(solution)/shard_map/all_to_all | solution.py:357
  95.0 0.5 combine.2
  95.5 9.7 %all-to-all-done.1.x_ref = bf16[16,32,640]{2,1,0:T(8,128)(2,1)S(1)} async-done(((bf16[16,32,640]{2,1,0:T(8,128)(2,1)}), bf16[16,32,640]{2,1,0:T(8,128)(2,1)S(1)}, u32[]{:S(2)}, u32[]{:S(2)}) %all-to-all-start.1) | async-done | bytes 655392 | tf_op jit(solution)/shard_map/all_to_all | solution.py:357
  105.7 4.0 %collective-permute-start.15 = (bf16[32,512]{1,0:T(8,128)(2,1)S(1)}, bf16[32,512]{1,0:T(8,128)(2,1)S(1)}, u32[]{:S(2)}, u32[]{:S(2)}) collective-permute-start(bf16[32,512]{1,0:T(8,128)(2,1)S(1)} %broadcast_select_fusion), channel_id=1, source_target_pairs={{0,8},{8,0},{1,9},{9,1},{2,10},{10,2},{3,11},{11,3},{4,12},{12,4},... | collective-permute-start | bytes 98312 | tf_op jit(solution)/shard_map/ppermute | solution.py:362
  109.8 0.9 collective-permute-done.15
  111.0 1.5 collective-permute-start.17
  112.5 2.4 collective-permute-start.18
  115.0 0.6 collective-permute-done.17
  115.6 2.4 collective-permute-done.18
  118.1 0.9 broadcast_in_dim.66
  118.9 3.6 %all-to-all-start.2 = ((bf16[16,32,512]{2,1,0:T(8,128)(2,1)}), bf16[16,32,512]{2,1,0:T(8,128)(2,1)S(1)}, u32[]{:S(2)}, u32[]{:S(2)}) async-start(bf16[16,32,512]{2,1,0:T(8,128)(2,1)} %bitcast.38), calls=%async_computation.2 | async-start | bytes 1048576 | tf_op jit(solution)/shard_map/all_to_all | solution.py:374
  122.7 9.1 %all-to-all-done.2 = bf16[16,32,512]{2,1,0:T(8,128)(2,1)S(1)} async-done(((bf16[16,32,512]{2,1,0:T(8,128)(2,1)}), bf16[16,32,512]{2,1,0:T(8,128)(2,1)S(1)}, u32[]{:S(2)}, u32[]{:S(2)}) %all-to-all-start.2) | async-done | bytes 524320 | tf_op jit(solution)/shard_map/all_to_all | solution.py:374
  132.3 3.6 %collective-permute-start.19 = (bf16[8,32,512]{2,1,0:T(8,128)(2,1)S(1)}, bf16[8,32,512]{2,1,0:T(8,128)(2,1)S(1)}, u32[]{:S(2)}, u32[]{:S(2)}) collective-permute-start(bf16[8,32,512]{2,1,0:T(8,128)(2,1)S(1)} %fusion.8), channel_id=1, source_target_pairs={{0,8},{8,0},{1,9},{9,1},{2,10},{10,2},{3,11},{11,3},{4,12},{12,4},... | collective-permute-start | bytes 786440 | tf_op jit(solution)/shard_map/ppermute | solution.py:381
  136.0 0.6 reduce-window.6
  137.0 0.8 fusion.6
  137.8 3.4 %all-to-all-start.3 = ((bf16[8,32,512]{2,1,0:T(8,128)(2,1)}), bf16[8,32,512]{2,1,0:T(8,128)(2,1)S(1)}, u32[]{:S(2)}, u32[]{:S(2)}) async-start(bf16[8,32,512]{2,1,0:T(8,128)(2,1)} %fusion.6), calls=%async_computation.3 | async-start | bytes 524288 | tf_op jit(solution)/shard_map/all_to_all | solution.py:382
  141.4 7.1 %all-to-all-done.3 = bf16[8,32,512]{2,1,0:T(8,128)(2,1)S(1)} async-done(((bf16[8,32,512]{2,1,0:T(8,128)(2,1)}), bf16[8,32,512]{2,1,0:T(8,128)(2,1)S(1)}, u32[]{:S(2)}, u32[]{:S(2)}) %all-to-all-start.3) | async-done | bytes 262176 | tf_op jit(solution)/shard_map/all_to_all | solution.py:382
  148.6 1.1 convolution_convert_fusion
  149.7 4.2 %all-to-all-start.4 = ((bf16[16,24,512]{2,1,0:T(8,128)(2,1)}), bf16[16,24,512]{2,1,0:T(8,128)(2,1)S(1)}, u32[]{:S(2)}, u32[]{:S(2)}) async-start(bf16[16,24,512]{2,1,0:T(8,128)(2,1)} %bitcast.45), calls=%async_computation.4 | async-start | bytes 786432 | tf_op jit(solution)/shard_map/all_to_all | solution.py:400
  154.0 8.2 %all-to-all-done.4 = bf16[16,24,512]{2,1,0:T(8,128)(2,1)S(1)} async-done(((bf16[16,24,512]{2,1,0:T(8,128)(2,1)}), bf16[16,24,512]{2,1,0:T(8,128)(2,1)S(1)}, u32[]{:S(2)}, u32[]{:S(2)}) %all-to-all-start.4) | async-done | bytes 393248 | tf_op jit(solution)/shard_map/all_to_all | solution.py:400
  162.2 2.8 %copy-done.1 = bf16[4,512,1536]{2,1,0:T(8,128)(2,1)S(1)} copy-done((bf16[4,512,1536]{2,1,0:T(8,128)(2,1)S(1)}, bf16[4,512,1536]{2,1,0:T(8,128)(2,1)}, u32[]{:S(2)}) %copy-start.1) | copy-done | bytes 6291480
  165.0 2.8 %copy-done.2 = bf16[4,512,1536]{2,1,0:T(8,128)(2,1)S(1)} copy-done((bf16[4,512,1536]{2,1,0:T(8,128)(2,1)S(1)}, bf16[4,512,1536]{2,1,0:T(8,128)(2,1)}, u32[]{:S(2)}) %copy-start.2) | copy-done | bytes 6291480
  167.8 2.8 %gate_up.1 = bf16[384,3200]{1,0:T(8,128)(2,1)S(1)} custom-call(bf16[384,512]{1,0:T(8,128)(2,1)S(1)} %bitcast.95, bf16[384,384]{1,0:T(8,128)(2,1)S(1)} %get-tuple-element.14.perm_ref, f32[1,512]{1,0:T(1,128)S(1)} %bitcast.96, bf16[4,512,1536]{2,1,0:T(8,128)(2,1)S(1)} %copy-done.1, bf16[4,512,1536]{2,1,0:T(8,128)(2,1)S(1)} %copy-done.2), custom_call_target="tpu_custom_call" | custom-call | flops 1207959552 | bytes 14942208 | tf_op jit(solution)/shard_map/gate_up/pallas_call | solution.py:208
  170.6 34.7 %all_to_all.40.x_ref = bf16[8,48,3200]{2,1,0:T(8,128)(2,1)S(1)} all-to-all(bf16[8,48,3200]{2,1,0:T(8,128)(2,1)S(1)} %bitcast.93), channel_id=1, replica_groups=mesh['zl'=2,'x'=4,'core'=2,'zh'=2,'yh'=2,'yl'=2] {'zh','yh','yl'}, dimensions={0} | all-to-all | bytes 4915200 | tf_op jit(solution)/shard_map/all_to_all | solution.py:411
  205.9 18.1 %all_to_all.41 = bf16[8,48,1536]{2,1,0:T(8,128)(2,1)S(1)} all-to-all(bf16[8,48,1536]{2,1,0:T(8,128)(2,1)S(1)} %broadcast_in_dim.69), channel_id=1, replica_groups=mesh['zl'=2,'x'=4,'core'=2,'zh'=2,'yh'=2,'yl'=2] {'zh','yh','yl'}, dimensions={0} | all-to-all | bytes 2359296 | tf_op jit(solution)/shard_map/all_to_all | solution.py:46
  223.9 2.8 %copy-done.3 = bf16[4,1536,512]{2,1,0:T(8,128)(2,1)S(1)} copy-done((bf16[4,1536,512]{2,1,0:T(8,128)(2,1)S(1)}, bf16[4,1536,512]{2,1,0:T(8,128)(2,1)}, u32[]{:S(2)}) %copy-start.3) | copy-done | bytes 6291480
  226.7 2.1 down.1
  228.8 8.4 %all-to-all-start.7 = ((bf16[16,24,512]{2,1,0:T(8,128)(2,1)}), bf16[16,24,512]{2,1,0:T(8,128)(2,1)S(1)}, u32[]{:S(2)}, u32[]{:S(2)}) async-start(bf16[16,24,512]{2,1,0:T(8,128)(2,1)} %bitcast.50), calls=%async_computation.7 | async-start | bytes 786432 | tf_op jit(solution)/shard_map/all_to_all | solution.py:414
  237.5 8.0 %all-to-all-done.7 = bf16[16,24,512]{2,1,0:T(8,128)(2,1)S(1)} async-done(((bf16[16,24,512]{2,1,0:T(8,128)(2,1)}), bf16[16,24,512]{2,1,0:T(8,128)(2,1)S(1)}, u32[]{:S(2)}, u32[]{:S(2)}) %all-to-all-start.7) | async-done | bytes 393248 | tf_op jit(solution)/shard_map/all_to_all | solution.py:414
  245.6 0.8 fusion.1
  (91 shorter events, 4.6 us)
Async XLA Ops:
  0.0 131.8 %copy-start = (bf16[512,512]{1,0:T(8,128)(2,1)S(1)}, bf16[512,512]{1,0:T(8,128)(2,1)}, u32[]{:S(2)}) copy-start(bf16[512,512]{1,0:T(8,128)(2,1)} %param.18) | copy-start | bytes 1572868
  0.0 5.7 %copy-start.19 = (bf16[4,128,512]{2,1,0:T(8,128)(2,1)S(1)}, bf16[4,128,512]{2,1,0:T(8,128)(2,1)}, u32[]{:S(2)}) copy-start(bf16[4,128,512]{2,1,0:T(8,128)(2,1)} %param.15) | copy-start | bytes 1572868
  2.9 3.0 %collective-permute-start = (bf16[32,1152]{1,0:T(8,128)(2,1)S(1)}, bf16[32,1152]{1,0:T(8,128)(2,1)S(1)}, u32[]{:S(2)}, u32[]{:S(2)}) collective-permute-start(bf16[32,1152]{1,0:T(8,128)(2,1)S(1)} %concatenate.14), channel_id=1, source_target_pairs={{0,8},{8,0},{1,9},{9,1},{2,10},{10,2},{3,11},{11,3},{4,12},{12,4},... | collective-permute-start | bytes 221192 | tf_op jit(solution)/shard_map/ppermute | solution.py:336
  5.9 9.1 %collective-permute-start.1 = (bf16[64,1152]{1,0:T(8,128)(2,1)S(1)}, bf16[64,1152]{1,0:T(8,128)(2,1)S(1)}, u32[]{:S(2)}, u32[]{:S(2)}) collective-permute-start(bf16[64,1152]{1,0:T(8,128)(2,1)S(1)} %pad_maximum_fusion.refs_1_), channel_id=1, source_target_pairs={{0,64},{16,80},{32,96},{48,112},{64,0},{80,16},{96,32},{112,48},{1... | collective-permute-start | bytes 442376 | tf_op jit(solution)/shard_map/ppermute | solution.py:346
  7.9 8.2 %collective-permute-start.2 = (bf16[64,1152]{1,0:T(8,128)(2,1)S(1)}, bf16[64,1152]{1,0:T(8,128)(2,1)S(1)}, u32[]{:S(2)}, u32[]{:S(2)}) collective-permute-start(bf16[64,1152]{1,0:T(8,128)(2,1)S(1)} %pad_maximum_fusion.refs_1_), channel_id=1, source_target_pairs={{0,16},{16,32},{32,48},{48,0},{64,80},{80,96},{96,112},{112,64},{1... | collective-permute-start | bytes 442376 | tf_op jit(solution)/shard_map/ppermute | solution.py:346
  9.2 9.7 %collective-permute-start.3 = (bf16[64,1152]{1,0:T(8,128)(2,1)S(1)}, bf16[64,1152]{1,0:T(8,128)(2,1)S(1)}, u32[]{:S(2)}, u32[]{:S(2)}) collective-permute-start(bf16[64,1152]{1,0:T(8,128)(2,1)S(1)} %pad_maximum_fusion.refs_1_), channel_id=1, source_target_pairs={{0,80},{16,96},{32,112},{48,64},{64,16},{80,32},{96,48},{112,0},{1... | collective-permute-start | bytes 442376 | tf_op jit(solution)/shard_map/ppermute | solution.py:346
  10.2 19.4 %collective-permute-start.8 = (bf16[2,4,128,128]{3,2,1,0:T(8,128)(2,1)S(1)}, bf16[2,4,128,128]{3,2,1,0:T(8,128)(2,1)S(1)}, u32[]{:S(2)}, u32[]{:S(2)}) collective-permute-start(bf16[2,4,128,128]{3,2,1,0:T(8,128)(2,1)S(1)} %get-tuple-element.7), channel_id=1, source_target_pairs={{0,1},{1,0},{4,5},{5,4},{2,3},{3,2},{6,7},{7,6},{8,9},{9,8},{12,13... | collective-permute-start | bytes 786440 | tf_op jit(solution)/shard_map/ppermute | solution.py:320
  11.6 20.9 %collective-permute-start.9 = (bf16[2,4,128,128]{3,2,1,0:T(8,128)(2,1)S(1)}, bf16[2,4,128,128]{3,2,1,0:T(8,128)(2,1)S(1)}, u32[]{:S(2)}, u32[]{:S(2)}) collective-permute-start(bf16[2,4,128,128]{3,2,1,0:T(8,128)(2,1)S(1)} %get-tuple-element.6), channel_id=1, source_target_pairs={{0,4},{1,5},{4,0},{5,1},{2,6},{3,7},{6,2},{7,3},{8,12},{9,13},{12,... | collective-permute-start | bytes 786440 | tf_op jit(solution)/shard_map/ppermute | solution.py:320
  15.0 43.7 %copy-start.5 = (bf16[64,1152]{1,0:T(8,128)(2,1)}, bf16[64,1152]{1,0:T(8,128)(2,1)S(1)}, u32[]{:S(2)}) copy-start(bf16[64,1152]{1,0:T(8,128)(2,1)S(1)} %collective-permute-done.1.refs_2_) | copy-start | bytes 442372
  15.0 19.2 %collective-permute-start.10 = (bf16[2,4,128,128]{3,2,1,0:T(8,128)(2,1)S(1)}, bf16[2,4,128,128]{3,2,1,0:T(8,128)(2,1)S(1)}, u32[]{:S(2)}, u32[]{:S(2)}) collective-permute-start(bf16[2,4,128,128]{3,2,1,0:T(8,128)(2,1)S(1)} %get-tuple-element.5), channel_id=1, source_target_pairs={{0,5},{1,4},{4,1},{5,0},{2,7},{3,6},{6,3},{7,2},{8,13},{9,12},{12,... | collective-permute-start | bytes 786440 | tf_op jit(solution)/shard_map/ppermute | solution.py:320
  16.1 42.6 %copy-start.7 = (bf16[64,1152]{1,0:T(8,128)(2,1)}, bf16[64,1152]{1,0:T(8,128)(2,1)S(1)}, u32[]{:S(2)}) copy-start(bf16[64,1152]{1,0:T(8,128)(2,1)S(1)} %collective-permute-done.2.refs_3_) | copy-start | bytes 442372
  16.1 5.8 %collective-permute-start.4 = (bf16[64,1152]{1,0:T(8,128)(2,1)S(1)}, bf16[64,1152]{1,0:T(8,128)(2,1)S(1)}, u32[]{:S(2)}, u32[]{:S(2)}) collective-permute-start(bf16[64,1152]{1,0:T(8,128)(2,1)S(1)} %pad_maximum_fusion.refs_1_), channel_id=1, source_target_pairs={{0,32},{16,48},{32,0},{48,16},{64,96},{80,112},{96,64},{112,80},{1... | collective-permute-start | bytes 442376 | tf_op jit(solution)/shard_map/ppermute | solution.py:346
  18.9 39.9 %copy-start.9 = (bf16[64,1152]{1,0:T(8,128)(2,1)}, bf16[64,1152]{1,0:T(8,128)(2,1)S(1)}, u32[]{:S(2)}) copy-start(bf16[64,1152]{1,0:T(8,128)(2,1)S(1)} %collective-permute-done.3.refs_4_) | copy-start | bytes 442372
  18.9 7.8 %collective-permute-start.5 = (bf16[64,1152]{1,0:T(8,128)(2,1)S(1)}, bf16[64,1152]{1,0:T(8,128)(2,1)S(1)}, u32[]{:S(2)}, u32[]{:S(2)}) collective-permute-start(bf16[64,1152]{1,0:T(8,128)(2,1)S(1)} %pad_maximum_fusion.refs_1_), channel_id=1, source_target_pairs={{0,96},{16,112},{32,64},{48,80},{64,32},{80,48},{96,0},{112,16},{1... | collective-permute-start | bytes 442376 | tf_op jit(solution)/shard_map/ppermute | solution.py:346
  21.9 36.8 %copy-start.11 = (bf16[64,1152]{1,0:T(8,128)(2,1)}, bf16[64,1152]{1,0:T(8,128)(2,1)S(1)}, u32[]{:S(2)}) copy-start(bf16[64,1152]{1,0:T(8,128)(2,1)S(1)} %collective-permute-done.4.refs_5_) | copy-start | bytes 442372
  21.9 12.3 %collective-permute-start.6 = (bf16[64,1152]{1,0:T(8,128)(2,1)S(1)}, bf16[64,1152]{1,0:T(8,128)(2,1)S(1)}, u32[]{:S(2)}, u32[]{:S(2)}) collective-permute-start(bf16[64,1152]{1,0:T(8,128)(2,1)S(1)} %pad_maximum_fusion.refs_1_), channel_id=1, source_target_pairs={{0,48},{16,0},{32,16},{48,32},{64,112},{80,64},{96,80},{112,96},{1... | collective-permute-start | bytes 442376 | tf_op jit(solution)/shard_map/ppermute | solution.py:346
  26.6 0.7 copy-start.13
  27.3 13.4 %collective-permute-start.11 = (bf16[2,4,128,128]{3,2,1,0:T(8,128)(2,1)S(1)}, bf16[2,4,128,128]{3,2,1,0:T(8,128)(2,1)S(1)}, u32[]{:S(2)}, u32[]{:S(2)}) collective-permute-start(bf16[2,4,128,128]{3,2,1,0:T(8,128)(2,1)S(1)} %get-tuple-element.8.refs_9_), channel_id=1, source_target_pairs={{0,8},{8,0},{1,9},{9,1},{2,10},{10,2},{3,11},{11,3},{4,12},{12,4},... | collective-permute-start | bytes 786440 | tf_op jit(solution)/shard_map/ppermute | solution.py:321
  29.6 11.1 %collective-permute-start.12 = (bf16[2,4,128,128]{3,2,1,0:T(8,128)(2,1)S(1)}, bf16[2,4,128,128]{3,2,1,0:T(8,128)(2,1)S(1)}, u32[]{:S(2)}, u32[]{:S(2)}) collective-permute-start(bf16[2,4,128,128]{3,2,1,0:T(8,128)(2,1)S(1)} %collective-permute-done.8.refs_10_), channel_id=1, source_target_pairs={{0,8},{8,0},{1,9},{9,1},{2,10},{10,2},{3,11},{11,3},{4,12},{12,4},... | collective-permute-start | bytes 786440 | tf_op jit(solution)/shard_map/ppermute | solution.py:321
  32.5 8.3 %collective-permute-start.13 = (bf16[2,4,128,128]{3,2,1,0:T(8,128)(2,1)S(1)}, bf16[2,4,128,128]{3,2,1,0:T(8,128)(2,1)S(1)}, u32[]{:S(2)}, u32[]{:S(2)}) collective-permute-start(bf16[2,4,128,128]{3,2,1,0:T(8,128)(2,1)S(1)} %collective-permute-done.9.refs_11_), channel_id=1, source_target_pairs={{0,8},{8,0},{1,9},{9,1},{2,10},{10,2},{3,11},{11,3},{4,12},{12,4},... | collective-permute-start | bytes 786440 | tf_op jit(solution)/shard_map/ppermute | solution.py:321
  34.1 6.6 %collective-permute-start.14 = (bf16[2,4,128,128]{3,2,1,0:T(8,128)(2,1)S(1)}, bf16[2,4,128,128]{3,2,1,0:T(8,128)(2,1)S(1)}, u32[]{:S(2)}, u32[]{:S(2)}) collective-permute-start(bf16[2,4,128,128]{3,2,1,0:T(8,128)(2,1)S(1)} %collective-permute-done.10.refs_12_), channel_id=1, source_target_pairs={{0,8},{8,0},{1,9},{9,1},{2,10},{10,2},{3,11},{11,3},{4,12},{12,4},... | collective-permute-start | bytes 786440 | tf_op jit(solution)/shard_map/ppermute | solution.py:321
  34.2 0.7 copy-start.16
  34.8 5.9 %collective-permute-start.7 = (bf16[64,1152]{1,0:T(8,128)(2,1)S(1)}, bf16[64,1152]{1,0:T(8,128)(2,1)}, u32[]{:S(2)}, u32[]{:S(2)}) collective-permute-start(bf16[64,1152]{1,0:T(8,128)(2,1)S(1)} %pad_maximum_fusion.refs_1_), channel_id=1, source_target_pairs={{0,112},{16,64},{32,80},{48,96},{64,48},{80,0},{96,16},{112,32},{1... | collective-permute-start | bytes 442376 | tf_op jit(solution)/shard_map/ppermute | solution.py:346
  40.7 0.9 copy-start.14
  41.7 0.9 copy-start.17
  58.7 28.7 %all-to-all-start = ((bf16[16,32,640]{2,1,0:T(8,128)(2,1)}), bf16[16,32,640]{2,1,0:T(8,128)(2,1)S(1)}, u32[]{:S(2)}, u32[]{:S(2)}) async-start(bf16[16,32,640]{2,1,0:T(8,128)(2,1)} %bitcast.29), calls=%async_computation | async-start | bytes 1310720 | tf_op jit(solution)/shard_map/all_to_all | solution.py:357
  65.8 0.9 copy-start.6
  66.7 0.9 copy-start.8
  67.6 0.9 copy-start.10
  68.5 0.9 copy-start.12
  69.4 0.9 copy-start.15
  70.3 0.9 copy-start.18
  87.4 17.8 %all-to-all-start.1 = ((bf16[16,32,640]{2,1,0:T(8,128)(2,1)}), bf16[16,32,640]{2,1,0:T(8,128)(2,1)S(1)}, u32[]{:S(2)}, u32[]{:S(2)}) async-start(bf16[16,32,640]{2,1,0:T(8,128)(2,1)} %bitcast.30), calls=%async_computation.1 | async-start | bytes 1310720 | tf_op jit(solution)/shard_map/all_to_all | solution.py:357
  95.0 27.5 %copy-start.21 = (s32[32,8]{0,1:T(8,128)S(1)}, s32[32,8]{0,1:T(8,128)}, u32[]{:S(2)}) copy-start(s32[32,8]{0,1:T(8,128)} %param.21) | copy-start | bytes 3076
  105.7 4.9 %collective-permute-start.15 = (bf16[32,512]{1,0:T(8,128)(2,1)S(1)}, bf16[32,512]{1,0:T(8,128)(2,1)S(1)}, u32[]{:S(2)}, u32[]{:S(2)}) collective-permute-start(bf16[32,512]{1,0:T(8,128)(2,1)S(1)} %broadcast_select_fusion), channel_id=1, source_target_pairs={{0,8},{8,0},{1,9},{9,1},{2,10},{10,2},{3,11},{11,3},{4,12},{12,4},... | collective-permute-start | bytes 98312 | tf_op jit(solution)/shard_map/ppermute | solution.py:362
  110.7 4.3 %collective-permute-start.16 = (bf16[2,32,512]{2,1,0:T(8,128)(2,1)S(1)}, bf16[2,32,512]{2,1,0:T(8,128)(2,1)S(1)}, u32[]{:S(2)}, u32[]{:S(2)}) collective-permute-start(bf16[2,32,512]{2,1,0:T(8,128)(2,1)S(1)} %pad_maximum_fusion.1), channel_id=1, source_target_pairs={{0,1},{1,0},{4,5},{5,4},{2,3},{3,2},{6,7},{7,6},{8,9},{9,8},{12,13... | collective-permute-start | bytes 196616 | tf_op jit(solution)/shard_map/ppermute | solution.py:370
  111.0 4.6 %collective-permute-start.17 = (bf16[2,32,512]{2,1,0:T(8,128)(2,1)S(1)}, bf16[2,32,512]{2,1,0:T(8,128)(2,1)S(1)}, u32[]{:S(2)}, u32[]{:S(2)}) collective-permute-start(bf16[2,32,512]{2,1,0:T(8,128)(2,1)S(1)} %pad_maximum_fusion.1), channel_id=1, source_target_pairs={{0,4},{1,5},{4,0},{5,1},{2,6},{3,7},{6,2},{7,3},{8,12},{9,13},{12,... | collective-permute-start | bytes 196616 | tf_op jit(solution)/shard_map/ppermute | solution.py:370
  112.5 5.5 %collective-permute-start.18 = (bf16[2,32,512]{2,1,0:T(8,128)(2,1)S(1)}, bf16[2,32,512]{2,1,0:T(8,128)(2,1)S(1)}, u32[]{:S(2)}, u32[]{:S(2)}) collective-permute-start(bf16[2,32,512]{2,1,0:T(8,128)(2,1)S(1)} %pad_maximum_fusion.1), channel_id=1, source_target_pairs={{0,5},{1,4},{4,1},{5,0},{2,7},{3,6},{6,3},{7,2},{8,13},{9,12},{12,... | collective-permute-start | bytes 196616 | tf_op jit(solution)/shard_map/ppermute | solution.py:370
  118.9 12.9 %all-to-all-start.2 = ((bf16[16,32,512]{2,1,0:T(8,128)(2,1)}), bf16[16,32,512]{2,1,0:T(8,128)(2,1)S(1)}, u32[]{:S(2)}, u32[]{:S(2)}) async-start(bf16[16,32,512]{2,1,0:T(8,128)(2,1)} %bitcast.38), calls=%async_computation.2 | async-start | bytes 1048576 | tf_op jit(solution)/shard_map/all_to_all | solution.py:374
  131.8 16.8 %copy-start.20 = (bf16[32,512]{1,0:T(8,128)(2,1)S(1)}, bf16[32,512]{1,0:T(8,128)(2,1)}, u32[]{:S(2)}) copy-start(bf16[32,512]{1,0:T(8,128)(2,1)} %param.19) | copy-start | bytes 98308
  132.2 30.0 %copy-start.4 = (f32[512]{0:T(512)S(1)}, f32[512]{0:T(512)}, u32[]{:S(2)}) copy-start(f32[512]{0:T(512)} %param.20) | copy-start | bytes 6148
  132.3 4.7 %collective-permute-start.19 = (bf16[8,32,512]{2,1,0:T(8,128)(2,1)S(1)}, bf16[8,32,512]{2,1,0:T(8,128)(2,1)S(1)}, u32[]{:S(2)}, u32[]{:S(2)}) collective-permute-start(bf16[8,32,512]{2,1,0:T(8,128)(2,1)S(1)} %fusion.8), channel_id=1, source_target_pairs={{0,8},{8,0},{1,9},{9,1},{2,10},{10,2},{3,11},{11,3},{4,12},{12,4},... | collective-permute-start | bytes 786440 | tf_op jit(solution)/shard_map/ppermute | solution.py:381
  137.8 10.8 %all-to-all-start.3 = ((bf16[8,32,512]{2,1,0:T(8,128)(2,1)}), bf16[8,32,512]{2,1,0:T(8,128)(2,1)S(1)}, u32[]{:S(2)}, u32[]{:S(2)}) async-start(bf16[8,32,512]{2,1,0:T(8,128)(2,1)} %fusion.6), calls=%async_computation.3 | async-start | bytes 524288 | tf_op jit(solution)/shard_map/all_to_all | solution.py:382
  149.7 12.5 %all-to-all-start.4 = ((bf16[16,24,512]{2,1,0:T(8,128)(2,1)}), bf16[16,24,512]{2,1,0:T(8,128)(2,1)S(1)}, u32[]{:S(2)}, u32[]{:S(2)}) async-start(bf16[16,24,512]{2,1,0:T(8,128)(2,1)} %bitcast.45), calls=%async_computation.4 | async-start | bytes 786432 | tf_op jit(solution)/shard_map/all_to_all | solution.py:400
  162.2 2.8 %copy-start.1 = (bf16[4,512,1536]{2,1,0:T(8,128)(2,1)S(1)}, bf16[4,512,1536]{2,1,0:T(8,128)(2,1)}, u32[]{:S(2)}) copy-start(bf16[4,512,1536]{2,1,0:T(8,128)(2,1)} %gate_ref.1) | copy-start | bytes 18874372
  165.0 2.8 %copy-start.2 = (bf16[4,512,1536]{2,1,0:T(8,128)(2,1)S(1)}, bf16[4,512,1536]{2,1,0:T(8,128)(2,1)}, u32[]{:S(2)}) copy-start(bf16[4,512,1536]{2,1,0:T(8,128)(2,1)} %up_ref.1) | copy-start | bytes 18874372
  223.9 2.8 %copy-start.3 = (bf16[4,1536,512]{2,1,0:T(8,128)(2,1)S(1)}, bf16[4,1536,512]{2,1,0:T(8,128)(2,1)}, u32[]{:S(2)}) copy-start(bf16[4,1536,512]{2,1,0:T(8,128)(2,1)} %down_ref.1) | copy-start | bytes 18874372
  226.7 10.5 %copy-start.22 = (f32[32,8]{0,1:T(8,128)S(1)}, f32[32,8]{0,1:T(8,128)}, u32[]{:S(2)}) copy-start(f32[32,8]{0,1:T(8,128)} %param.22) | copy-start | bytes 3076
  228.8 16.6 %all-to-all-start.7 = ((bf16[16,24,512]{2,1,0:T(8,128)(2,1)}), bf16[16,24,512]{2,1,0:T(8,128)(2,1)S(1)}, u32[]{:S(2)}, u32[]{:S(2)}) async-start(bf16[16,24,512]{2,1,0:T(8,128)(2,1)} %bitcast.50), calls=%async_computation.7 | async-start | bytes 786432 | tf_op jit(solution)/shard_map/all_to_all | solution.py:414

commit v3 on v2

--- a/solution.py
+++ b/solution.py
@@ -24,7 +24,9 @@
 LANES = 128
 BLK = ("zl", "x", "core")
 NARROW = ("zh", "yh", "yl")
-VMEM_LIMIT = 32 * 1024 * 1024
+SAFE_POWER = 60.0
+VMEM_LIMIT = 40 * 1024 * 1024
+LARGE_LIMIT = 56 * 1024 * 1024
 SMALL_LIMIT = 12 * 1024 * 1024
 
 
@@ -40,70 +42,67 @@
     return high, mid, low
 
 
-def gather_by_exchange(value, axis):
-    length = lax.axis_size(axis)
-    spread = jnp.broadcast_to(value[None], (length,) + value.shape)
-    return lax.all_to_all(spread, axis, 0, 0)
-
-
-def attention_kernel(start, heads, *refs):
-    info_ref = refs[0]
-    q_refs = refs[1:9]
-    kv_refs = refs[9:17]
-    out_ref, q_ref, k_ref, vt_ref, lim_ref, s_ref = refs[17:]
+def attention_kernel(heads, info_ref, *refs):
+    q_in = refs[0:4]
+    kv_in = refs[4:12]
+    out_ref, q_ref, k_ref, v_ref, vt_ref, lim_ref, mask_ref, s_ref, lse_ref, sem = refs[12:]
     rows = q_ref.shape[0]
-    base = q_refs[0].shape[1] - LANES
-    chip, core, my_yh = info_ref[0], info_ref[1], info_ref[2]
-    sources = len(kv_refs) // 2
-    blocks = kv_refs[0].shape[1]
+    base = heads * HEAD_SIZE
+    chip, core = info_ref[0], info_ref[1]
+    chip_blocks, sources = k_ref.shape[:2]
+    blocks = chip_blocks // 2
     span = sources * LANES
-    step = rows // len(q_refs)
-
-    for i, ref in enumerate(q_refs):
-        q_ref[i * step : (i + 1) * step, :] = ref[...]
+    tokens = chip_blocks * span
+    step = rows // len(q_in)
+    factor = SCORE_SCALE * LOG2E
+
+    copies = []
+    for i, ref in enumerate(q_in):
+        at = pl.ds(i * step, step)
+        copies.append(pltpu.make_async_copy(ref, q_ref.at[at], sem.at[len(copies)]))
+    for i, ref in enumerate(kv_in):
+        side, s = i // sources, i % sources
+        for part, target in enumerate((k_ref, v_ref)):
+            to = target.at[pl.ds(side * blocks, blocks), s]
+            copies.append(pltpu.make_async_copy(ref.at[part], to, sem.at[len(copies)]))
+    for copy in copies:
+        copy.start()
+    for copy in copies:
+        copy.wait()
+
     extra = q_ref[:, base:].astype(jnp.float32).T
     lim_ref[...] = extra
     length = extra[TREE_BLOCKS : TREE_BLOCKS + 1] * 256.0 + extra[TREE_BLOCKS + 1 : TREE_BLOCKS + 2]
-    chip_blocks = 2 * blocks
     first = pl.multiple_of(chip * chip_blocks, chip_blocks)
-    mask = lim_ref[pl.ds(first, chip_blocks), :]
+    reads = lim_ref[pl.ds(first, chip_blocks), :]
     block_id = lax.broadcasted_iota(jnp.int32, (chip_blocks, rows), 0) + first
     bound = length - (block_id * BLOCK_TOKENS).astype(jnp.float32)
-    bound = jnp.where(mask > 0.5, bound, 0.0)
-    lim_ref[0:chip_blocks, :] = bound
-    sub = lax.broadcasted_iota(jnp.int32, (16, blocks * 2 * span), 0)
+    lim_ref[0:chip_blocks, :] = jnp.where(reads > 0.5, bound, 0.0)
+    token = lax.broadcasted_iota(jnp.int32, (LANES, 1), 0)
+    token = [
+        (token + info_ref[4 + s] * LANES).astype(jnp.float32) for s in range(sources)
+    ]
+    token = jnp.concatenate(token, axis=0)
+    sub = lax.broadcasted_iota(jnp.int32, (16, tokens), 0)
     vt_ref[HEAD_SIZE:, :] = jnp.where(sub == 0, 1.0, 0.0).astype(jnp.bfloat16)
-    for side in range(2):
-        for i in range(blocks):
-            for s in range(sources):
-                at = (side * blocks + i) * span + s * LANES
-                ref = kv_refs[side * sources + s]
-                k_ref[at : at + LANES, :] = ref[0, i]
-                vt_ref[:HEAD_SIZE, at : at + LANES] = ref[1, i].T
-
-    token = lax.broadcasted_iota(jnp.int32, (LANES, 1), 0) + my_yh * (2 * LANES)
-    token = [(token + info_ref[4 + s] * LANES).astype(jnp.float32) for s in range(sources)]
-    token = jnp.concatenate(token, axis=0)
-    sub_row = lax.broadcasted_iota(jnp.int32, (8, rows), 0)
-
-    def one_head(h, info):
-        cols = pl.ds(pl.multiple_of(h * HEAD_SIZE, HEAD_SIZE), HEAD_SIZE)
-        q_cols = pl.ds(pl.multiple_of((start + h) * HEAD_SIZE, HEAD_SIZE), HEAD_SIZE)
-        qt = q_ref[:, q_cols].T
-        top = jnp.full((1, rows), -1e29, jnp.float32)
-        for i in range(2 * blocks):
-            at = slice(i * span, (i + 1) * span)
-            side = core if i < blocks else 1 - core
-            lim = lim_ref[pl.ds(side * blocks + i % blocks, 1), :]
-            s = jnp.dot(k_ref[at, :], qt, preferred_element_type=jnp.float32)
-            s = jnp.where(token < lim, s, NEGATIVE_FILLER)
-            s_ref[at, :] = s
-            top = jnp.maximum(top, jnp.max(s, axis=0, keepdims=True))
-        acc = jnp.zeros((HEAD_SIZE + 16, rows), jnp.float32)
-        for i in range(2 * blocks):
-            at = slice(i * span, (i + 1) * span)
-            p = jnp.exp2((s_ref[at, :] - top) * (SCORE_SCALE * LOG2E)).astype(jnp.bfloat16)
-            acc = acc + jnp.dot(vt_ref[:, at], p, preferred_element_type=jnp.float32)
+    most_k = jnp.zeros((LANES, 1), jnp.float32)
+    for i in range(chip_blocks):
+        at = slice(i * span, (i + 1) * span)
+        vt_ref[:HEAD_SIZE, at] = v_ref[i].reshape(span, HEAD_SIZE).T
+        side = core if i < blocks else 1 - core
+        lim = lim_ref[pl.ds(side * blocks + i % blocks, 1), :]
+        mask_ref[at, :] = jnp.where(token < lim, 1.0, 0.0).astype(jnp.bfloat16)
+        for s in range(sources):
+            keys = k_ref[i, s].astype(jnp.float32)
+            most_k = jnp.maximum(most_k, jnp.sum(keys * keys, axis=1, keepdims=True))
+    most_q = jnp.zeros((rows, 1), jnp.float32)
+    for h in range(heads):
+        q = q_ref[:, h * HEAD_SIZE : (h + 1) * HEAD_SIZE].astype(jnp.float32)
+        most_q = jnp.maximum(most_q, jnp.sum(q * q, axis=1, keepdims=True))
+    most = jnp.max(most_q) * jnp.max(most_k) * (factor * factor)
+    small = most <= SAFE_POWER * SAFE_POWER
+
+    def finish(h, cols, acc, top):
         total = acc[HEAD_SIZE : HEAD_SIZE + 1]
         some = total > 0
         safe = jnp.where(some, total, 1.0)
@@ -113,37 +112,87 @@
             row = pl.multiple_of(info_ref[8 + i] * group, group)
             out_ref[pl.ds(row, group), cols] = result[i * group : (i + 1) * group]
         lse = jnp.where(some, top * SCORE_SCALE + jnp.log(safe), NEGATIVE_FILLER)
-        return jnp.where(sub_row == h, lse, info)
-
-    info = lax.fori_loop(0, heads, one_head, jnp.zeros((8, rows), jnp.float32))
-    high, mid, low = split_bf16(info)
+        lse_ref[pl.ds(h, 1), :] = lse
+
+    def head_columns(h):
+        return pl.ds(pl.multiple_of(h * HEAD_SIZE, HEAD_SIZE), HEAD_SIZE)
+
+    chunk = 2
+
+    def small_head(h, carry):
+        cols = head_columns(h)
+        qt = q_ref[:, cols].T
+        acc = jnp.zeros((HEAD_SIZE + 16, rows), jnp.float32)
+        for i in range(0, chip_blocks, chunk):
+            at = slice(i * span, (i + chunk) * span)
+            keys = k_ref[i : i + chunk].reshape(chunk * span, HEAD_SIZE)
+            s = jnp.dot(keys, qt, preferred_element_type=jnp.float32) * factor
+            p = jnp.exp2(s).astype(jnp.bfloat16) * mask_ref[at, :]
+            acc = acc + jnp.dot(vt_ref[:, at], p, preferred_element_type=jnp.float32)
+        finish(h, cols, acc, 0.0)
+        return carry
+
+    def any_head(h, carry):
+        cols = head_columns(h)
+        qt = q_ref[:, cols].T
+        top = jnp.full((1, rows), -1e29, jnp.float32)
+        for i in range(chip_blocks):
+            at = slice(i * span, (i + 1) * span)
+            keys = k_ref[i].reshape(span, HEAD_SIZE)
+            s = jnp.dot(keys, qt, preferred_element_type=jnp.float32)
+            s = jnp.where(mask_ref[at, :].astype(jnp.float32) > 0.5, s, NEGATIVE_FILLER)
+            s_ref[at, :] = s
+            top = jnp.maximum(top, jnp.max(s, axis=0, keepdims=True))
+        acc = jnp.zeros((HEAD_SIZE + 16, rows), jnp.float32)
+        for i in range(chip_blocks):
+            at = slice(i * span, (i + 1) * span)
+            p = jnp.exp2((s_ref[at, :] - top) * factor).astype(jnp.bfloat16)
+            acc = acc + jnp.dot(vt_ref[:, at], p, preferred_element_type=jnp.float32)
+        finish(h, cols, acc, top)
+        return carry
+
+    @pl.when(small)
+    def _():
+        lax.fori_loop(0, heads, small_head, 0)
+
+    @pl.when(jnp.logical_not(small))
+    def _():
+        lax.fori_loop(0, heads, any_head, 0)
+
+    high, mid, low = split_bf16(lse_ref[...])
     pieces = [piece.astype(jnp.float32) for piece in (high, mid, low)]
-    pieces.append(jnp.zeros((LANES - 24, rows), jnp.float32))
+    pieces.append(jnp.zeros((LANES - 3 * heads, rows), jnp.float32))
     result = jnp.concatenate(pieces, axis=0).T.astype(jnp.bfloat16)
     group = rows // 16
     for i in range(16):
         row = pl.multiple_of(info_ref[8 + i] * group, group)
-        out_ref[pl.ds(row, group), heads * HEAD_SIZE :] = result[i * group : (i + 1) * group]
-
-
-def attention(info, queries, kv, start, heads):
+        out_ref[pl.ds(row, group), base:] = result[i * group : (i + 1) * group]
+
+
+def attention(info, queries, kv):
     step, width = queries[0].shape
     rows = step * len(queries)
-    out_width = heads * HEAD_SIZE + LANES
+    heads = (width - LANES) // HEAD_SIZE
     blocks = kv[0].shape[1]
+    sources = len(kv) // 2
     tokens = len(kv) * blocks * LANES
-    vmem = pl.BlockSpec(memory_space=pltpu.VMEM)
+    anywhere = pl.BlockSpec(memory_space=pl.ANY)
+    tiles = (2 * blocks, sources, LANES, HEAD_SIZE)
     return pl.pallas_call(
-        functools.partial(attention_kernel, start, heads),
-        in_specs=[pl.BlockSpec(memory_space=pltpu.SMEM)] + [vmem] * (len(queries) + len(kv)),
-        out_specs=vmem,
-        out_shape=jax.ShapeDtypeStruct((rows, out_width), jnp.bfloat16),
+        functools.partial(attention_kernel, heads),
+        in_specs=[pl.BlockSpec(memory_space=pltpu.SMEM)] + [anywhere] * (len(queries) + len(kv)),
+        out_specs=pl.BlockSpec(memory_space=pltpu.VMEM),
+        out_shape=jax.ShapeDtypeStruct((rows, width), jnp.bfloat16),
         scratch_shapes=[
             pltpu.VMEM((rows, width), jnp.bfloat16),
-            pltpu.VMEM((tokens, HEAD_SIZE), jnp.bfloat16),
+            pltpu.VMEM(tiles, jnp.bfloat16),
+            pltpu.VMEM(tiles, jnp.bfloat16),
             pltpu.VMEM((HEAD_SIZE + 16, tokens), jnp.bfloat16),
             pltpu.VMEM((LANES, rows), jnp.float32),
+            pltpu.VMEM((tokens, rows), jnp.bfloat16),
             pltpu.VMEM((tokens, rows), jnp.float32),
+            pltpu.VMEM((heads, rows), jnp.float32),
+            pltpu.SemaphoreType.DMA((len(queries) + 2 * len(kv),)),
         ],
         compiler_params=params(limit=VMEM_LIMIT),
         cost_estimate=pl.CostEstimate(
@@ -180,9 +229,19 @@
     )(parts)
 
 
-def gate_up_kernel(x_ref, perm_ref, gain_ref, gate_ref, up_ref, out_ref):
+def gate_up_kernel(x_ref, perm_ref, gain_ref, gate_hbm, up_hbm, out_ref, gate_ref, up_ref, sem):
     experts, _, width = gate_ref.shape
     count = x_ref.shape[0] // experts
+    copies = [
+        [
+            pltpu.make_async_copy(gate_hbm.at[e], gate_ref.at[e], sem.at[0, e]),
+            pltpu.make_async_copy(up_hbm.at[e], up_ref.at[e], sem.at[1, e]),
+        ]
+        for e in range(experts)
+    ]
+    for pair in copies:
+        for copy in pair:
+            copy.start()
     for e in range(experts):
         at = slice(e * count, (e + 1) * count)
         rows = jnp.dot(perm_ref[at, :], x_ref[...], preferred_element_type=jnp.float32)
@@ -193,9 +252,11 @@
         pad = jnp.where(lane == 0, high.astype(jnp.float32), 0.0)
         pad = jnp.where(lane == 1, mid.astype(jnp.float32), pad)
         out_ref[at, 2 * width :] = pad.astype(jnp.bfloat16)
+        copies[e][0].wait()
         out_ref[at, :width] = jnp.dot(
             scaled, gate_ref[e], preferred_element_type=jnp.float32
         ).astype(jnp.bfloat16)
+        copies[e][1].wait()
         out_ref[at, width : 2 * width] = jnp.dot(
             scaled, up_ref[e], preferred_element_type=jnp.float32
         ).astype(jnp.bfloat16)
@@ -205,12 +266,18 @@
     experts, depth, ff = gate_proj.shape
     slots = x.shape[0]
     vmem = pl.BlockSpec(memory_space=pltpu.VMEM)
+    anywhere = pl.BlockSpec(memory_space=pl.ANY)
     return pl.pallas_call(
         gate_up_kernel,
-        in_specs=[vmem] * 5,
+        in_specs=[vmem] * 3 + [anywhere] * 2,
         out_specs=vmem,
         out_shape=jax.ShapeDtypeStruct((slots, 2 * ff + LANES), jnp.bfloat16),
-        compiler_params=params(limit=SMALL_LIMIT),
+        scratch_shapes=[
+            pltpu.VMEM(gate_proj.shape, jnp.bfloat16),
+            pltpu.VMEM(up_proj.shape, jnp.bfloat16),
+            pltpu.SemaphoreType.DMA((2, experts)),
+        ],
+        compiler_params=params(limit=LARGE_LIMIT),
         cost_estimate=pl.CostEstimate(
             flops=4 * slots * depth * ff,
             bytes_accessed=4 * experts * depth * ff + 4 * slots * ff,
@@ -221,9 +288,7 @@
 
 
 def activate_kernel(x_ref, out_ref):
-    ff = out_ref.shape[1]
-    rows = out_ref.shape[0]
-    parts = x_ref.shape[0]
+    parts, rows, ff = out_ref.shape
     squares = jnp.zeros((rows, 1), jnp.float32)
     for part in range(parts):
         pad = x_ref[part, :, 2 * ff :].astype(jnp.float32)
@@ -238,24 +303,32 @@
             up = up + x_ref[part, :, ff + at : ff + at + step].astype(jnp.float32)
         gate = gate * inv_rms
         up = up * inv_rms
-        out_ref[:, at : at + step] = (gate / (1.0 + jnp.exp(-gate)) * up).astype(jnp.bfloat16)
+        result = (gate / (1.0 + jnp.exp(-gate)) * up).astype(jnp.bfloat16)
+        for part in range(parts):
+            out_ref[part, :, at : at + step] = result
 
 
 def activate(parts):
-    _, rows, width = parts.shape
+    count, rows, width = parts.shape
     return pl.pallas_call(
         activate_kernel,
-        out_shape=jax.ShapeDtypeStruct((rows, (width - LANES) // 2), jnp.bfloat16),
+        out_shape=jax.ShapeDtypeStruct((count, rows, (width - LANES) // 2), jnp.bfloat16),
         compiler_params=params(limit=SMALL_LIMIT),
         name="activate",
     )(parts)
 
 
-def down_kernel(act_ref, back_ref, down_ref, out_ref, all_ref):
+def down_kernel(act_ref, back_ref, down_hbm, out_ref, all_ref, down_ref, sem):
     experts = down_ref.shape[0]
     count = act_ref.shape[0] // experts
+    copies = [
+        pltpu.make_async_copy(down_hbm.at[e], down_ref.at[e], sem.at[e]) for e in range(experts)
+    ]
+    for copy in copies:
+        copy.start()
     for e in range(experts):
         at = slice(e * count, (e + 1) * count)
+        copies[e].wait()
         all_ref[at, :] = jnp.dot(
             act_ref[at, :], down_ref[e], preferred_element_type=jnp.float32
         ).astype(jnp.bfloat16)
@@ -270,11 +343,15 @@
     vmem = pl.BlockSpec(memory_space=pltpu.VMEM)
     return pl.pallas_call(
         down_kernel,
-        in_specs=[vmem] * 3,
+        in_specs=[vmem] * 2 + [pl.BlockSpec(memory_space=pl.ANY)],
         out_specs=vmem,
         out_shape=jax.ShapeDtypeStruct((slots, width), jnp.bfloat16),
-        scratch_shapes=[pltpu.VMEM((slots, width), jnp.bfloat16)],
-        compiler_params=params(limit=SMALL_LIMIT),
+        scratch_shapes=[
+            pltpu.VMEM((slots, width), jnp.bfloat16),
+            pltpu.VMEM(down_proj.shape, jnp.bfloat16),
+            pltpu.SemaphoreType.DMA((experts,)),
+        ],
+        compiler_params=params(limit=LARGE_LIMIT),
         cost_estimate=pl.CostEstimate(
             flops=2 * slots * ff * width,
             bytes_accessed=2 * experts * ff * width,
@@ -305,20 +382,11 @@
     n_narrow = lax.axis_size(NARROW)
     zl, x, core = (lax.axis_index(name) for name in BLK)
     zh, yh, yl = (lax.axis_index(name) for name in NARROW)
-    kv_head = zh * 2 + yl
+    kv_head = yh * 2 + yl
     heads = QUERY_HEADS // n_narrow
     width = heads * HEAD_SIZE
     swap = [(0, 1), (1, 0)]
     size_x = lax.axis_size("x")
-
-    kv = jnp.stack([tree_key_cache, tree_value_cache])
-    kv = kv.reshape(2, blocks, part_tokens, KEY_VALUE_HEADS, HEAD_SIZE).transpose(3, 0, 1, 2, 4)
-    own_kv = [lax.dynamic_index_in_dim(kv, kv_head, 0, False)]
-    for step in range(1, KEY_VALUE_HEADS):
-        piece = lax.dynamic_index_in_dim(kv, kv_head ^ step, 0, False)
-        pairs = [(i, i ^ step) for i in range(KEY_VALUE_HEADS)]
-        own_kv.append(lax.ppermute(piece, ("zh", "yl"), pairs))
-    kv = own_kv + [lax.ppermute(piece, "core", swap) for piece in own_kv]
 
     both = lax.dynamic_slice_in_dim(queries, kv_head * 2 * width, 2 * width, 1)
     extra = jnp.concatenate(
@@ -335,27 +403,40 @@
     own_q = jnp.concatenate([own_q, extra], axis=1)
     other_q = lax.ppermute(jnp.concatenate([other_q, extra], axis=1), "core", swap)
     pair = jnp.concatenate([own_q, other_q], axis=0)
-    all_q, groups = [], []
+    pair = jnp.concatenate([pair, lax.ppermute(pair, "zl", swap)], axis=0)
+
+    def head_piece(head):
+        at = head * HEAD_SIZE
+        return jnp.stack(
+            [
+                lax.dynamic_slice_in_dim(cache, at, HEAD_SIZE, 2) + other_q[0, 0] * 0
+                for cache in (tree_key_cache, tree_value_cache)
+            ]
+        )
+
+    kv = [head_piece(kv_head)]
+    for step in range(1, KEY_VALUE_HEADS):
+        pairs = [(i, i ^ step) for i in range(KEY_VALUE_HEADS)]
+        kv.append(lax.ppermute(head_piece(kv_head ^ step), ("yh", "yl"), pairs))
+    kv = kv + [lax.ppermute(piece, "core", swap) for piece in kv]
+    sources = [zh * KEY_VALUE_HEADS + (kv_head ^ s) for s in range(KEY_VALUE_HEADS)]
+
+    all_q, groups = [pair], []
     for dx in range(size_x):
+        if dx:
+            pairs = [(i, (i + dx) % size_x) for i in range(size_x)]
+            all_q.append(lax.ppermute(pair, "x", pairs))
         for dz in range(2):
-            pairs = [
-                (z * size_x + i, (z ^ dz) * size_x + (i + dx) % size_x)
-                for z in range(2)
-                for i in range(size_x)
-            ]
-            all_q.append(lax.ppermute(pair, ("zl", "x"), pairs) if dx + dz else pair)
             origin = (zl ^ dz) * size_x + (x - dx) % size_x
             groups += [origin * 2 + core, origin * 2 + (1 - core)]
-    sources = [((kv_head ^ s) // 2) * 4 + (kv_head ^ s) % 2 for s in range(KEY_VALUE_HEADS)]
     zero = jnp.int32(0)
-    info = [zl * size_x + x, core, yh, zero] + sources + groups
+    info = [zl * size_x + x, core, zero, zero] + sources + groups
     info = jnp.stack([value.astype(jnp.int32) for value in info])
-    group_axes = ("zl", "x", "yh")
-    attended = []
-    for half in range(2):
-        partial = attention(info, all_q, kv, half * (heads // 2), heads // 2)
-        partial = lax.all_to_all(partial.reshape(n_blk, rows, -1), group_axes, 0, 0)
-        attended.append(combine(partial, heads // 2))
+    group_axes = ("zl", "x", "zh")
+    partial = attention(info, all_q, kv)
+    partial = lax.all_to_all(partial.reshape(n_blk, rows, width + LANES), group_axes, 0, 0)
+    attended = combine(partial, heads)
+    attended = [attended[:, : width // 2], attended[:, width // 2 :]]
 
     mine = jnp.where(core == 0, attended[0], attended[1])
     other = jnp.where(core == 0, attended[1], attended[0])
@@ -367,7 +448,7 @@
     gathered = lax.dynamic_update_index_in_dim(gathered, attended, kv_head, 0)
     for step in range(1, KEY_VALUE_HEADS):
         pairs = [(i, i ^ step) for i in range(KEY_VALUE_HEADS)]
-        piece = lax.ppermute(attended, ("zh", "yl"), pairs)
+        piece = lax.ppermute(attended, ("yh", "yl"), pairs)
         gathered = lax.dynamic_update_index_in_dim(gathered, piece, kv_head ^ step, 0)
     gathered = gathered.reshape(n_blk // 2, 1, rows, -1)
     gathered = jnp.broadcast_to(gathered, (n_blk // 2, 2) + gathered.shape[2:])
@@ -409,7 +490,8 @@
         incoming.reshape(slots, -1), perm, norm_gain.reshape(1, -1), gate_proj, up_proj
     )
     sums = lax.all_to_all(sums.reshape(n_narrow, slots // n_narrow, -1), NARROW, 0, 0)
-    activated = gather_by_exchange(activate(sums), NARROW).reshape(slots, -1)
+    activated = activate(sums)
+    activated = lax.all_to_all(activated, NARROW, 0, 0).reshape(slots, -1)
     expert_out = down(activated, back, down_proj)
     returned = lax.all_to_all(expert_out.reshape(n_blk, exp_dev * CAP, -1), BLK, 0, 0)
     returned = returned.reshape(slots, -1)

time: 248 us -> 236 us (0.952)
  local copies, waits for them, and re-layouts: 21.8 us -> 4.41 us
  starting transfers between devices: 69.5 us -> 54.7 us
  Pallas kernels: 38.7 us -> 47.4 us
  waiting for transfers between devices: 57.1 us -> 65.2 us
  other arithmetic: 3.69 us -> 6.17 us
    unnamed x49 -> x12, local copies, waits for them, and re-layouts: 17.2 us -> 0.93 us
    pallas_call x5 -> x4, Pallas kernels: 37.7 us -> 46.6 us  [the longest x1 32.8 us: attention(): pl.pallas_call(functools.partial(attention_kernel, heads), in_specs=[pl.B...]
    all_to_all x2 -> x1, waiting for transfers between devices: 9.66 us -> 17.6 us  [per_device(): lax.all_to_all(partial.reshape(n_blk, rows, width + LANES), group_axes, 0...]
    all_to_all x2 -> x1, starting transfers between devices: 14.6 us -> 7.8 us  [per_device(): lax.all_to_all(partial.reshape(n_blk, rows, width + LANES), group_axes, 0...]
    ppermute x17 -> x14, starting transfers between devices: 26.3 us -> 19.7 us  [the longest x3 6.33 us: per_device(): all_q.append(lax.ppermute(pair, 'x', pairs))]
    ppermute x17 -> x14, waiting for transfers between devices: 14.1 us -> 14.4 us  [the longest x3 6.65 us: per_device(): all_q.append(lax.ppermute(pair, 'x', pairs))]
  transfers between devices with their start and end apart: 26 -> 22, of which waited for: 12 -> 13; matrix products, arithmetic and copies ran while one was open for 2% -> 1% of each run, Pallas kernels for 7% -> 0%
where the time goes in v3:
time: 236 us; the launch traced here: 235 us
  waiting for transfers between devices  65.2 us (28%)
  starting transfers between devices  54.7 us (23%)
  blocking collectives  54.1 us (23%)
  Pallas kernels  47.4 us (20%)
  other arithmetic  6.17 us (3%)
  local copies, waits for them, and re-layouts  4.41 us (2%)
  matrix products  2.49 us (1%)
    all_to_all x1, blocking collectives, per_device(): lax.all_to_all(sums.reshape(n_narrow, slots // n_narrow, -1), NARROW, 0, 0)  34.7 us
    pallas_call x1, Pallas kernels, attention(): pl.pallas_call(functools.partial(attention_kernel, heads), in_specs=[pl.B...  32.8 us
    all_to_all x1, blocking collectives, per_device(): activated = lax.all_to_all(activated, NARROW, 0, 0).reshape(slots, -1)  19.4 us
    all_to_all x1, waiting for transfers between devices, per_device(): lax.all_to_all(partial.reshape(n_blk, rows, width + LANES), group_axes, 0...  17.6 us
    all_to_all x1, waiting for transfers between devices, per_device(): lax.all_to_all(gathered.reshape((n_blk,) + gathered.shape[2:]), group_axe...  9 us
    all_to_all x1, waiting for transfers between devices, per_device(): lax.all_to_all(expert_out.reshape(n_blk, exp_dev * CAP, -1), BLK, 0, 0)  8 us
    all_to_all x1, starting transfers between devices, per_device(): lax.all_to_all(partial.reshape(n_blk, rows, width + LANES), group_axes, 0...  7.8 us
    all_to_all x1, starting transfers between devices, per_device(): lax.all_to_all(expert_out.reshape(n_blk, exp_dev * CAP, -1), BLK, 0, 0)  7.74 us
  transfers between devices with their start and end apart: 22, of which 13 were waited for; matrix products, arithmetic and copies ran while one was open for 1% of the time, Pallas kernels for 0%

profile of v3, /device:TPU:1, one launch (start us, length us, event | category | flops | bytes accessed | tf_op | source)
XLA Modules:
  0.0 235.5 jit_solution(11465471550821590105)
XLA Ops:
  0.0 0.7 fusion.28
  0.7 0.1 copy.29
  0.8 0.1 copy.30
  0.9 0.7 convert_element_type.60
  1.7 1.1 constant_dynamic-slice_fusion.1
  2.7 0.1 concatenate.17
  2.8 1.5 collective-permute-start
  4.3 0.1 concatenate.16
  4.4 0.8 collective-permute-done
  5.2 0.5 slice.27
  6.4 1.6 add_bitcast_fusion
  8.1 3.1 %collective-permute-start.6 = (bf16[2,4,128,128]{3,2,1,0:T(8,128)(2,1)S(1)}, bf16[2,4,128,128]{3,2,1,0:T(8,128)(2,1)S(1)}, u32[]{:S(2)}, u32[]{:S(2)}) collective-permute-start(bf16[2,4,128,128]{3,2,1,0:T(8,128)(2,1)S(1)} %pad_maximum_fusion.3), channel_id=1, source_target_pairs={{0,2},{1,3},{2,0},{3,1},{4,6},{5,7},{6,4},{7,5},{8,10},{9,11},{10,... | collective-permute-start | bytes 786440 | tf_op jit(solution)/shard_map/ppermute | solution.py:420
  11.2 1.7 collective-permute-start.1
  12.9 0.9 collective-permute-start.7
  13.9 2.5 %collective-permute-done.1 = bf16[64,1152]{1,0:T(8,128)(2,1)S(1)} collective-permute-done((bf16[64,1152]{1,0:T(8,128)(2,1)S(1)}, bf16[64,1152]{1,0:T(8,128)(2,1)S(1)}, u32[]{:S(2)}, u32[]{:S(2)}) %collective-permute-start.1) | collective-permute-done | bytes 147488 | tf_op jit(solution)/shard_map/ppermute | solution.py:406
  16.4 1.3 collective-permute-start.2
  17.7 1.7 collective-permute-start.8
  19.4 2.5 %collective-permute-start.3 = (bf16[128,1152]{1,0:T(8,128)(2,1)S(1)}, bf16[128,1152]{1,0:T(8,128)(2,1)S(1)}, u32[]{:S(2)}, u32[]{:S(2)}) collective-permute-start(bf16[128,1152]{1,0:T(8,128)(2,1)S(1)} %pad_maximum_fusion.refs_0_), channel_id=1, source_target_pairs={{0,32},{16,48},{32,0},{48,16},{1,33},{17,49},{33,1},{49,17},{2,34}... | collective-permute-start | bytes 884744 | tf_op jit(solution)/shard_map/ppermute | solution.py:428
  21.9 1.5 collective-permute-done.7.refs_7_
  23.4 2.6 %collective-permute-start.4 = (bf16[128,1152]{1,0:T(8,128)(2,1)S(1)}, bf16[128,1152]{1,0:T(8,128)(2,1)S(1)}, u32[]{:S(2)}, u32[]{:S(2)}) collective-permute-start(bf16[128,1152]{1,0:T(8,128)(2,1)S(1)} %pad_maximum_fusion.refs_0_), channel_id=1, source_target_pairs={{0,48},{16,0},{32,16},{48,32},{1,49},{17,1},{33,17},{49,33},{2,50}... | collective-permute-start | bytes 884744 | tf_op jit(solution)/shard_map/ppermute | solution.py:428
  25.9 0.9 collective-permute-start.10
  26.9 1.0 collective-permute-start.9
  27.9 0.1 stack.136.info_ref
  28.1 4.1 %collective-permute-done.3.refs_2_ = bf16[128,1152]{1,0:T(8,128)(2,1)S(1)} collective-permute-done((bf16[128,1152]{1,0:T(8,128)(2,1)S(1)}, bf16[128,1152]{1,0:T(8,128)(2,1)S(1)}, u32[]{:S(2)}, u32[]{:S(2)}) %collective-permute-start.3) | collective-permute-done | bytes 294944 | tf_op jit(solution)/shard_map/ppermute | solution.py:428
  32.2 2.5 %collective-permute-done.4.refs_3_ = bf16[128,1152]{1,0:T(8,128)(2,1)S(1)} collective-permute-done((bf16[128,1152]{1,0:T(8,128)(2,1)S(1)}, bf16[128,1152]{1,0:T(8,128)(2,1)S(1)}, u32[]{:S(2)}, u32[]{:S(2)}) %collective-permute-start.4) | collective-permute-done | bytes 294944 | tf_op jit(solution)/shard_map/ppermute | solution.py:428
  34.7 32.8 %attention.1 = bf16[512,1152]{1,0:T(8,128)(2,1)} custom-call(s32[24]{0:T(128)S(1)} %stack.136.info_ref, bf16[128,1152]{1,0:T(8,128)(2,1)S(1)} %pad_maximum_fusion.refs_0_, bf16[128,1152]{1,0:T(8,128)(2,1)S(1)} %collective-permute-done.2.refs_1_, bf16[128,1152]{1,0:T(8,128)(2,1)S(1)} %collective-permute-done.3.refs_2_, ...), custom_call_target="tpu_custom_call" | custom-call | flops 12884901888 | bytes 6291456 | tf_op jit(solution)/shard_map/attention/pallas_call | solution.py:181
  67.5 7.8 %all-to-all-start = ((bf16[16,32,1152]{2,1,0:T(8,128)(2,1)}), bf16[16,32,1152]{2,1,0:T(8,128)(2,1)S(1)}, u32[]{:S(2)}, u32[]{:S(2)}) async-start(bf16[16,32,1152]{2,1,0:T(8,128)(2,1)} %bitcast.33), calls=%async_computation | async-start | bytes 2359296 | tf_op jit(solution)/shard_map/all_to_all | solution.py:437
  75.3 17.6 %all-to-all-done.x_ref = bf16[16,32,1152]{2,1,0:T(8,128)(2,1)S(1)} async-done(((bf16[16,32,1152]{2,1,0:T(8,128)(2,1)}), bf16[16,32,1152]{2,1,0:T(8,128)(2,1)S(1)}, u32[]{:S(2)}, u32[]{:S(2)}) %all-to-all-start) | async-done | bytes 1179680 | tf_op jit(solution)/shard_map/all_to_all | solution.py:437
  92.9 0.9 combine.1
  93.8 3.5 %collective-permute-start.12 = (bf16[32,512]{1,0:T(8,128)(2,1)S(1)}, bf16[32,512]{1,0:T(8,128)(2,1)S(1)}, u32[]{:S(2)}, u32[]{:S(2)}) collective-permute-start(bf16[32,512]{1,0:T(8,128)(2,1)S(1)} %broadcast_select_fusion), channel_id=1, source_target_pairs={{0,8},{8,0},{1,9},{9,1},{2,10},{10,2},{3,11},{11,3},{4,12},{12,4},... | collective-permute-start | bytes 98312 | tf_op jit(solution)/shard_map/ppermute | solution.py:443
  97.3 0.9 collective-permute-done.12
  98.2 0.7 collective-permute-start.13
  98.9 2.6 %collective-permute-start.14 = (bf16[2,32,512]{2,1,0:T(8,128)(2,1)S(1)}, bf16[2,32,512]{2,1,0:T(8,128)(2,1)S(1)}, u32[]{:S(2)}, u32[]{:S(2)}) collective-permute-start(bf16[2,32,512]{2,1,0:T(8,128)(2,1)S(1)} %pad_maximum_fusion.6), channel_id=1, source_target_pairs={{0,2},{1,3},{2,0},{3,1},{4,6},{5,7},{6,4},{7,5},{8,10},{9,11},{10,... | collective-permute-start | bytes 196616 | tf_op jit(solution)/shard_map/ppermute | solution.py:451
  101.5 0.6 collective-permute-start.15
  102.2 2.3 collective-permute-done.14
  104.5 1.5 collective-permute-done.15
  105.9 0.8 broadcast_in_dim.60
  106.8 3.7 %all-to-all-start.1 = ((bf16[16,32,512]{2,1,0:T(8,128)(2,1)}), bf16[16,32,512]{2,1,0:T(8,128)(2,1)S(1)}, u32[]{:S(2)}, u32[]{:S(2)}) async-start(bf16[16,32,512]{2,1,0:T(8,128)(2,1)} %bitcast.41), calls=%async_computation.1 | async-start | bytes 1048576 | tf_op jit(solution)/shard_map/all_to_all | solution.py:455
  110.6 0.1 eq.89
  110.6 9.0 %all-to-all-done.1 = bf16[16,32,512]{2,1,0:T(8,128)(2,1)S(1)} async-done(((bf16[16,32,512]{2,1,0:T(8,128)(2,1)}), bf16[16,32,512]{2,1,0:T(8,128)(2,1)S(1)}, u32[]{:S(2)}, u32[]{:S(2)}) %all-to-all-start.1) | async-done | bytes 524320 | tf_op jit(solution)/shard_map/all_to_all | solution.py:455
  119.7 0.4 fusion.4
  120.1 3.3 %collective-permute-start.16 = (bf16[8,32,512]{2,1,0:T(8,128)(2,1)S(1)}, bf16[8,32,512]{2,1,0:T(8,128)(2,1)S(1)}, u32[]{:S(2)}, u32[]{:S(2)}) collective-permute-start(bf16[8,32,512]{2,1,0:T(8,128)(2,1)S(1)} %fusion.8), channel_id=1, source_target_pairs={{0,8},{8,0},{1,9},{9,1},{2,10},{10,2},{3,11},{11,3},{4,12},{12,4},... | collective-permute-start | bytes 786440 | tf_op jit(solution)/shard_map/ppermute | solution.py:462
  123.5 0.6 reduce-window.6
  124.1 0.2 slice_reduce_fusion
  124.4 0.1 fusion.11
  124.6 0.8 fusion.6
  125.4 3.4 %all-to-all-start.2 = ((bf16[8,32,512]{2,1,0:T(8,128)(2,1)}), bf16[8,32,512]{2,1,0:T(8,128)(2,1)S(1)}, u32[]{:S(2)}, u32[]{:S(2)}) async-start(bf16[8,32,512]{2,1,0:T(8,128)(2,1)} %fusion.6), calls=%async_computation.2 | async-start | bytes 524288 | tf_op jit(solution)/shard_map/all_to_all | solution.py:463
  128.8 0.2 fusion.7
  129.0 7.1 %all-to-all-done.2 = bf16[8,32,512]{2,1,0:T(8,128)(2,1)S(1)} async-done(((bf16[8,32,512]{2,1,0:T(8,128)(2,1)}), bf16[8,32,512]{2,1,0:T(8,128)(2,1)S(1)}, u32[]{:S(2)}, u32[]{:S(2)}) %all-to-all-start.2) | async-done | bytes 262176 | tf_op jit(solution)/shard_map/all_to_all | solution.py:463
  136.2 1.1 convolution_convert_fusion
  137.3 4.2 %all-to-all-start.3 = ((bf16[16,24,512]{2,1,0:T(8,128)(2,1)}), bf16[16,24,512]{2,1,0:T(8,128)(2,1)S(1)}, u32[]{:S(2)}, u32[]{:S(2)}) async-start(bf16[16,24,512]{2,1,0:T(8,128)(2,1)} %bitcast.48), calls=%async_computation.3 | async-start | bytes 786432 | tf_op jit(solution)/shard_map/all_to_all | solution.py:481
  141.4 1.0 fusion.3
  142.4 7.4 %all-to-all-done.3 = bf16[16,24,512]{2,1,0:T(8,128)(2,1)S(1)} async-done(((bf16[16,24,512]{2,1,0:T(8,128)(2,1)}), bf16[16,24,512]{2,1,0:T(8,128)(2,1)S(1)}, u32[]{:S(2)}, u32[]{:S(2)}) %all-to-all-start.3) | async-done | bytes 393248 | tf_op jit(solution)/shard_map/all_to_all | solution.py:481
  149.8 0.8 copy-done.1
  150.5 7.7 %gate_up.1 = bf16[384,3200]{1,0:T(8,128)(2,1)} custom-call(bf16[384,512]{1,0:T(8,128)(2,1)} %bitcast.106, bf16[384,384]{1,0:T(8,128)(2,1)} %get-tuple-element.18.perm_ref, f32[1,512]{1,0:T(1,128)} %bitcast.108, bf16[4,512,1536]{2,1,0:T(8,128)(2,1)} %gate_hbm.1, bf16[4,512,1536]{2,1,0:T(8,128)(2,1)} %up_hbm.1), custom_call_target="tpu_custom_call" | custom-call | flops 1207959552 | bytes 14942208 | tf_op jit(solution)/shard_map/gate_up/pallas_call | solution.py:270
  158.3 34.7 %all_to_all.35.x_ref = bf16[8,48,3200]{2,1,0:T(8,128)(2,1)S(1)} all-to-all(bf16[8,48,3200]{2,1,0:T(8,128)(2,1)} %bitcast.100), channel_id=1, replica_groups=mesh['zl'=2,'x'=4,'core'=2,'zh'=2,'yh'=2,'yl'=2] {'zh','yh','yl'}, dimensions={0} | all-to-all | bytes 4915200 | tf_op jit(solution)/shard_map/all_to_all | solution.py:492
  193.0 0.5 activate.1
  193.5 19.4 %all_to_all.36 = bf16[8,48,1536]{2,1,0:T(8,128)(2,1)} all-to-all(bf16[8,48,1536]{2,1,0:T(8,128)(2,1)S(1)} %activate.1), channel_id=1, replica_groups=mesh['zl'=2,'x'=4,'core'=2,'zh'=2,'yh'=2,'yl'=2] {'zh','yh','yl'}, dimensions={0} | all-to-all | bytes 2359296 | tf_op jit(solution)/shard_map/all_to_all | solution.py:494
  212.9 5.6 %down.1 = bf16[384,512]{1,0:T(8,128)(2,1)} custom-call(bf16[384,1536]{1,0:T(8,128)(2,1)} %bitcast.101, bf16[384,384]{1,0:T(8,128)(2,1)} %get-tuple-element.17.back_ref, bf16[4,1536,512]{2,1,0:T(8,128)(2,1)} %down_hbm.1), custom_call_target="tpu_custom_call" | custom-call | flops 603979776 | bytes 6291456 | tf_op jit(solution)/shard_map/down/pallas_call | solution.py:344
  218.5 7.7 %all-to-all-start.6 = ((bf16[16,24,512]{2,1,0:T(8,128)(2,1)}), bf16[16,24,512]{2,1,0:T(8,128)(2,1)S(1)}, u32[]{:S(2)}, u32[]{:S(2)}) async-start(bf16[16,24,512]{2,1,0:T(8,128)(2,1)} %bitcast.105), calls=%async_computation.6 | async-start | bytes 786432 | tf_op jit(solution)/shard_map/all_to_all | solution.py:496
  226.3 0.2 select_reduce_fusion
  226.5 8.0 %all-to-all-done.6 = bf16[16,24,512]{2,1,0:T(8,128)(2,1)S(1)} async-done(((bf16[16,24,512]{2,1,0:T(8,128)(2,1)}), bf16[16,24,512]{2,1,0:T(8,128)(2,1)S(1)}, u32[]{:S(2)}, u32[]{:S(2)}) %all-to-all-start.6) | async-done | bytes 393248 | tf_op jit(solution)/shard_map/all_to_all | solution.py:496
  234.5 0.2 fusion.15
  234.7 0.8 fusion.1
  (47 shorter events, 1.0 us)
Async XLA Ops:
  0.0 119.6 %copy-start = (bf16[512,512]{1,0:T(8,128)(2,1)S(1)}, bf16[512,512]{1,0:T(8,128)(2,1)}, u32[]{:S(2)}) copy-start(bf16[512,512]{1,0:T(8,128)(2,1)} %param.18) | copy-start | bytes 1572868
  2.8 2.4 %collective-permute-start = (bf16[32,1152]{1,0:T(8,128)(2,1)S(1)}, bf16[32,1152]{1,0:T(8,128)(2,1)S(1)}, u32[]{:S(2)}, u32[]{:S(2)}) collective-permute-start(bf16[32,1152]{1,0:T(8,128)(2,1)S(1)} %concatenate.17), channel_id=1, source_target_pairs={{0,8},{8,0},{1,9},{9,1},{2,10},{10,2},{3,11},{11,3},{4,12},{12,4},... | collective-permute-start | bytes 221192 | tf_op jit(solution)/shard_map/ppermute | solution.py:404
  8.1 11.3 %collective-permute-start.6 = (bf16[2,4,128,128]{3,2,1,0:T(8,128)(2,1)S(1)}, bf16[2,4,128,128]{3,2,1,0:T(8,128)(2,1)S(1)}, u32[]{:S(2)}, u32[]{:S(2)}) collective-permute-start(bf16[2,4,128,128]{3,2,1,0:T(8,128)(2,1)S(1)} %pad_maximum_fusion.3), channel_id=1, source_target_pairs={{0,2},{1,3},{2,0},{3,1},{4,6},{5,7},{6,4},{7,5},{8,10},{9,11},{10,... | collective-permute-start | bytes 786440 | tf_op jit(solution)/shard_map/ppermute | solution.py:420
  11.2 5.2 %collective-permute-start.1 = (bf16[64,1152]{1,0:T(8,128)(2,1)S(1)}, bf16[64,1152]{1,0:T(8,128)(2,1)S(1)}, u32[]{:S(2)}, u32[]{:S(2)}) collective-permute-start(bf16[64,1152]{1,0:T(8,128)(2,1)S(1)} %pad_maximum_fusion.5), channel_id=1, source_target_pairs={{0,64},{64,0},{1,65},{65,1},{2,66},{66,2},{3,67},{67,3},{4,68},{68... | collective-permute-start | bytes 442376 | tf_op jit(solution)/shard_map/ppermute | solution.py:406
  12.9 10.5 %collective-permute-start.7 = (bf16[2,4,128,128]{3,2,1,0:T(8,128)(2,1)S(1)}, bf16[2,4,128,128]{3,2,1,0:T(8,128)(2,1)S(1)}, u32[]{:S(2)}, u32[]{:S(2)}) collective-permute-start(bf16[2,4,128,128]{3,2,1,0:T(8,128)(2,1)S(1)} %pad_maximum_fusion.4), channel_id=1, source_target_pairs={{0,3},{1,2},{2,1},{3,0},{4,7},{5,6},{6,5},{7,4},{8,11},{9,10},{10,... | collective-permute-start | bytes 786440 | tf_op jit(solution)/shard_map/ppermute | solution.py:420
  13.8 12.2 %collective-permute-start.5 = (bf16[2,4,128,128]{3,2,1,0:T(8,128)(2,1)S(1)}, bf16[2,4,128,128]{3,2,1,0:T(8,128)(2,1)S(1)}, u32[]{:S(2)}, u32[]{:S(2)}) collective-permute-start(bf16[2,4,128,128]{3,2,1,0:T(8,128)(2,1)S(1)} %pad_maximum_fusion.2), channel_id=1, source_target_pairs={{0,1},{1,0},{2,3},{3,2},{4,5},{5,4},{6,7},{7,6},{8,9},{9,8},{10,11... | collective-permute-start | bytes 786440 | tf_op jit(solution)/shard_map/ppermute | solution.py:420
  16.4 10.5 %collective-permute-start.2 = (bf16[128,1152]{1,0:T(8,128)(2,1)S(1)}, bf16[128,1152]{1,0:T(8,128)(2,1)S(1)}, u32[]{:S(2)}, u32[]{:S(2)}) collective-permute-start(bf16[128,1152]{1,0:T(8,128)(2,1)S(1)} %pad_maximum_fusion.refs_0_), channel_id=1, source_target_pairs={{0,16},{16,32},{32,48},{48,0},{1,17},{17,33},{33,49},{49,1},{2,18}... | collective-permute-start | bytes 884744 | tf_op jit(solution)/shard_map/ppermute | solution.py:428
  17.7 9.1 %collective-permute-start.8 = (bf16[2,4,128,128]{3,2,1,0:T(8,128)(2,1)S(1)}, bf16[2,4,128,128]{3,2,1,0:T(8,128)(2,1)S(1)}, u32[]{:S(2)}, u32[]{:S(2)}) collective-permute-start(bf16[2,4,128,128]{3,2,1,0:T(8,128)(2,1)S(1)} %pad_maximum_fusion.1.refs_4_), channel_id=1, source_target_pairs={{0,8},{8,0},{1,9},{9,1},{2,10},{10,2},{3,11},{11,3},{4,12},{12,4},... | collective-permute-start | bytes 786440 | tf_op jit(solution)/shard_map/ppermute | solution.py:421
  19.4 12.8 %collective-permute-start.3 = (bf16[128,1152]{1,0:T(8,128)(2,1)S(1)}, bf16[128,1152]{1,0:T(8,128)(2,1)S(1)}, u32[]{:S(2)}, u32[]{:S(2)}) collective-permute-start(bf16[128,1152]{1,0:T(8,128)(2,1)S(1)} %pad_maximum_fusion.refs_0_), channel_id=1, source_target_pairs={{0,32},{16,48},{32,0},{48,16},{1,33},{17,49},{33,1},{49,17},{2,34}... | collective-permute-start | bytes 884744 | tf_op jit(solution)/shard_map/ppermute | solution.py:428
  23.4 11.3 %collective-permute-start.4 = (bf16[128,1152]{1,0:T(8,128)(2,1)S(1)}, bf16[128,1152]{1,0:T(8,128)(2,1)S(1)}, u32[]{:S(2)}, u32[]{:S(2)}) collective-permute-start(bf16[128,1152]{1,0:T(8,128)(2,1)S(1)} %pad_maximum_fusion.refs_0_), channel_id=1, source_target_pairs={{0,48},{16,0},{32,16},{48,32},{1,49},{17,1},{33,17},{49,33},{2,50}... | collective-permute-start | bytes 884744 | tf_op jit(solution)/shard_map/ppermute | solution.py:428
  25.9 8.8 %collective-permute-start.10 = (bf16[2,4,128,128]{3,2,1,0:T(8,128)(2,1)S(1)}, bf16[2,4,128,128]{3,2,1,0:T(8,128)(2,1)S(1)}, u32[]{:S(2)}, u32[]{:S(2)}) collective-permute-start(bf16[2,4,128,128]{3,2,1,0:T(8,128)(2,1)S(1)} %collective-permute-done.6.refs_6_), channel_id=1, source_target_pairs={{0,8},{8,0},{1,9},{9,1},{2,10},{10,2},{3,11},{11,3},{4,12},{12,4},... | collective-permute-start | bytes 786440 | tf_op jit(solution)/shard_map/ppermute | solution.py:421
  26.8 7.9 %collective-permute-start.11 = (bf16[2,4,128,128]{3,2,1,0:T(8,128)(2,1)S(1)}, bf16[2,4,128,128]{3,2,1,0:T(8,128)(2,1)S(1)}, u32[]{:S(2)}, u32[]{:S(2)}) collective-permute-start(bf16[2,4,128,128]{3,2,1,0:T(8,128)(2,1)S(1)} %collective-permute-done.7.refs_7_), channel_id=1, source_target_pairs={{0,8},{8,0},{1,9},{9,1},{2,10},{10,2},{3,11},{11,3},{4,12},{12,4},... | collective-permute-start | bytes 786440 | tf_op jit(solution)/shard_map/ppermute | solution.py:421
  26.9 7.8 %collective-permute-start.9 = (bf16[2,4,128,128]{3,2,1,0:T(8,128)(2,1)S(1)}, bf16[2,4,128,128]{3,2,1,0:T(8,128)(2,1)}, u32[]{:S(2)}, u32[]{:S(2)}) collective-permute-start(bf16[2,4,128,128]{3,2,1,0:T(8,128)(2,1)S(1)} %collective-permute-done.5.refs_5_), channel_id=1, source_target_pairs={{0,8},{8,0},{1,9},{9,1},{2,10},{10,2},{3,11},{11,3},{4,12},{12,4},... | collective-permute-start | bytes 786440 | tf_op jit(solution)/shard_map/ppermute | solution.py:421
  67.5 25.4 %all-to-all-start = ((bf16[16,32,1152]{2,1,0:T(8,128)(2,1)}), bf16[16,32,1152]{2,1,0:T(8,128)(2,1)S(1)}, u32[]{:S(2)}, u32[]{:S(2)}) async-start(bf16[16,32,1152]{2,1,0:T(8,128)(2,1)} %bitcast.33), calls=%async_computation | async-start | bytes 2359296 | tf_op jit(solution)/shard_map/all_to_all | solution.py:437
  75.3 35.2 %copy-start.3 = (s32[32,8]{0,1:T(8,128)S(1)}, s32[32,8]{0,1:T(8,128)}, u32[]{:S(2)}) copy-start(s32[32,8]{0,1:T(8,128)} %param.21) | copy-start | bytes 3076
  93.8 4.3 %collective-permute-start.12 = (bf16[32,512]{1,0:T(8,128)(2,1)S(1)}, bf16[32,512]{1,0:T(8,128)(2,1)S(1)}, u32[]{:S(2)}, u32[]{:S(2)}) collective-permute-start(bf16[32,512]{1,0:T(8,128)(2,1)S(1)} %broadcast_select_fusion), channel_id=1, source_target_pairs={{0,8},{8,0},{1,9},{9,1},{2,10},{10,2},{3,11},{11,3},{4,12},{12,4},... | collective-permute-start | bytes 98312 | tf_op jit(solution)/shard_map/ppermute | solution.py:443
  98.2 4.0 %collective-permute-start.13 = (bf16[2,32,512]{2,1,0:T(8,128)(2,1)S(1)}, bf16[2,32,512]{2,1,0:T(8,128)(2,1)S(1)}, u32[]{:S(2)}, u32[]{:S(2)}) collective-permute-start(bf16[2,32,512]{2,1,0:T(8,128)(2,1)S(1)} %pad_maximum_fusion.6), channel_id=1, source_target_pairs={{0,1},{1,0},{2,3},{3,2},{4,5},{5,4},{6,7},{7,6},{8,9},{9,8},{10,11... | collective-permute-start | bytes 196616 | tf_op jit(solution)/shard_map/ppermute | solution.py:451
  98.9 5.6 %collective-permute-start.14 = (bf16[2,32,512]{2,1,0:T(8,128)(2,1)S(1)}, bf16[2,32,512]{2,1,0:T(8,128)(2,1)S(1)}, u32[]{:S(2)}, u32[]{:S(2)}) collective-permute-start(bf16[2,32,512]{2,1,0:T(8,128)(2,1)S(1)} %pad_maximum_fusion.6), channel_id=1, source_target_pairs={{0,2},{1,3},{2,0},{3,1},{4,6},{5,7},{6,4},{7,5},{8,10},{9,11},{10,... | collective-permute-start | bytes 196616 | tf_op jit(solution)/shard_map/ppermute | solution.py:451
  101.5 4.5 %collective-permute-start.15 = (bf16[2,32,512]{2,1,0:T(8,128)(2,1)S(1)}, bf16[2,32,512]{2,1,0:T(8,128)(2,1)S(1)}, u32[]{:S(2)}, u32[]{:S(2)}) collective-permute-start(bf16[2,32,512]{2,1,0:T(8,128)(2,1)S(1)} %pad_maximum_fusion.6), channel_id=1, source_target_pairs={{0,3},{1,2},{2,1},{3,0},{4,7},{5,6},{6,5},{7,4},{8,11},{9,10},{10,... | collective-permute-start | bytes 196616 | tf_op jit(solution)/shard_map/ppermute | solution.py:451
  106.8 12.8 %all-to-all-start.1 = ((bf16[16,32,512]{2,1,0:T(8,128)(2,1)}), bf16[16,32,512]{2,1,0:T(8,128)(2,1)S(1)}, u32[]{:S(2)}, u32[]{:S(2)}) async-start(bf16[16,32,512]{2,1,0:T(8,128)(2,1)} %bitcast.41), calls=%async_computation.1 | async-start | bytes 1048576 | tf_op jit(solution)/shard_map/all_to_all | solution.py:455
  119.6 16.5 %copy-start.2 = (bf16[32,512]{1,0:T(8,128)(2,1)S(1)}, bf16[32,512]{1,0:T(8,128)(2,1)}, u32[]{:S(2)}) copy-start(bf16[32,512]{1,0:T(8,128)(2,1)} %param.19) | copy-start | bytes 98308
  120.1 4.4 %collective-permute-start.16 = (bf16[8,32,512]{2,1,0:T(8,128)(2,1)S(1)}, bf16[8,32,512]{2,1,0:T(8,128)(2,1)S(1)}, u32[]{:S(2)}, u32[]{:S(2)}) collective-permute-start(bf16[8,32,512]{2,1,0:T(8,128)(2,1)S(1)} %fusion.8), channel_id=1, source_target_pairs={{0,8},{8,0},{1,9},{9,1},{2,10},{10,2},{3,11},{11,3},{4,12},{12,4},... | collective-permute-start | bytes 786440 | tf_op jit(solution)/shard_map/ppermute | solution.py:462
  125.4 10.8 %all-to-all-start.2 = ((bf16[8,32,512]{2,1,0:T(8,128)(2,1)}), bf16[8,32,512]{2,1,0:T(8,128)(2,1)S(1)}, u32[]{:S(2)}, u32[]{:S(2)}) async-start(bf16[8,32,512]{2,1,0:T(8,128)(2,1)} %fusion.6), calls=%async_computation.2 | async-start | bytes 524288 | tf_op jit(solution)/shard_map/all_to_all | solution.py:463
  137.3 12.5 %all-to-all-start.3 = ((bf16[16,24,512]{2,1,0:T(8,128)(2,1)}), bf16[16,24,512]{2,1,0:T(8,128)(2,1)S(1)}, u32[]{:S(2)}, u32[]{:S(2)}) async-start(bf16[16,24,512]{2,1,0:T(8,128)(2,1)} %bitcast.48), calls=%async_computation.3 | async-start | bytes 786432 | tf_op jit(solution)/shard_map/all_to_all | solution.py:481
  149.8 0.8 copy-start.1
  212.9 13.3 %copy-start.4 = (f32[32,8]{0,1:T(8,128)S(1)}, f32[32,8]{0,1:T(8,128)}, u32[]{:S(2)}) copy-start(f32[32,8]{0,1:T(8,128)} %param.22) | copy-start | bytes 3076
  218.5 16.0 %all-to-all-start.6 = ((bf16[16,24,512]{2,1,0:T(8,128)(2,1)}), bf16[16,24,512]{2,1,0:T(8,128)(2,1)S(1)}, u32[]{:S(2)}, u32[]{:S(2)}) async-start(bf16[16,24,512]{2,1,0:T(8,128)(2,1)} %bitcast.105), calls=%async_computation.6 | async-start | bytes 786432 | tf_op jit(solution)/shard_map/all_to_all | solution.py:496

commit v4 on v3

--- a/solution.py
+++ b/solution.py
@@ -24,7 +24,7 @@
 LANES = 128
 BLK = ("zl", "x", "core")
 NARROW = ("zh", "yh", "yl")
-SAFE_POWER = 60.0
+SAFE_POWER = 100.0
 VMEM_LIMIT = 40 * 1024 * 1024
 LARGE_LIMIT = 56 * 1024 * 1024
 SMALL_LIMIT = 12 * 1024 * 1024
@@ -67,9 +67,11 @@
             copies.append(pltpu.make_async_copy(ref.at[part], to, sem.at[len(copies)]))
     for copy in copies:
         copy.start()
-    for copy in copies:
+
+    sub = lax.broadcasted_iota(jnp.int32, (16, tokens), 0)
+    vt_ref[HEAD_SIZE:, :] = jnp.where(sub == 0, 1.0, 0.0).astype(jnp.bfloat16)
+    for copy in copies[: len(q_in)]:
         copy.wait()
-
     extra = q_ref[:, base:].astype(jnp.float32).T
     lim_ref[...] = extra
     length = extra[TREE_BLOCKS : TREE_BLOCKS + 1] * 256.0 + extra[TREE_BLOCKS + 1 : TREE_BLOCKS + 2]
@@ -78,27 +80,27 @@
     block_id = lax.broadcasted_iota(jnp.int32, (chip_blocks, rows), 0) + first
     bound = length - (block_id * BLOCK_TOKENS).astype(jnp.float32)
     lim_ref[0:chip_blocks, :] = jnp.where(reads > 0.5, bound, 0.0)
-    token = lax.broadcasted_iota(jnp.int32, (LANES, 1), 0)
-    token = [
-        (token + info_ref[4 + s] * LANES).astype(jnp.float32) for s in range(sources)
-    ]
-    token = jnp.concatenate(token, axis=0)
-    sub = lax.broadcasted_iota(jnp.int32, (16, tokens), 0)
-    vt_ref[HEAD_SIZE:, :] = jnp.where(sub == 0, 1.0, 0.0).astype(jnp.bfloat16)
-    most_k = jnp.zeros((LANES, 1), jnp.float32)
-    for i in range(chip_blocks):
-        at = slice(i * span, (i + 1) * span)
-        vt_ref[:HEAD_SIZE, at] = v_ref[i].reshape(span, HEAD_SIZE).T
-        side = core if i < blocks else 1 - core
-        lim = lim_ref[pl.ds(side * blocks + i % blocks, 1), :]
-        mask_ref[at, :] = jnp.where(token < lim, 1.0, 0.0).astype(jnp.bfloat16)
-        for s in range(sources):
-            keys = k_ref[i, s].astype(jnp.float32)
-            most_k = jnp.maximum(most_k, jnp.sum(keys * keys, axis=1, keepdims=True))
     most_q = jnp.zeros((rows, 1), jnp.float32)
     for h in range(heads):
         q = q_ref[:, h * HEAD_SIZE : (h + 1) * HEAD_SIZE].astype(jnp.float32)
         most_q = jnp.maximum(most_q, jnp.sum(q * q, axis=1, keepdims=True))
+    token = lax.broadcasted_iota(jnp.int32, (LANES, 1), 0)
+    token = [(token + info_ref[4 + s] * LANES).astype(jnp.float32) for s in range(sources)]
+    token = jnp.concatenate(token, axis=0)
+    for i in range(chip_blocks):
+        at = slice(i * span, (i + 1) * span)
+        side = core if i < blocks else 1 - core
+        lim = lim_ref[pl.ds(side * blocks + i % blocks, 1), :]
+        mask_ref[at, :] = jnp.where(token < lim, 1.0, 0.0).astype(jnp.bfloat16)
+    for copy in copies[len(q_in) :]:
+        copy.wait()
+    most_k = jnp.zeros((LANES, HEAD_SIZE), jnp.float32)
+    for i in range(chip_blocks):
+        vt_ref[:HEAD_SIZE, i * span : (i + 1) * span] = v_ref[i].reshape(span, HEAD_SIZE).T
+        for s in range(sources):
+            keys = k_ref[i, s].astype(jnp.float32)
+            most_k = jnp.maximum(most_k, keys * keys)
+    most_k = jnp.sum(jnp.max(most_k, axis=0, keepdims=True), axis=1, keepdims=True)
     most = jnp.max(most_q) * jnp.max(most_k) * (factor * factor)
     small = most <= SAFE_POWER * SAFE_POWER
 
@@ -213,20 +215,52 @@
         scale = jnp.exp(lse - jnp.max(lse, axis=0, keepdims=True))
         cols = slice(h * HEAD_SIZE, (h + 1) * HEAD_SIZE)
         acc = jnp.sum(x_ref[:, :, cols].astype(jnp.float32) * scale, axis=0)
-        out_ref[:, cols] = (acc / jnp.sum(scale, axis=0)).astype(jnp.bfloat16)
+        at = h % (heads // 2) * HEAD_SIZE
+        out_ref[h // (heads // 2), :, at : at + HEAD_SIZE] = (
+            acc / jnp.sum(scale, axis=0)
+        ).astype(jnp.bfloat16)
 
 
 def combine(parts, heads):
     _, rows, _ = parts.shape
     return pl.pallas_call(
         functools.partial(combine_kernel, heads),
-        out_shape=jax.ShapeDtypeStruct((rows, heads * HEAD_SIZE), jnp.bfloat16),
+        out_shape=jax.ShapeDtypeStruct((2, rows, heads * HEAD_SIZE // 2), jnp.bfloat16),
         compiler_params=params(limit=SMALL_LIMIT),
         cost_estimate=pl.CostEstimate(
             flops=4 * parts.size, bytes_accessed=2 * parts.size, transcendentals=0
         ),
         name="combine",
     )(parts)
+
+
+def project_kernel(core_ref, x_ref, weight_ref, mine_ref, other_ref):
+    chips, _, rows, depth = x_ref.shape
+    core = core_ref[0]
+    for ref, side in ((other_ref, 1 - core), (mine_ref, core)):
+        x = x_ref[:, pl.ds(side, 1)].reshape(chips * rows, depth)
+        product = jnp.dot(x, weight_ref[...], preferred_element_type=jnp.float32)
+        ref[...] = product.astype(ref.dtype)
+
+
+def project(core, x, weight):
+    chips, _, rows, _ = x.shape
+    shape = (chips * rows, weight.shape[1])
+    vmem = pl.BlockSpec(memory_space=pltpu.VMEM)
+    return pl.pallas_call(
+        project_kernel,
+        in_specs=[pl.BlockSpec(memory_space=pltpu.SMEM), vmem, vmem],
+        out_specs=[vmem, vmem],
+        out_shape=[
+            jax.ShapeDtypeStruct(shape, jnp.float32),
+            jax.ShapeDtypeStruct(shape, jnp.bfloat16),
+        ],
+        compiler_params=params(limit=SMALL_LIMIT),
+        cost_estimate=pl.CostEstimate(
+            flops=2 * x.size * weight.shape[1], bytes_accessed=4 * x.size, transcendentals=0
+        ),
+        name="project",
+    )(core.astype(jnp.int32).reshape(1), x, weight)
 
 
 def gate_up_kernel(x_ref, perm_ref, gain_ref, gate_hbm, up_hbm, out_ref, gate_ref, up_ref, sem):
@@ -388,38 +422,41 @@
     swap = [(0, 1), (1, 0)]
     size_x = lax.axis_size("x")
 
+    def head_piece(head):
+        at = head * HEAD_SIZE
+        return jnp.stack(
+            [
+                lax.dynamic_slice_in_dim(cache, at, HEAD_SIZE, 2)
+                for cache in (tree_key_cache, tree_value_cache)
+            ]
+        )
+
+    pieces = [head_piece(kv_head ^ step) for step in range(KEY_VALUE_HEADS)]
+    kv = [pieces[0]]
+    for step in (2, 1, 3):
+        pairs = [(i, i ^ step) for i in range(KEY_VALUE_HEADS)]
+        kv.append(lax.ppermute(pieces[step], ("yh", "yl"), pairs))
+    kv = kv + [lax.ppermute(piece, "core", swap) for piece in kv]
+    sources = [zh * KEY_VALUE_HEADS + (kv_head ^ s) for s in (0, 2, 1, 3)]
+
     both = lax.dynamic_slice_in_dim(queries, kv_head * 2 * width, 2 * width, 1)
+    both = both.reshape(rows, 2, 2, width // 2)
     extra = jnp.concatenate(
         [
             tree_mask.astype(jnp.bfloat16),
             (lengths // 256).astype(jnp.bfloat16)[:, None],
             (lengths % 256).astype(jnp.bfloat16)[:, None],
-            jnp.zeros((rows, LANES - TREE_BLOCKS - 2), jnp.bfloat16),
+            jnp.zeros((rows, LANES - TREE_BLOCKS - 2), jnp.bfloat16) + pieces[1][0, 0, 0, 0] * 0,
         ],
         axis=1,
     )
-    own_q = lax.dynamic_slice_in_dim(both, core * width, width, 1)
-    other_q = lax.dynamic_slice_in_dim(both, (1 - core) * width, width, 1)
+    own_q = lax.dynamic_index_in_dim(both, core, 2, False).reshape(rows, width)
+    other_q = lax.dynamic_index_in_dim(both, 1 - core, 2, False).reshape(rows, width)
     own_q = jnp.concatenate([own_q, extra], axis=1)
     other_q = lax.ppermute(jnp.concatenate([other_q, extra], axis=1), "core", swap)
     pair = jnp.concatenate([own_q, other_q], axis=0)
-    pair = jnp.concatenate([pair, lax.ppermute(pair, "zl", swap)], axis=0)
-
-    def head_piece(head):
-        at = head * HEAD_SIZE
-        return jnp.stack(
-            [
-                lax.dynamic_slice_in_dim(cache, at, HEAD_SIZE, 2) + other_q[0, 0] * 0
-                for cache in (tree_key_cache, tree_value_cache)
-            ]
-        )
-
-    kv = [head_piece(kv_head)]
-    for step in range(1, KEY_VALUE_HEADS):
-        pairs = [(i, i ^ step) for i in range(KEY_VALUE_HEADS)]
-        kv.append(lax.ppermute(head_piece(kv_head ^ step), ("yh", "yl"), pairs))
-    kv = kv + [lax.ppermute(piece, "core", swap) for piece in kv]
-    sources = [zh * KEY_VALUE_HEADS + (kv_head ^ s) for s in range(KEY_VALUE_HEADS)]
+    far = lax.ppermute(pair, "zl", swap)
+    pair = jnp.concatenate([pair, far], axis=0)
 
     all_q, groups = [pair], []
     for dx in range(size_x):
@@ -436,14 +473,7 @@
     partial = attention(info, all_q, kv)
     partial = lax.all_to_all(partial.reshape(n_blk, rows, width + LANES), group_axes, 0, 0)
     attended = combine(partial, heads)
-    attended = [attended[:, : width // 2], attended[:, width // 2 :]]
-
-    mine = jnp.where(core == 0, attended[0], attended[1])
-    other = jnp.where(core == 0, attended[1], attended[0])
-    other = lax.ppermute(other, "core", swap)
-    first = jnp.where(core == 0, mine, other)
-    second = jnp.where(core == 0, other, mine)
-    attended = jnp.stack([first, second])
+
     gathered = jnp.zeros((KEY_VALUE_HEADS,) + attended.shape, attended.dtype)
     gathered = lax.dynamic_update_index_in_dim(gathered, attended, kv_head, 0)
     for step in range(1, KEY_VALUE_HEADS):
@@ -453,13 +483,9 @@
     gathered = gathered.reshape(n_blk // 2, 1, rows, -1)
     gathered = jnp.broadcast_to(gathered, (n_blk // 2, 2) + gathered.shape[2:])
     gathered = lax.all_to_all(gathered.reshape((n_blk,) + gathered.shape[2:]), group_axes, 0, 0)
-    projected = jnp.dot(
-        gathered.reshape(n_blk * rows, -1), out_weight, preferred_element_type=jnp.float32
-    )
-    projected = projected.reshape(n_blk // 2, 2, rows, -1)
-    mine = lax.dynamic_index_in_dim(projected, core, 1, False)
-    other = lax.dynamic_index_in_dim(projected, 1 - core, 1, False).astype(jnp.bfloat16)
+    mine, other = project(core, gathered.reshape(n_blk // 2, 2, rows, -1), out_weight)
     projected = (mine + lax.ppermute(other, "core", swap).astype(jnp.float32)).astype(jnp.bfloat16)
+    projected = projected.reshape(n_blk // 2, rows, -1)
     projected = lax.all_to_all(projected, ("zl", "x"), 0, 0)
     projected = jnp.sum(projected.astype(jnp.float32), axis=0)
     hidden_b = (residual.astype(jnp.float32) + projected).astype(jnp.bfloat16)

time: 236 us -> 229 us (0.970)
  waiting for transfers between devices: 65.2 us -> 58.9 us
  other arithmetic: 6.17 us -> 3.11 us
    ppermute x3, waiting for transfers between devices: 6.65 us -> 2.51 us  [per_device(): all_q.append(lax.ppermute(pair, 'x', pairs))]
    ppermute x5 -> x4, starting transfers between devices: 9.22 us -> 6.01 us  [the longest x3 4.3 us: per_device(): kv.append(lax.ppermute(pieces[step], ('yh', 'yl'), pairs))]
    all_to_all x1, waiting for transfers between devices: 17.6 us -> 14.7 us  [per_device(): lax.all_to_all(partial.reshape(n_blk, rows, width + LANES), group_axes, 0...]
    all_to_all x1, starting transfers between devices: 3.66 us -> 6.03 us  [per_device(): lax.all_to_all(gathered.reshape((n_blk,) + gathered.shape[2:]), group_axe...]
    ppermute x5 -> x4, waiting for transfers between devices: 4.87 us -> 6.27 us  [the longest x3 5.25 us: per_device(): kv.append(lax.ppermute(pieces[step], ('yh', 'yl'), pairs))]
  transfers between devices with their start and end apart: 22 -> 21, of which waited for: 13 -> 11; matrix products, arithmetic and copies ran while one was open for 1% -> 1% of each run, Pallas kernels for 0% -> 0%
where the time goes in v4:
time: 229 us; the launch traced here: 228 us
  waiting for transfers between devices  58.9 us (26%)
  starting transfers between devices  56.2 us (25%)
  blocking collectives  54.2 us (24%)
  Pallas kernels  46.9 us (20%)
  local copies, waits for them, and re-layouts  5.78 us (3%)
  other arithmetic  3.11 us (1%)
    all_to_all x1, blocking collectives, per_device(): lax.all_to_all(sums.reshape(n_narrow, slots // n_narrow, -1), NARROW, 0, 0)  34.7 us
    pallas_call x1, Pallas kernels, attention(): pl.pallas_call(functools.partial(attention_kernel, heads), in_specs=[pl.B...  31.8 us
    all_to_all x1, blocking collectives, per_device(): activated = lax.all_to_all(activated, NARROW, 0, 0).reshape(slots, -1)  19.5 us
    all_to_all x1, waiting for transfers between devices, per_device(): lax.all_to_all(partial.reshape(n_blk, rows, width + LANES), group_axes, 0...  14.7 us
    all_to_all x1, waiting for transfers between devices, per_device(): lax.all_to_all(gathered.reshape((n_blk,) + gathered.shape[2:]), group_axe...  8.79 us
    all_to_all x1, waiting for transfers between devices, per_device(): lax.all_to_all(expert_out.reshape(n_blk, exp_dev * CAP, -1), BLK, 0, 0)  8 us
    all_to_all x1, starting transfers between devices, per_device(): lax.all_to_all(partial.reshape(n_blk, rows, width + LANES), group_axes, 0...  7.83 us
    pallas_call x1, Pallas kernels, gate_up(): pl.pallas_call(gate_up_kernel, in_specs=[vmem] * 3 + [anywhere] * 2, out_...  7.72 us
  transfers between devices with their start and end apart: 21, of which 11 were waited for; matrix products, arithmetic and copies ran while one was open for 1% of the time, Pallas kernels for 0%

profile of v4, /device:TPU:1, one launch (start us, length us, event | category | flops | bytes accessed | tf_op | source)
XLA Modules:
  0.0 228.1 jit_solution(5412304380202359790)
XLA Ops:
  0.0 1.4 dynamic-slice_bitcast_fusion
  1.5 0.5 slice.12
  2.0 0.1 reshape.143
  2.1 0.9 dynamic-slice_reduce_fusion.1
  3.1 0.1 copy.38
  3.2 0.1 copy.39
  3.9 0.1 concatenate.17
  4.0 1.5 collective-permute-start
  5.5 1.5 collective-permute-start.6
  7.0 0.1 concatenate.16
  7.2 1.7 collective-permute-start.1
  8.9 2.2 collective-permute-start.7
  11.1 0.6 collective-permute-start.5
  11.7 1.0 collective-permute-done.1
  12.8 1.3 collective-permute-start.2
  14.1 1.3 collective-permute-start.8
  15.4 2.5 %collective-permute-start.3 = (bf16[128,1152]{1,0:T(8,128)(2,1)S(1)}, bf16[128,1152]{1,0:T(8,128)(2,1)S(1)}, u32[]{:S(2)}, u32[]{:S(2)}) collective-permute-start(bf16[128,1152]{1,0:T(8,128)(2,1)S(1)} %pad_maximum_fusion.refs_0_), channel_id=1, source_target_pairs={{0,32},{16,48},{32,0},{48,16},{1,33},{17,49},{33,1},{49,17},{2,34}... | collective-permute-start | bytes 884744 | tf_op jit(solution)/shard_map/ppermute | solution.py:465
  17.9 5.2 %collective-permute-done.7.refs_7_ = bf16[2,4,128,128]{3,2,1,0:T(8,128)(2,1)S(1)} collective-permute-done((bf16[2,4,128,128]{3,2,1,0:T(8,128)(2,1)S(1)}, bf16[2,4,128,128]{3,2,1,0:T(8,128)(2,1)S(1)}, u32[]{:S(2)}, u32[]{:S(2)}) %collective-permute-start.7) | collective-permute-done | bytes 262176 | tf_op jit(solution)/shard_map/ppermute | solution.py:438
  23.1 2.5 %collective-permute-start.4 = (bf16[128,1152]{1,0:T(8,128)(2,1)S(1)}, bf16[128,1152]{1,0:T(8,128)(2,1)S(1)}, u32[]{:S(2)}, u32[]{:S(2)}) collective-permute-start(bf16[128,1152]{1,0:T(8,128)(2,1)S(1)} %pad_maximum_fusion.refs_0_), channel_id=1, source_target_pairs={{0,48},{16,0},{32,16},{48,32},{1,49},{17,1},{33,17},{49,33},{2,50}... | collective-permute-start | bytes 884744 | tf_op jit(solution)/shard_map/ppermute | solution.py:465
  25.6 1.7 collective-permute-start.10
  27.3 0.1 collective-permute-start.11
  27.4 0.4 collective-permute-start.9
  27.8 0.1 stack.124.info_ref
  27.9 1.0 collective-permute-done.3.refs_2_
  29.0 1.5 collective-permute-done.4.refs_3_
  30.4 31.8 %attention.1 = bf16[512,1152]{1,0:T(8,128)(2,1)} custom-call(s32[24]{0:T(128)S(1)} %stack.124.info_ref, bf16[128,1152]{1,0:T(8,128)(2,1)S(1)} %pad_maximum_fusion.refs_0_, bf16[128,1152]{1,0:T(8,128)(2,1)S(1)} %collective-permute-done.2.refs_1_, bf16[128,1152]{1,0:T(8,128)(2,1)S(1)} %collective-permute-done.3.refs_2_, ...), custom_call_target="tpu_custom_call" | custom-call | flops 12884901888 | bytes 6291456 | tf_op jit(solution)/shard_map/attention/pallas_call | solution.py:183
  62.3 7.8 %all-to-all-start = ((bf16[16,32,1152]{2,1,0:T(8,128)(2,1)}), bf16[16,32,1152]{2,1,0:T(8,128)(2,1)S(1)}, u32[]{:S(2)}, u32[]{:S(2)}) async-start(bf16[16,32,1152]{2,1,0:T(8,128)(2,1)} %bitcast.33), calls=%async_computation | async-start | bytes 2359296 | tf_op jit(solution)/shard_map/all_to_all | solution.py:474
  70.1 14.7 %all-to-all-done.x_ref = bf16[16,32,1152]{2,1,0:T(8,128)(2,1)S(1)} async-done(((bf16[16,32,1152]{2,1,0:T(8,128)(2,1)}), bf16[16,32,1152]{2,1,0:T(8,128)(2,1)S(1)}, u32[]{:S(2)}, u32[]{:S(2)}) %all-to-all-start) | async-done | bytes 1179680 | tf_op jit(solution)/shard_map/all_to_all | solution.py:474
  84.8 0.9 combine.1
  85.7 2.1 collective-permute-start.12
  87.8 3.3 %collective-permute-start.13 = (bf16[2,32,512]{2,1,0:T(8,128)(2,1)S(1)}, bf16[2,32,512]{2,1,0:T(8,128)(2,1)S(1)}, u32[]{:S(2)}, u32[]{:S(2)}) collective-permute-start(bf16[2,32,512]{2,1,0:T(8,128)(2,1)S(1)} %combine.1), channel_id=1, source_target_pairs={{0,2},{1,3},{2,0},{3,1},{4,6},{5,7},{6,4},{7,5},{8,10},{9,11},{10,... | collective-permute-start | bytes 196616 | tf_op jit(solution)/shard_map/ppermute | solution.py:481
  91.1 0.2 collective-permute-start.14
  91.4 2.0 collective-permute-done.13
  93.4 2.1 collective-permute-done.14
  95.5 0.9 broadcast_in_dim.56
  96.3 6.0 %all-to-all-start.1 = ((bf16[16,32,512]{2,1,0:T(8,128)(2,1)}), bf16[16,32,512]{2,1,0:T(8,128)(2,1)S(1)}, u32[]{:S(2)}, u32[]{:S(2)}) async-start(bf16[16,32,512]{2,1,0:T(8,128)(2,1)} %bitcast.39), calls=%async_computation.1 | async-start | bytes 1048576 | tf_op jit(solution)/shard_map/all_to_all | solution.py:485
  102.5 0.1 eq.82
  102.5 8.8 %all-to-all-done.1 = bf16[16,32,512]{2,1,0:T(8,128)(2,1)S(1)} async-done(((bf16[16,32,512]{2,1,0:T(8,128)(2,1)}), bf16[16,32,512]{2,1,0:T(8,128)(2,1)S(1)}, u32[]{:S(2)}, u32[]{:S(2)}) %all-to-all-start.1) | async-done | bytes 524320 | tf_op jit(solution)/shard_map/all_to_all | solution.py:485
  111.3 0.4 project.1
  111.8 4.3 %collective-permute-start.15 = (bf16[256,512]{1,0:T(8,128)(2,1)S(1)}, bf16[256,512]{1,0:T(8,128)(2,1)S(1)}, u32[]{:S(2)}, u32[]{:S(2)}) collective-permute-start(bf16[256,512]{1,0:T(8,128)(2,1)S(1)} %get-tuple-element.8), channel_id=1, source_target_pairs={{0,8},{8,0},{1,9},{9,1},{2,10},{10,2},{3,11},{11,3},{4,12},{12,4},... | collective-permute-start | bytes 786440 | tf_op jit(solution)/shard_map/ppermute | solution.py:487
  116.1 0.1 eq.78
  116.2 0.6 reduce-window.6
  116.8 0.2 slice_reduce_fusion
  117.0 0.1 fusion.7
  117.1 0.1 reduce_sum.31
  117.2 0.8 add_convert_fusion
  118.0 3.4 %all-to-all-start.2 = ((bf16[8,32,512]{2,1,0:T(8,128)(2,1)}), bf16[8,32,512]{2,1,0:T(8,128)(2,1)S(1)}, u32[]{:S(2)}, u32[]{:S(2)}) async-start(bf16[8,32,512]{2,1,0:T(8,128)(2,1)} %bitcast.41), calls=%async_computation.2 | async-start | bytes 524288 | tf_op jit(solution)/shard_map/all_to_all | solution.py:489
  121.4 0.2 fusion.4
  121.6 7.1 %all-to-all-done.2 = bf16[8,32,512]{2,1,0:T(8,128)(2,1)S(1)} async-done(((bf16[8,32,512]{2,1,0:T(8,128)(2,1)}), bf16[8,32,512]{2,1,0:T(8,128)(2,1)S(1)}, u32[]{:S(2)}, u32[]{:S(2)}) %all-to-all-start.2) | async-done | bytes 262176 | tf_op jit(solution)/shard_map/all_to_all | solution.py:489
  128.8 1.1 convolution_convert_fusion
  129.9 4.2 %all-to-all-start.3 = ((bf16[16,24,512]{2,1,0:T(8,128)(2,1)}), bf16[16,24,512]{2,1,0:T(8,128)(2,1)S(1)}, u32[]{:S(2)}, u32[]{:S(2)}) async-start(bf16[16,24,512]{2,1,0:T(8,128)(2,1)} %bitcast.43), calls=%async_computation.3 | async-start | bytes 786432 | tf_op jit(solution)/shard_map/all_to_all | solution.py:507
  134.1 1.0 fusion.3
  135.0 7.4 %all-to-all-done.3 = bf16[16,24,512]{2,1,0:T(8,128)(2,1)S(1)} async-done(((bf16[16,24,512]{2,1,0:T(8,128)(2,1)}), bf16[16,24,512]{2,1,0:T(8,128)(2,1)S(1)}, u32[]{:S(2)}, u32[]{:S(2)}) %all-to-all-start.3) | async-done | bytes 393248 | tf_op jit(solution)/shard_map/all_to_all | solution.py:507
  142.4 0.7 copy-done.2
  143.2 7.7 %gate_up.1 = bf16[384,3200]{1,0:T(8,128)(2,1)} custom-call(bf16[384,512]{1,0:T(8,128)(2,1)} %bitcast.95, bf16[384,384]{1,0:T(8,128)(2,1)} %get-tuple-element.20.perm_ref, f32[1,512]{1,0:T(1,128)} %bitcast.101, bf16[4,512,1536]{2,1,0:T(8,128)(2,1)} %gate_hbm.1, bf16[4,512,1536]{2,1,0:T(8,128)(2,1)} %up_hbm.1), custom_call_target="tpu_custom_call" | custom-call | flops 1207959552 | bytes 14942208 | tf_op jit(solution)/shard_map/gate_up/pallas_call | solution.py:304
  150.9 34.7 %all_to_all.35.x_ref = bf16[8,48,3200]{2,1,0:T(8,128)(2,1)S(1)} all-to-all(bf16[8,48,3200]{2,1,0:T(8,128)(2,1)} %bitcast.90), channel_id=1, replica_groups=mesh['zl'=2,'x'=4,'core'=2,'zh'=2,'yh'=2,'yl'=2] {'zh','yh','yl'}, dimensions={0} | all-to-all | bytes 4915200 | tf_op jit(solution)/shard_map/all_to_all | solution.py:518
  185.6 0.5 activate.1
  186.1 19.5 %all_to_all.36 = bf16[8,48,1536]{2,1,0:T(8,128)(2,1)} all-to-all(bf16[8,48,1536]{2,1,0:T(8,128)(2,1)S(1)} %activate.1), channel_id=1, replica_groups=mesh['zl'=2,'x'=4,'core'=2,'zh'=2,'yh'=2,'yl'=2] {'zh','yh','yl'}, dimensions={0} | all-to-all | bytes 2359296 | tf_op jit(solution)/shard_map/all_to_all | solution.py:520
  205.6 5.6 %down.1 = bf16[384,512]{1,0:T(8,128)(2,1)} custom-call(bf16[384,1536]{1,0:T(8,128)(2,1)} %bitcast.91, bf16[384,384]{1,0:T(8,128)(2,1)} %get-tuple-element.19.back_ref, bf16[4,1536,512]{2,1,0:T(8,128)(2,1)} %down_hbm.1), custom_call_target="tpu_custom_call" | custom-call | flops 603979776 | bytes 6291456 | tf_op jit(solution)/shard_map/down/pallas_call | solution.py:378
  211.2 7.7 %all-to-all-start.6 = ((bf16[16,24,512]{2,1,0:T(8,128)(2,1)}), bf16[16,24,512]{2,1,0:T(8,128)(2,1)S(1)}, u32[]{:S(2)}, u32[]{:S(2)}) async-start(bf16[16,24,512]{2,1,0:T(8,128)(2,1)} %bitcast.94), calls=%async_computation.6 | async-start | bytes 786432 | tf_op jit(solution)/shard_map/all_to_all | solution.py:522
  218.9 0.2 select_reduce_fusion
  219.1 8.0 %all-to-all-done.6 = bf16[16,24,512]{2,1,0:T(8,128)(2,1)S(1)} async-done(((bf16[16,24,512]{2,1,0:T(8,128)(2,1)}), bf16[16,24,512]{2,1,0:T(8,128)(2,1)S(1)}, u32[]{:S(2)}, u32[]{:S(2)}) %all-to-all-start.6) | async-done | bytes 393248 | tf_op jit(solution)/shard_map/all_to_all | solution.py:522
  227.1 0.2 fusion.11
  227.3 0.8 fusion.1
  (51 shorter events, 0.6 us)
Async XLA Ops:
  0.0 2.0 copy-start
  0.0 3.0 %copy-start.7 = (s32[32]{0:T(128)S(1)}, s32[32]{0:T(128)}, u32[]{:S(2)}) copy-start(s32[32]{0:T(128)} %param.17) | copy-start | bytes 388
  0.0 3.3 %copy-start.4 = (s32[32,64]{1,0:T(8,128)S(1)}, s32[32,64]{1,0:T(8,128)}, u32[]{:S(2)}) copy-start(s32[32,64]{1,0:T(8,128)} %param.16) | copy-start | bytes 24580
  4.0 3.1 %collective-permute-start = (bf16[32,1152]{1,0:T(8,128)(2,1)S(1)}, bf16[32,1152]{1,0:T(8,128)(2,1)S(1)}, u32[]{:S(2)}, u32[]{:S(2)}) collective-permute-start(bf16[32,1152]{1,0:T(8,128)(2,1)S(1)} %concatenate.17), channel_id=1, source_target_pairs={{0,8},{8,0},{1,9},{9,1},{2,10},{10,2},{3,11},{11,3},{4,12},{12,4},... | collective-permute-start | bytes 221192 | tf_op jit(solution)/shard_map/ppermute | solution.py:456
  5.5 9.9 %collective-permute-start.6 = (bf16[2,4,128,128]{3,2,1,0:T(8,128)(2,1)S(1)}, bf16[2,4,128,128]{3,2,1,0:T(8,128)(2,1)S(1)}, u32[]{:S(2)}, u32[]{:S(2)}) collective-permute-start(bf16[2,4,128,128]{3,2,1,0:T(8,128)(2,1)S(1)} %pad_maximum_fusion.3), channel_id=1, source_target_pairs={{0,1},{1,0},{2,3},{3,2},{4,5},{5,4},{6,7},{7,6},{8,9},{9,8},{10,11... | collective-permute-start | bytes 786440 | tf_op jit(solution)/shard_map/ppermute | solution.py:438
  7.2 5.6 %collective-permute-start.1 = (bf16[64,1152]{1,0:T(8,128)(2,1)S(1)}, bf16[64,1152]{1,0:T(8,128)(2,1)S(1)}, u32[]{:S(2)}, u32[]{:S(2)}) collective-permute-start(bf16[64,1152]{1,0:T(8,128)(2,1)S(1)} %pad_maximum_fusion.5), channel_id=1, source_target_pairs={{0,64},{64,0},{1,65},{65,1},{2,66},{66,2},{3,67},{67,3},{4,68},{68... | collective-permute-start | bytes 442376 | tf_op jit(solution)/shard_map/ppermute | solution.py:458
  8.9 14.2 %collective-permute-start.7 = (bf16[2,4,128,128]{3,2,1,0:T(8,128)(2,1)S(1)}, bf16[2,4,128,128]{3,2,1,0:T(8,128)(2,1)S(1)}, u32[]{:S(2)}, u32[]{:S(2)}) collective-permute-start(bf16[2,4,128,128]{3,2,1,0:T(8,128)(2,1)S(1)} %pad_maximum_fusion.4), channel_id=1, source_target_pairs={{0,3},{1,2},{2,1},{3,0},{4,7},{5,6},{6,5},{7,4},{8,11},{9,10},{10,... | collective-permute-start | bytes 786440 | tf_op jit(solution)/shard_map/ppermute | solution.py:438
  11.1 14.4 %collective-permute-start.5 = (bf16[2,4,128,128]{3,2,1,0:T(8,128)(2,1)S(1)}, bf16[2,4,128,128]{3,2,1,0:T(8,128)(2,1)S(1)}, u32[]{:S(2)}, u32[]{:S(2)}) collective-permute-start(bf16[2,4,128,128]{3,2,1,0:T(8,128)(2,1)S(1)} %pad_maximum_fusion.2), channel_id=1, source_target_pairs={{0,2},{1,3},{2,0},{3,1},{4,6},{5,7},{6,4},{7,5},{8,10},{9,11},{10,... | collective-permute-start | bytes 786440 | tf_op jit(solution)/shard_map/ppermute | solution.py:438
  12.8 14.6 %collective-permute-start.2 = (bf16[128,1152]{1,0:T(8,128)(2,1)S(1)}, bf16[128,1152]{1,0:T(8,128)(2,1)S(1)}, u32[]{:S(2)}, u32[]{:S(2)}) collective-permute-start(bf16[128,1152]{1,0:T(8,128)(2,1)S(1)} %pad_maximum_fusion.refs_0_), channel_id=1, source_target_pairs={{0,16},{16,32},{32,48},{48,0},{1,17},{17,33},{33,49},{49,1},{2,18}... | collective-permute-start | bytes 884744 | tf_op jit(solution)/shard_map/ppermute | solution.py:465
  14.1 13.2 %collective-permute-start.8 = (bf16[2,4,128,128]{3,2,1,0:T(8,128)(2,1)S(1)}, bf16[2,4,128,128]{3,2,1,0:T(8,128)(2,1)S(1)}, u32[]{:S(2)}, u32[]{:S(2)}) collective-permute-start(bf16[2,4,128,128]{3,2,1,0:T(8,128)(2,1)S(1)} %pad_maximum_fusion.1.refs_4_), channel_id=1, source_target_pairs={{0,8},{8,0},{1,9},{9,1},{2,10},{10,2},{3,11},{11,3},{4,12},{12,4},... | collective-permute-start | bytes 786440 | tf_op jit(solution)/shard_map/ppermute | solution.py:439
  15.4 13.6 %collective-permute-start.3 = (bf16[128,1152]{1,0:T(8,128)(2,1)S(1)}, bf16[128,1152]{1,0:T(8,128)(2,1)S(1)}, u32[]{:S(2)}, u32[]{:S(2)}) collective-permute-start(bf16[128,1152]{1,0:T(8,128)(2,1)S(1)} %pad_maximum_fusion.refs_0_), channel_id=1, source_target_pairs={{0,32},{16,48},{32,0},{48,16},{1,33},{17,49},{33,1},{49,17},{2,34}... | collective-permute-start | bytes 884744 | tf_op jit(solution)/shard_map/ppermute | solution.py:465
  23.1 7.3 %collective-permute-start.4 = (bf16[128,1152]{1,0:T(8,128)(2,1)S(1)}, bf16[128,1152]{1,0:T(8,128)(2,1)S(1)}, u32[]{:S(2)}, u32[]{:S(2)}) collective-permute-start(bf16[128,1152]{1,0:T(8,128)(2,1)S(1)} %pad_maximum_fusion.refs_0_), channel_id=1, source_target_pairs={{0,48},{16,0},{32,16},{48,32},{1,49},{17,1},{33,17},{49,33},{2,50}... | collective-permute-start | bytes 884744 | tf_op jit(solution)/shard_map/ppermute | solution.py:465
  25.6 4.9 %collective-permute-start.10 = (bf16[2,4,128,128]{3,2,1,0:T(8,128)(2,1)S(1)}, bf16[2,4,128,128]{3,2,1,0:T(8,128)(2,1)S(1)}, u32[]{:S(2)}, u32[]{:S(2)}) collective-permute-start(bf16[2,4,128,128]{3,2,1,0:T(8,128)(2,1)S(1)} %collective-permute-done.6.refs_6_), channel_id=1, source_target_pairs={{0,8},{8,0},{1,9},{9,1},{2,10},{10,2},{3,11},{11,3},{4,12},{12,4},... | collective-permute-start | bytes 786440 | tf_op jit(solution)/shard_map/ppermute | solution.py:439
  27.3 3.1 %collective-permute-start.11 = (bf16[2,4,128,128]{3,2,1,0:T(8,128)(2,1)S(1)}, bf16[2,4,128,128]{3,2,1,0:T(8,128)(2,1)S(1)}, u32[]{:S(2)}, u32[]{:S(2)}) collective-permute-start(bf16[2,4,128,128]{3,2,1,0:T(8,128)(2,1)S(1)} %collective-permute-done.7.refs_7_), channel_id=1, source_target_pairs={{0,8},{8,0},{1,9},{9,1},{2,10},{10,2},{3,11},{11,3},{4,12},{12,4},... | collective-permute-start | bytes 786440 | tf_op jit(solution)/shard_map/ppermute | solution.py:439
  27.4 3.0 %collective-permute-start.9 = (bf16[2,4,128,128]{3,2,1,0:T(8,128)(2,1)S(1)}, bf16[2,4,128,128]{3,2,1,0:T(8,128)(2,1)}, u32[]{:S(2)}, u32[]{:S(2)}) collective-permute-start(bf16[2,4,128,128]{3,2,1,0:T(8,128)(2,1)S(1)} %collective-permute-done.5.refs_5_), channel_id=1, source_target_pairs={{0,8},{8,0},{1,9},{9,1},{2,10},{10,2},{3,11},{11,3},{4,12},{12,4},... | collective-permute-start | bytes 786440 | tf_op jit(solution)/shard_map/ppermute | solution.py:439
  62.3 22.6 %all-to-all-start = ((bf16[16,32,1152]{2,1,0:T(8,128)(2,1)}), bf16[16,32,1152]{2,1,0:T(8,128)(2,1)S(1)}, u32[]{:S(2)}, u32[]{:S(2)}) async-start(bf16[16,32,1152]{2,1,0:T(8,128)(2,1)} %bitcast.33), calls=%async_computation | async-start | bytes 2359296 | tf_op jit(solution)/shard_map/all_to_all | solution.py:474
  70.1 32.3 %copy-start.5 = (s32[32,8]{0,1:T(8,128)S(1)}, s32[32,8]{0,1:T(8,128)}, u32[]{:S(2)}) copy-start(s32[32,8]{0,1:T(8,128)} %param.21) | copy-start | bytes 3076
  70.1 41.2 %copy-start.1 = (bf16[512,512]{1,0:T(8,128)(2,1)S(1)}, bf16[512,512]{1,0:T(8,128)(2,1)}, u32[]{:S(2)}) copy-start(bf16[512,512]{1,0:T(8,128)(2,1)} %weight_ref.1) | copy-start | bytes 1572868
  85.7 5.6 %collective-permute-start.12 = (bf16[2,32,512]{2,1,0:T(8,128)(2,1)S(1)}, bf16[2,32,512]{2,1,0:T(8,128)(2,1)S(1)}, u32[]{:S(2)}, u32[]{:S(2)}) collective-permute-start(bf16[2,32,512]{2,1,0:T(8,128)(2,1)S(1)} %combine.1), channel_id=1, source_target_pairs={{0,1},{1,0},{2,3},{3,2},{4,5},{5,4},{6,7},{7,6},{8,9},{9,8},{10,11... | collective-permute-start | bytes 196616 | tf_op jit(solution)/shard_map/ppermute | solution.py:481
  87.8 5.6 %collective-permute-start.13 = (bf16[2,32,512]{2,1,0:T(8,128)(2,1)S(1)}, bf16[2,32,512]{2,1,0:T(8,128)(2,1)S(1)}, u32[]{:S(2)}, u32[]{:S(2)}) collective-permute-start(bf16[2,32,512]{2,1,0:T(8,128)(2,1)S(1)} %combine.1), channel_id=1, source_target_pairs={{0,2},{1,3},{2,0},{3,1},{4,6},{5,7},{6,4},{7,5},{8,10},{9,11},{10,... | collective-permute-start | bytes 196616 | tf_op jit(solution)/shard_map/ppermute | solution.py:481
  91.1 4.3 %collective-permute-start.14 = (bf16[2,32,512]{2,1,0:T(8,128)(2,1)S(1)}, bf16[2,32,512]{2,1,0:T(8,128)(2,1)S(1)}, u32[]{:S(2)}, u32[]{:S(2)}) collective-permute-start(bf16[2,32,512]{2,1,0:T(8,128)(2,1)S(1)} %combine.1), channel_id=1, source_target_pairs={{0,3},{1,2},{2,1},{3,0},{4,7},{5,6},{6,5},{7,4},{8,11},{9,10},{10,... | collective-permute-start | bytes 196616 | tf_op jit(solution)/shard_map/ppermute | solution.py:481
  95.5 33.4 %copy-start.3 = (bf16[32,512]{1,0:T(8,128)(2,1)S(1)}, bf16[32,512]{1,0:T(8,128)(2,1)}, u32[]{:S(2)}) copy-start(bf16[32,512]{1,0:T(8,128)(2,1)} %param.19) | copy-start | bytes 98308
  96.3 15.0 %all-to-all-start.1 = ((bf16[16,32,512]{2,1,0:T(8,128)(2,1)}), bf16[16,32,512]{2,1,0:T(8,128)(2,1)S(1)}, u32[]{:S(2)}, u32[]{:S(2)}) async-start(bf16[16,32,512]{2,1,0:T(8,128)(2,1)} %bitcast.39), calls=%async_computation.1 | async-start | bytes 1048576 | tf_op jit(solution)/shard_map/all_to_all | solution.py:485
  111.8 5.5 %collective-permute-start.15 = (bf16[256,512]{1,0:T(8,128)(2,1)S(1)}, bf16[256,512]{1,0:T(8,128)(2,1)S(1)}, u32[]{:S(2)}, u32[]{:S(2)}) collective-permute-start(bf16[256,512]{1,0:T(8,128)(2,1)S(1)} %get-tuple-element.8), channel_id=1, source_target_pairs={{0,8},{8,0},{1,9},{9,1},{2,10},{10,2},{3,11},{11,3},{4,12},{12,4},... | collective-permute-start | bytes 786440 | tf_op jit(solution)/shard_map/ppermute | solution.py:487
  118.0 10.8 %all-to-all-start.2 = ((bf16[8,32,512]{2,1,0:T(8,128)(2,1)}), bf16[8,32,512]{2,1,0:T(8,128)(2,1)S(1)}, u32[]{:S(2)}, u32[]{:S(2)}) async-start(bf16[8,32,512]{2,1,0:T(8,128)(2,1)} %bitcast.41), calls=%async_computation.2 | async-start | bytes 524288 | tf_op jit(solution)/shard_map/all_to_all | solution.py:489
  129.9 12.5 %all-to-all-start.3 = ((bf16[16,24,512]{2,1,0:T(8,128)(2,1)}), bf16[16,24,512]{2,1,0:T(8,128)(2,1)S(1)}, u32[]{:S(2)}, u32[]{:S(2)}) async-start(bf16[16,24,512]{2,1,0:T(8,128)(2,1)} %bitcast.43), calls=%async_computation.3 | async-start | bytes 786432 | tf_op jit(solution)/shard_map/all_to_all | solution.py:507
  142.4 0.8 copy-start.2
  205.6 13.3 %copy-start.6 = (f32[32,8]{0,1:T(8,128)S(1)}, f32[32,8]{0,1:T(8,128)}, u32[]{:S(2)}) copy-start(f32[32,8]{0,1:T(8,128)} %param.22) | copy-start | bytes 3076
  211.2 15.9 %all-to-all-start.6 = ((bf16[16,24,512]{2,1,0:T(8,128)(2,1)}), bf16[16,24,512]{2,1,0:T(8,128)(2,1)S(1)}, u32[]{:S(2)}, u32[]{:S(2)}) async-start(bf16[16,24,512]{2,1,0:T(8,128)(2,1)} %bitcast.94), calls=%async_computation.6 | async-start | bytes 786432 | tf_op jit(solution)/shard_map/all_to_all | solution.py:522

commit v5 on v4

--- a/solution.py
+++ b/solution.py
@@ -155,7 +155,7 @@
 
     @pl.when(small)
     def _():
-        lax.fori_loop(0, heads, small_head, 0)
+        lax.fori_loop(0, heads, small_head, 0, unroll=2)
 
     @pl.when(jnp.logical_not(small))
     def _():
@@ -279,7 +279,7 @@
     for e in range(experts):
         at = slice(e * count, (e + 1) * count)
         rows = jnp.dot(perm_ref[at, :], x_ref[...], preferred_element_type=jnp.float32)
-        scaled = (rows * gain_ref[...]).astype(jnp.bfloat16)
+        scaled = (rows * gain_ref[0:1, :]).astype(jnp.bfloat16)
         squares = jnp.sum(rows * rows, axis=1, keepdims=True)
         high, mid, _ = split_bf16(squares)
         lane = lax.broadcasted_iota(jnp.int32, (count, LANES), 1)
@@ -512,8 +512,9 @@
     perm = (order[:, None] == place[None, :]).astype(jnp.bfloat16)
 
     back = (place[:, None] == order[None, :]).astype(jnp.bfloat16)
+    gain = jnp.broadcast_to(norm_gain[None], (8, norm_gain.shape[0])) + perm[0, 1] * 0
     sums = gate_up(
-        incoming.reshape(slots, -1), perm, norm_gain.reshape(1, -1), gate_proj, up_proj
+        incoming.reshape(slots, -1), perm, gain, gate_proj, up_proj
     )
     sums = lax.all_to_all(sums.reshape(n_narrow, slots // n_narrow, -1), NARROW, 0, 0)
     activated = activate(sums)

time: 229 us -> 229 us (level)
  transfers between devices with their start and end apart: 21 -> 21, of which waited for: 11 -> 12; matrix products, arithmetic and copies ran while one was open for 1% -> 2% of each run, Pallas kernels for 0% -> 0%
where the time goes in v5:
time: 229 us; the launch traced here: 228 us
  waiting for transfers between devices  57.6 us (25%)
  starting transfers between devices  56.2 us (25%)
  blocking collectives  54.2 us (24%)
  Pallas kernels  46.9 us (20%)
  local copies, waits for them, and re-layouts  6.4 us (3%)
  other arithmetic  3.04 us (1%)
    all_to_all x1, blocking collectives, per_device(): lax.all_to_all(sums.reshape(n_narrow, slots // n_narrow, -1), NARROW, 0, 0)  34.7 us
    pallas_call x1, Pallas kernels, attention(): pl.pallas_call(functools.partial(attention_kernel, heads), in_specs=[pl.B...  31.8 us
    all_to_all x1, blocking collectives, per_device(): activated = lax.all_to_all(activated, NARROW, 0, 0).reshape(slots, -1)  19.5 us
    all_to_all x1, waiting for transfers between devices, per_device(): lax.all_to_all(partial.reshape(n_blk, rows, width + LANES), group_axes, 0...  14.7 us
    all_to_all x1, waiting for transfers between devices, per_device(): lax.all_to_all(expert_out.reshape(n_blk, exp_dev * CAP, -1), BLK, 0, 0)  8 us
    all_to_all x1, waiting for transfers between devices, per_device(): lax.all_to_all(gathered.reshape((n_blk,) + gathered.shape[2:]), group_axe...  7.85 us
    all_to_all x1, starting transfers between devices, per_device(): lax.all_to_all(partial.reshape(n_blk, rows, width + LANES), group_axes, 0...  7.83 us
    pallas_call x1, Pallas kernels, gate_up(): pl.pallas_call(gate_up_kernel, in_specs=[vmem] * 3 + [anywhere] * 2, out_...  7.71 us
  transfers between devices with their start and end apart: 21, of which 12 were waited for; matrix products, arithmetic and copies ran while one was open for 2% of the time, Pallas kernels for 0%

profile of v5, /device:TPU:1, one launch (start us, length us, event | category | flops | bytes accessed | tf_op | source)
XLA Modules:
  0.0 228.1 jit_solution(10072076523389061475)
XLA Ops:
  0.0 1.4 dynamic-slice_bitcast_fusion
  1.5 0.5 slice.16
  2.1 0.9 dynamic-slice_reduce_fusion.1
  3.1 0.1 copy.38
  3.2 0.1 copy.39
  3.9 0.1 concatenate.17
  4.0 1.5 collective-permute-start
  5.5 1.5 collective-permute-start.6
  7.0 0.1 concatenate.16
  7.2 1.7 collective-permute-start.1
  8.9 2.2 collective-permute-start.7
  11.1 0.6 collective-permute-start.5
  11.7 1.0 collective-permute-done.1
  12.8 1.3 collective-permute-start.2
  14.1 1.3 collective-permute-start.8
  15.4 2.5 %collective-permute-start.3 = (bf16[128,1152]{1,0:T(8,128)(2,1)S(1)}, bf16[128,1152]{1,0:T(8,128)(2,1)S(1)}, u32[]{:S(2)}, u32[]{:S(2)}) collective-permute-start(bf16[128,1152]{1,0:T(8,128)(2,1)S(1)} %pad_maximum_fusion.refs_0_), channel_id=1, source_target_pairs={{0,32},{16,48},{32,0},{48,16},{1,33},{17,49},{33,1},{49,17},{2,34}... | collective-permute-start | bytes 884744 | tf_op jit(solution)/shard_map/ppermute | solution.py:465
  17.9 5.2 %collective-permute-done.7.refs_7_ = bf16[2,4,128,128]{3,2,1,0:T(8,128)(2,1)S(1)} collective-permute-done((bf16[2,4,128,128]{3,2,1,0:T(8,128)(2,1)S(1)}, bf16[2,4,128,128]{3,2,1,0:T(8,128)(2,1)S(1)}, u32[]{:S(2)}, u32[]{:S(2)}) %collective-permute-start.7) | collective-permute-done | bytes 262176 | tf_op jit(solution)/shard_map/ppermute | solution.py:438
  23.1 2.5 %collective-permute-start.4 = (bf16[128,1152]{1,0:T(8,128)(2,1)S(1)}, bf16[128,1152]{1,0:T(8,128)(2,1)S(1)}, u32[]{:S(2)}, u32[]{:S(2)}) collective-permute-start(bf16[128,1152]{1,0:T(8,128)(2,1)S(1)} %pad_maximum_fusion.refs_0_), channel_id=1, source_target_pairs={{0,48},{16,0},{32,16},{48,32},{1,49},{17,1},{33,17},{49,33},{2,50}... | collective-permute-start | bytes 884744 | tf_op jit(solution)/shard_map/ppermute | solution.py:465
  25.6 1.7 collective-permute-start.10
  27.4 0.4 collective-permute-start.9
  27.8 0.1 stack.124.info_ref
  27.9 1.0 collective-permute-done.3.refs_2_
  29.0 1.5 collective-permute-done.4.refs_3_
  30.4 31.8 %attention.1 = bf16[512,1152]{1,0:T(8,128)(2,1)} custom-call(s32[24]{0:T(128)S(1)} %stack.124.info_ref, bf16[128,1152]{1,0:T(8,128)(2,1)S(1)} %pad_maximum_fusion.refs_0_, bf16[128,1152]{1,0:T(8,128)(2,1)S(1)} %collective-permute-done.2.refs_1_, bf16[128,1152]{1,0:T(8,128)(2,1)S(1)} %collective-permute-done.3.refs_2_, ...), custom_call_target="tpu_custom_call" | custom-call | flops 12884901888 | bytes 6291456 | tf_op jit(solution)/shard_map/attention/pallas_call | solution.py:183
  62.3 7.8 %all-to-all-start = ((bf16[16,32,1152]{2,1,0:T(8,128)(2,1)}), bf16[16,32,1152]{2,1,0:T(8,128)(2,1)S(1)}, u32[]{:S(2)}, u32[]{:S(2)}) async-start(bf16[16,32,1152]{2,1,0:T(8,128)(2,1)} %bitcast.33), calls=%async_computation | async-start | bytes 2359296 | tf_op jit(solution)/shard_map/all_to_all | solution.py:474
  70.2 14.7 %all-to-all-done.x_ref = bf16[16,32,1152]{2,1,0:T(8,128)(2,1)S(1)} async-done(((bf16[16,32,1152]{2,1,0:T(8,128)(2,1)}), bf16[16,32,1152]{2,1,0:T(8,128)(2,1)S(1)}, u32[]{:S(2)}, u32[]{:S(2)}) %all-to-all-start) | async-done | bytes 1179680 | tf_op jit(solution)/shard_map/all_to_all | solution.py:474
  84.8 0.9 combine.1
  85.7 2.1 collective-permute-start.12
  87.8 3.2 %collective-permute-start.13 = (bf16[2,32,512]{2,1,0:T(8,128)(2,1)S(1)}, bf16[2,32,512]{2,1,0:T(8,128)(2,1)S(1)}, u32[]{:S(2)}, u32[]{:S(2)}) collective-permute-start(bf16[2,32,512]{2,1,0:T(8,128)(2,1)S(1)} %combine.1), channel_id=1, source_target_pairs={{0,2},{1,3},{2,0},{3,1},{4,6},{5,7},{6,4},{7,5},{8,10},{9,11},{10,... | collective-permute-start | bytes 196616 | tf_op jit(solution)/shard_map/ppermute | solution.py:481
  91.1 0.2 collective-permute-start.14
  91.4 2.0 collective-permute-done.13
  93.4 2.1 collective-permute-done.14
  95.4 0.8 broadcast_in_dim.62
  96.3 5.9 %all-to-all-start.1 = ((bf16[16,32,512]{2,1,0:T(8,128)(2,1)}), bf16[16,32,512]{2,1,0:T(8,128)(2,1)S(1)}, u32[]{:S(2)}, u32[]{:S(2)}) async-start(bf16[16,32,512]{2,1,0:T(8,128)(2,1)} %bitcast.39), calls=%async_computation.1 | async-start | bytes 1048576 | tf_op jit(solution)/shard_map/all_to_all | solution.py:485
  102.3 0.1 eq.88
  102.3 0.1 eq.84
  102.5 0.6 reduce-window.6
  103.1 0.2 slice_reduce_fusion
  103.3 7.8 %all-to-all-done.1 = bf16[16,32,512]{2,1,0:T(8,128)(2,1)S(1)} async-done(((bf16[16,32,512]{2,1,0:T(8,128)(2,1)}), bf16[16,32,512]{2,1,0:T(8,128)(2,1)S(1)}, u32[]{:S(2)}, u32[]{:S(2)}) %all-to-all-start.1) | async-done | bytes 524320 | tf_op jit(solution)/shard_map/all_to_all | solution.py:485
  111.1 0.4 project.1
  111.6 4.5 %collective-permute-start.15 = (bf16[256,512]{1,0:T(8,128)(2,1)S(1)}, bf16[256,512]{1,0:T(8,128)(2,1)S(1)}, u32[]{:S(2)}, u32[]{:S(2)}) collective-permute-start(bf16[256,512]{1,0:T(8,128)(2,1)S(1)} %get-tuple-element.8), channel_id=1, source_target_pairs={{0,8},{8,0},{1,9},{9,1},{2,10},{10,2},{3,11},{11,3},{4,12},{12,4},... | collective-permute-start | bytes 786440 | tf_op jit(solution)/shard_map/ppermute | solution.py:487
  116.1 0.1 fusion.7
  116.3 1.0 collective-permute-done.15
  117.2 0.8 add_convert_fusion
  118.0 3.4 %all-to-all-start.2 = ((bf16[8,32,512]{2,1,0:T(8,128)(2,1)}), bf16[8,32,512]{2,1,0:T(8,128)(2,1)S(1)}, u32[]{:S(2)}, u32[]{:S(2)}) async-start(bf16[8,32,512]{2,1,0:T(8,128)(2,1)} %bitcast.41), calls=%async_computation.2 | async-start | bytes 524288 | tf_op jit(solution)/shard_map/all_to_all | solution.py:489
  121.5 0.2 fusion.4
  121.7 7.1 %all-to-all-done.2 = bf16[8,32,512]{2,1,0:T(8,128)(2,1)S(1)} async-done(((bf16[8,32,512]{2,1,0:T(8,128)(2,1)}), bf16[8,32,512]{2,1,0:T(8,128)(2,1)S(1)}, u32[]{:S(2)}, u32[]{:S(2)}) %all-to-all-start.2) | async-done | bytes 262176 | tf_op jit(solution)/shard_map/all_to_all | solution.py:489
  128.8 1.1 convolution_convert_fusion
  129.9 4.2 %all-to-all-start.3 = ((bf16[16,24,512]{2,1,0:T(8,128)(2,1)}), bf16[16,24,512]{2,1,0:T(8,128)(2,1)S(1)}, u32[]{:S(2)}, u32[]{:S(2)}) async-start(bf16[16,24,512]{2,1,0:T(8,128)(2,1)} %bitcast.43), calls=%async_computation.3 | async-start | bytes 786432 | tf_op jit(solution)/shard_map/all_to_all | solution.py:507
  134.0 0.9 fusion.3
  135.0 0.6 slice.18
  136.2 6.2 %all-to-all-done.3 = bf16[16,24,512]{2,1,0:T(8,128)(2,1)S(1)} async-done(((bf16[16,24,512]{2,1,0:T(8,128)(2,1)}), bf16[16,24,512]{2,1,0:T(8,128)(2,1)S(1)}, u32[]{:S(2)}, u32[]{:S(2)}) %all-to-all-start.3) | async-done | bytes 393248 | tf_op jit(solution)/shard_map/all_to_all | solution.py:507
  142.4 0.6 broadcast_in_dim.65.gain_ref
  143.1 0.1 copy-done.2
  143.2 7.7 %gate_up.1 = bf16[384,3200]{1,0:T(8,128)(2,1)} custom-call(bf16[384,512]{1,0:T(8,128)(2,1)} %bitcast.96, bf16[384,384]{1,0:T(8,128)(2,1)} %copy-done.3, f32[8,512]{1,0:T(8,128)} %broadcast_in_dim.65.gain_ref, bf16[4,512,1536]{2,1,0:T(8,128)(2,1)} %gate_hbm.1, bf16[4,512,1536]{2,1,0:T(8,128)(2,1)} %up_hbm.1), custom_call_target="tpu_custom_call" | custom-call | flops 1207959552 | bytes 14942208 | tf_op jit(solution)/shard_map/gate_up/pallas_call | solution.py:304
  150.9 34.7 %all_to_all.35.x_ref = bf16[8,48,3200]{2,1,0:T(8,128)(2,1)S(1)} all-to-all(bf16[8,48,3200]{2,1,0:T(8,128)(2,1)} %bitcast.91), channel_id=1, replica_groups=mesh['zl'=2,'x'=4,'core'=2,'zh'=2,'yh'=2,'yl'=2] {'zh','yh','yl'}, dimensions={0} | all-to-all | bytes 4915200 | tf_op jit(solution)/shard_map/all_to_all | solution.py:519
  185.6 0.5 activate.1
  186.1 19.5 %all_to_all.36 = bf16[8,48,1536]{2,1,0:T(8,128)(2,1)} all-to-all(bf16[8,48,1536]{2,1,0:T(8,128)(2,1)S(1)} %activate.1), channel_id=1, replica_groups=mesh['zl'=2,'x'=4,'core'=2,'zh'=2,'yh'=2,'yl'=2] {'zh','yh','yl'}, dimensions={0} | all-to-all | bytes 2359296 | tf_op jit(solution)/shard_map/all_to_all | solution.py:521
  205.6 5.6 %down.1 = bf16[384,512]{1,0:T(8,128)(2,1)} custom-call(bf16[384,1536]{1,0:T(8,128)(2,1)} %bitcast.92, bf16[384,384]{1,0:T(8,128)(2,1)} %get-tuple-element.19.back_ref, bf16[4,1536,512]{2,1,0:T(8,128)(2,1)} %down_hbm.1), custom_call_target="tpu_custom_call" | custom-call | flops 603979776 | bytes 6291456 | tf_op jit(solution)/shard_map/down/pallas_call | solution.py:378
  211.2 7.7 %all-to-all-start.6 = ((bf16[16,24,512]{2,1,0:T(8,128)(2,1)}), bf16[16,24,512]{2,1,0:T(8,128)(2,1)S(1)}, u32[]{:S(2)}, u32[]{:S(2)}) async-start(bf16[16,24,512]{2,1,0:T(8,128)(2,1)} %bitcast.95), calls=%async_computation.6 | async-start | bytes 786432 | tf_op jit(solution)/shard_map/all_to_all | solution.py:523
  218.9 0.2 select_reduce_fusion
  219.1 8.0 %all-to-all-done.6 = bf16[16,24,512]{2,1,0:T(8,128)(2,1)S(1)} async-done(((bf16[16,24,512]{2,1,0:T(8,128)(2,1)}), bf16[16,24,512]{2,1,0:T(8,128)(2,1)S(1)}, u32[]{:S(2)}, u32[]{:S(2)}) %all-to-all-start.6) | async-done | bytes 393248 | tf_op jit(solution)/shard_map/all_to_all | solution.py:523
  227.1 0.2 fusion.11
  227.3 0.8 fusion.1
  (58 shorter events, 0.8 us)
Async XLA Ops:
  0.0 2.0 copy-start
  0.0 3.0 %copy-start.9 = (s32[32]{0:T(128)S(1)}, s32[32]{0:T(128)}, u32[]{:S(2)}) copy-start(s32[32]{0:T(128)} %param.17) | copy-start | bytes 388
  0.0 3.3 %copy-start.5 = (s32[32,64]{1,0:T(8,128)S(1)}, s32[32,64]{1,0:T(8,128)}, u32[]{:S(2)}) copy-start(s32[32,64]{1,0:T(8,128)} %param.16) | copy-start | bytes 24580
  4.0 3.1 %collective-permute-start = (bf16[32,1152]{1,0:T(8,128)(2,1)S(1)}, bf16[32,1152]{1,0:T(8,128)(2,1)S(1)}, u32[]{:S(2)}, u32[]{:S(2)}) collective-permute-start(bf16[32,1152]{1,0:T(8,128)(2,1)S(1)} %concatenate.17), channel_id=1, source_target_pairs={{0,8},{8,0},{1,9},{9,1},{2,10},{10,2},{3,11},{11,3},{4,12},{12,4},... | collective-permute-start | bytes 221192 | tf_op jit(solution)/shard_map/ppermute | solution.py:456
  5.5 9.9 %collective-permute-start.6 = (bf16[2,4,128,128]{3,2,1,0:T(8,128)(2,1)S(1)}, bf16[2,4,128,128]{3,2,1,0:T(8,128)(2,1)S(1)}, u32[]{:S(2)}, u32[]{:S(2)}) collective-permute-start(bf16[2,4,128,128]{3,2,1,0:T(8,128)(2,1)S(1)} %pad_maximum_fusion.3), channel_id=1, source_target_pairs={{0,1},{1,0},{2,3},{3,2},{4,5},{5,4},{6,7},{7,6},{8,9},{9,8},{10,11... | collective-permute-start | bytes 786440 | tf_op jit(solution)/shard_map/ppermute | solution.py:438
  7.2 5.6 %collective-permute-start.1 = (bf16[64,1152]{1,0:T(8,128)(2,1)S(1)}, bf16[64,1152]{1,0:T(8,128)(2,1)S(1)}, u32[]{:S(2)}, u32[]{:S(2)}) collective-permute-start(bf16[64,1152]{1,0:T(8,128)(2,1)S(1)} %pad_maximum_fusion.5), channel_id=1, source_target_pairs={{0,64},{64,0},{1,65},{65,1},{2,66},{66,2},{3,67},{67,3},{4,68},{68... | collective-permute-start | bytes 442376 | tf_op jit(solution)/shard_map/ppermute | solution.py:458
  8.9 14.2 %collective-permute-start.7 = (bf16[2,4,128,128]{3,2,1,0:T(8,128)(2,1)S(1)}, bf16[2,4,128,128]{3,2,1,0:T(8,128)(2,1)S(1)}, u32[]{:S(2)}, u32[]{:S(2)}) collective-permute-start(bf16[2,4,128,128]{3,2,1,0:T(8,128)(2,1)S(1)} %pad_maximum_fusion.4), channel_id=1, source_target_pairs={{0,3},{1,2},{2,1},{3,0},{4,7},{5,6},{6,5},{7,4},{8,11},{9,10},{10,... | collective-permute-start | bytes 786440 | tf_op jit(solution)/shard_map/ppermute | solution.py:438
  11.1 14.4 %collective-permute-start.5 = (bf16[2,4,128,128]{3,2,1,0:T(8,128)(2,1)S(1)}, bf16[2,4,128,128]{3,2,1,0:T(8,128)(2,1)S(1)}, u32[]{:S(2)}, u32[]{:S(2)}) collective-permute-start(bf16[2,4,128,128]{3,2,1,0:T(8,128)(2,1)S(1)} %pad_maximum_fusion.2), channel_id=1, source_target_pairs={{0,2},{1,3},{2,0},{3,1},{4,6},{5,7},{6,4},{7,5},{8,10},{9,11},{10,... | collective-permute-start | bytes 786440 | tf_op jit(solution)/shard_map/ppermute | solution.py:438
  12.8 14.6 %collective-permute-start.2 = (bf16[128,1152]{1,0:T(8,128)(2,1)S(1)}, bf16[128,1152]{1,0:T(8,128)(2,1)S(1)}, u32[]{:S(2)}, u32[]{:S(2)}) collective-permute-start(bf16[128,1152]{1,0:T(8,128)(2,1)S(1)} %pad_maximum_fusion.refs_0_), channel_id=1, source_target_pairs={{0,16},{16,32},{32,48},{48,0},{1,17},{17,33},{33,49},{49,1},{2,18}... | collective-permute-start | bytes 884744 | tf_op jit(solution)/shard_map/ppermute | solution.py:465
  14.1 13.2 %collective-permute-start.8 = (bf16[2,4,128,128]{3,2,1,0:T(8,128)(2,1)S(1)}, bf16[2,4,128,128]{3,2,1,0:T(8,128)(2,1)S(1)}, u32[]{:S(2)}, u32[]{:S(2)}) collective-permute-start(bf16[2,4,128,128]{3,2,1,0:T(8,128)(2,1)S(1)} %pad_maximum_fusion.1.refs_4_), channel_id=1, source_target_pairs={{0,8},{8,0},{1,9},{9,1},{2,10},{10,2},{3,11},{11,3},{4,12},{12,4},... | collective-permute-start | bytes 786440 | tf_op jit(solution)/shard_map/ppermute | solution.py:439
  15.4 13.6 %collective-permute-start.3 = (bf16[128,1152]{1,0:T(8,128)(2,1)S(1)}, bf16[128,1152]{1,0:T(8,128)(2,1)S(1)}, u32[]{:S(2)}, u32[]{:S(2)}) collective-permute-start(bf16[128,1152]{1,0:T(8,128)(2,1)S(1)} %pad_maximum_fusion.refs_0_), channel_id=1, source_target_pairs={{0,32},{16,48},{32,0},{48,16},{1,33},{17,49},{33,1},{49,17},{2,34}... | collective-permute-start | bytes 884744 | tf_op jit(solution)/shard_map/ppermute | solution.py:465
  23.1 7.3 %collective-permute-start.4 = (bf16[128,1152]{1,0:T(8,128)(2,1)S(1)}, bf16[128,1152]{1,0:T(8,128)(2,1)S(1)}, u32[]{:S(2)}, u32[]{:S(2)}) collective-permute-start(bf16[128,1152]{1,0:T(8,128)(2,1)S(1)} %pad_maximum_fusion.refs_0_), channel_id=1, source_target_pairs={{0,48},{16,0},{32,16},{48,32},{1,49},{17,1},{33,17},{49,33},{2,50}... | collective-permute-start | bytes 884744 | tf_op jit(solution)/shard_map/ppermute | solution.py:465
  25.6 4.9 %collective-permute-start.10 = (bf16[2,4,128,128]{3,2,1,0:T(8,128)(2,1)S(1)}, bf16[2,4,128,128]{3,2,1,0:T(8,128)(2,1)S(1)}, u32[]{:S(2)}, u32[]{:S(2)}) collective-permute-start(bf16[2,4,128,128]{3,2,1,0:T(8,128)(2,1)S(1)} %collective-permute-done.6.refs_6_), channel_id=1, source_target_pairs={{0,8},{8,0},{1,9},{9,1},{2,10},{10,2},{3,11},{11,3},{4,12},{12,4},... | collective-permute-start | bytes 786440 | tf_op jit(solution)/shard_map/ppermute | solution.py:439
  27.3 3.1 %collective-permute-start.11 = (bf16[2,4,128,128]{3,2,1,0:T(8,128)(2,1)S(1)}, bf16[2,4,128,128]{3,2,1,0:T(8,128)(2,1)S(1)}, u32[]{:S(2)}, u32[]{:S(2)}) collective-permute-start(bf16[2,4,128,128]{3,2,1,0:T(8,128)(2,1)S(1)} %collective-permute-done.7.refs_7_), channel_id=1, source_target_pairs={{0,8},{8,0},{1,9},{9,1},{2,10},{10,2},{3,11},{11,3},{4,12},{12,4},... | collective-permute-start | bytes 786440 | tf_op jit(solution)/shard_map/ppermute | solution.py:439
  27.4 3.0 %collective-permute-start.9 = (bf16[2,4,128,128]{3,2,1,0:T(8,128)(2,1)S(1)}, bf16[2,4,128,128]{3,2,1,0:T(8,128)(2,1)}, u32[]{:S(2)}, u32[]{:S(2)}) collective-permute-start(bf16[2,4,128,128]{3,2,1,0:T(8,128)(2,1)S(1)} %collective-permute-done.5.refs_5_), channel_id=1, source_target_pairs={{0,8},{8,0},{1,9},{9,1},{2,10},{10,2},{3,11},{11,3},{4,12},{12,4},... | collective-permute-start | bytes 786440 | tf_op jit(solution)/shard_map/ppermute | solution.py:439
  62.3 22.6 %all-to-all-start = ((bf16[16,32,1152]{2,1,0:T(8,128)(2,1)}), bf16[16,32,1152]{2,1,0:T(8,128)(2,1)S(1)}, u32[]{:S(2)}, u32[]{:S(2)}) async-start(bf16[16,32,1152]{2,1,0:T(8,128)(2,1)} %bitcast.33), calls=%async_computation | async-start | bytes 2359296 | tf_op jit(solution)/shard_map/all_to_all | solution.py:474
  70.1 32.1 %copy-start.6 = (s32[32,8]{0,1:T(8,128)S(1)}, s32[32,8]{0,1:T(8,128)}, u32[]{:S(2)}) copy-start(s32[32,8]{0,1:T(8,128)} %param.21) | copy-start | bytes 3076
  70.1 41.0 %copy-start.1 = (bf16[512,512]{1,0:T(8,128)(2,1)S(1)}, bf16[512,512]{1,0:T(8,128)(2,1)}, u32[]{:S(2)}) copy-start(bf16[512,512]{1,0:T(8,128)(2,1)} %weight_ref.1) | copy-start | bytes 1572868
  85.7 5.6 %collective-permute-start.12 = (bf16[2,32,512]{2,1,0:T(8,128)(2,1)S(1)}, bf16[2,32,512]{2,1,0:T(8,128)(2,1)S(1)}, u32[]{:S(2)}, u32[]{:S(2)}) collective-permute-start(bf16[2,32,512]{2,1,0:T(8,128)(2,1)S(1)} %combine.1), channel_id=1, source_target_pairs={{0,1},{1,0},{2,3},{3,2},{4,5},{5,4},{6,7},{7,6},{8,9},{9,8},{10,11... | collective-permute-start | bytes 196616 | tf_op jit(solution)/shard_map/ppermute | solution.py:481
  87.8 5.5 %collective-permute-start.13 = (bf16[2,32,512]{2,1,0:T(8,128)(2,1)S(1)}, bf16[2,32,512]{2,1,0:T(8,128)(2,1)S(1)}, u32[]{:S(2)}, u32[]{:S(2)}) collective-permute-start(bf16[2,32,512]{2,1,0:T(8,128)(2,1)S(1)} %combine.1), channel_id=1, source_target_pairs={{0,2},{1,3},{2,0},{3,1},{4,6},{5,7},{6,4},{7,5},{8,10},{9,11},{10,... | collective-permute-start | bytes 196616 | tf_op jit(solution)/shard_map/ppermute | solution.py:481
  91.1 4.3 %collective-permute-start.14 = (bf16[2,32,512]{2,1,0:T(8,128)(2,1)S(1)}, bf16[2,32,512]{2,1,0:T(8,128)(2,1)S(1)}, u32[]{:S(2)}, u32[]{:S(2)}) collective-permute-start(bf16[2,32,512]{2,1,0:T(8,128)(2,1)S(1)} %combine.1), channel_id=1, source_target_pairs={{0,3},{1,2},{2,1},{3,0},{4,7},{5,6},{6,5},{7,4},{8,11},{9,10},{10,... | collective-permute-start | bytes 196616 | tf_op jit(solution)/shard_map/ppermute | solution.py:481
  95.4 33.4 %copy-start.4 = (bf16[32,512]{1,0:T(8,128)(2,1)S(1)}, bf16[32,512]{1,0:T(8,128)(2,1)}, u32[]{:S(2)}) copy-start(bf16[32,512]{1,0:T(8,128)(2,1)} %param.19) | copy-start | bytes 98308
  96.3 14.9 %all-to-all-start.1 = ((bf16[16,32,512]{2,1,0:T(8,128)(2,1)}), bf16[16,32,512]{2,1,0:T(8,128)(2,1)S(1)}, u32[]{:S(2)}, u32[]{:S(2)}) async-start(bf16[16,32,512]{2,1,0:T(8,128)(2,1)} %bitcast.39), calls=%async_computation.1 | async-start | bytes 1048576 | tf_op jit(solution)/shard_map/all_to_all | solution.py:485
  111.1 25.1 %copy-start.8 = (f32[512]{0:T(512)S(1)}, f32[512]{0:T(512)}, u32[]{:S(2)}) copy-start(f32[512]{0:T(512)} %param.20) | copy-start | bytes 6148
  111.6 5.7 %collective-permute-start.15 = (bf16[256,512]{1,0:T(8,128)(2,1)S(1)}, bf16[256,512]{1,0:T(8,128)(2,1)S(1)}, u32[]{:S(2)}, u32[]{:S(2)}) collective-permute-start(bf16[256,512]{1,0:T(8,128)(2,1)S(1)} %get-tuple-element.8), channel_id=1, source_target_pairs={{0,8},{8,0},{1,9},{9,1},{2,10},{10,2},{3,11},{11,3},{4,12},{12,4},... | collective-permute-start | bytes 786440 | tf_op jit(solution)/shard_map/ppermute | solution.py:487
  118.0 10.8 %all-to-all-start.2 = ((bf16[8,32,512]{2,1,0:T(8,128)(2,1)}), bf16[8,32,512]{2,1,0:T(8,128)(2,1)S(1)}, u32[]{:S(2)}, u32[]{:S(2)}) async-start(bf16[8,32,512]{2,1,0:T(8,128)(2,1)} %bitcast.41), calls=%async_computation.2 | async-start | bytes 524288 | tf_op jit(solution)/shard_map/all_to_all | solution.py:489
  129.9 12.5 %all-to-all-start.3 = ((bf16[16,24,512]{2,1,0:T(8,128)(2,1)}), bf16[16,24,512]{2,1,0:T(8,128)(2,1)S(1)}, u32[]{:S(2)}, u32[]{:S(2)}) async-start(bf16[16,24,512]{2,1,0:T(8,128)(2,1)} %bitcast.43), calls=%async_computation.3 | async-start | bytes 786432 | tf_op jit(solution)/shard_map/all_to_all | solution.py:507
  135.0 8.1 %copy-start.3 = (bf16[384,384]{1,0:T(8,128)(2,1)}, bf16[384,384]{1,0:T(8,128)(2,1)S(1)}, u32[]{:S(2)}) copy-start(bf16[384,384]{1,0:T(8,128)(2,1)S(1)} %get-tuple-element.20.perm_ref) | copy-start | bytes 884740
  142.4 0.8 copy-start.2
  205.6 13.3 %copy-start.7 = (f32[32,8]{0,1:T(8,128)S(1)}, f32[32,8]{0,1:T(8,128)}, u32[]{:S(2)}) copy-start(f32[32,8]{0,1:T(8,128)} %param.22) | copy-start | bytes 3076
  211.2 15.9 %all-to-all-start.6 = ((bf16[16,24,512]{2,1,0:T(8,128)(2,1)}), bf16[16,24,512]{2,1,0:T(8,128)(2,1)S(1)}, u32[]{:S(2)}, u32[]{:S(2)}) async-start(bf16[16,24,512]{2,1,0:T(8,128)(2,1)} %bitcast.95), calls=%async_computation.6 | async-start | bytes 786432 | tf_op jit(solution)/shard_map/all_to_all | solution.py:523

commit v6 on v5

--- a/solution.py
+++ b/solution.py
@@ -119,7 +119,7 @@
     def head_columns(h):
         return pl.ds(pl.multiple_of(h * HEAD_SIZE, HEAD_SIZE), HEAD_SIZE)
 
-    chunk = 2
+    chunk = 4
 
     def small_head(h, carry):
         cols = head_columns(h)
@@ -433,11 +433,11 @@
 
     pieces = [head_piece(kv_head ^ step) for step in range(KEY_VALUE_HEADS)]
     kv = [pieces[0]]
-    for step in (2, 1, 3):
+    for step in (1, 3, 2):
         pairs = [(i, i ^ step) for i in range(KEY_VALUE_HEADS)]
         kv.append(lax.ppermute(pieces[step], ("yh", "yl"), pairs))
     kv = kv + [lax.ppermute(piece, "core", swap) for piece in kv]
-    sources = [zh * KEY_VALUE_HEADS + (kv_head ^ s) for s in (0, 2, 1, 3)]
+    sources = [zh * KEY_VALUE_HEADS + (kv_head ^ s) for s in (0, 1, 3, 2)]
 
     both = lax.dynamic_slice_in_dim(queries, kv_head * 2 * width, 2 * width, 1)
     both = both.reshape(rows, 2, 2, width // 2)
@@ -459,7 +459,7 @@
     pair = jnp.concatenate([pair, far], axis=0)
 
     all_q, groups = [pair], []
-    for dx in range(size_x):
+    for dx in (0, 2, 1, 3):
         if dx:
             pairs = [(i, (i + dx) % size_x) for i in range(size_x)]
             all_q.append(lax.ppermute(pair, "x", pairs))

time: 229 us -> 228 us (level)
    ppermute x3, waiting for transfers between devices: 5.25 us -> 2.1 us  [per_device(): kv.append(lax.ppermute(pieces[step], ('yh', 'yl'), pairs))]
    all_to_all x1, waiting for transfers between devices: 14.7 us -> 17.5 us  [per_device(): lax.all_to_all(partial.reshape(n_blk, rows, width + LANES), group_axes, 0...]
    ppermute x3, waiting for transfers between devices: 4.05 us -> 1.57 us  [per_device(): piece = lax.ppermute(attended, ('yh', 'yl'), pairs)]
where the time goes in v6:
time: 228 us; the launch traced here: 227 us
  waiting for transfers between devices  58.5 us (26%)
  starting transfers between devices  54.7 us (24%)
  blocking collectives  53.9 us (24%)
  Pallas kernels  46.9 us (21%)
  local copies, waits for them, and re-layouts  6.4 us (3%)
  other arithmetic  3.04 us (1%)
    all_to_all x1, blocking collectives, per_device(): lax.all_to_all(sums.reshape(n_narrow, slots // n_narrow, -1), NARROW, 0, 0)  34.6 us
    pallas_call x1, Pallas kernels, attention(): pl.pallas_call(functools.partial(attention_kernel, heads), in_specs=[pl.B...  31.8 us
    all_to_all x1, blocking collectives, per_device(): activated = lax.all_to_all(activated, NARROW, 0, 0).reshape(slots, -1)  19.3 us
    all_to_all x1, waiting for transfers between devices, per_device(): lax.all_to_all(partial.reshape(n_blk, rows, width + LANES), group_axes, 0...  17.5 us
    all_to_all x1, waiting for transfers between devices, per_device(): lax.all_to_all(expert_out.reshape(n_blk, exp_dev * CAP, -1), BLK, 0, 0)  8 us
    all_to_all x1, starting transfers between devices, per_device(): lax.all_to_all(expert_out.reshape(n_blk, exp_dev * CAP, -1), BLK, 0, 0)  7.98 us
    all_to_all x1, waiting for transfers between devices, per_device(): lax.all_to_all(gathered.reshape((n_blk,) + gathered.shape[2:]), group_axe...  7.85 us
    pallas_call x1, Pallas kernels, gate_up(): pl.pallas_call(gate_up_kernel, in_specs=[vmem] * 3 + [anywhere] * 2, out_...  7.71 us
  transfers between devices with their start and end apart: 21, of which 12 were waited for; matrix products, arithmetic and copies ran while one was open for 2% of the time, Pallas kernels for 0%

profile of v6, /device:TPU:1, one launch (start us, length us, event | category | flops | bytes accessed | tf_op | source)
XLA Modules:
  0.0 227.1 jit_solution(14438675714141837261)
XLA Ops:
  0.0 1.4 dynamic-slice_bitcast_fusion
  1.5 0.5 slice.16
  2.1 0.9 dynamic-slice_reduce_fusion.1
  3.1 0.1 copy.38
  3.2 0.1 copy.39
  3.9 0.1 concatenate.17
  4.0 1.5 collective-permute-start
  5.5 2.9 %collective-permute-start.6 = (bf16[2,4,128,128]{3,2,1,0:T(8,128)(2,1)S(1)}, bf16[2,4,128,128]{3,2,1,0:T(8,128)(2,1)S(1)}, u32[]{:S(2)}, u32[]{:S(2)}) collective-permute-start(bf16[2,4,128,128]{3,2,1,0:T(8,128)(2,1)S(1)} %pad_maximum_fusion.3), channel_id=1, source_target_pairs={{0,3},{1,2},{2,1},{3,0},{4,7},{5,6},{6,5},{7,4},{8,11},{9,10},{10,... | collective-permute-start | bytes 786440 | tf_op jit(solution)/shard_map/ppermute | solution.py:438
  8.5 0.1 concatenate.16
  8.6 1.7 collective-permute-start.1
  10.3 0.9 collective-permute-start.7
  11.3 0.5 collective-permute-start.5
  11.8 2.4 %collective-permute-done.1 = bf16[64,1152]{1,0:T(8,128)(2,1)S(1)} collective-permute-done((bf16[64,1152]{1,0:T(8,128)(2,1)S(1)}, bf16[64,1152]{1,0:T(8,128)(2,1)S(1)}, u32[]{:S(2)}, u32[]{:S(2)}) %collective-permute-start.1) | collective-permute-done | bytes 147488 | tf_op jit(solution)/shard_map/ppermute | solution.py:458
  14.2 2.8 %collective-permute-start.2 = (bf16[128,1152]{1,0:T(8,128)(2,1)S(1)}, bf16[128,1152]{1,0:T(8,128)(2,1)S(1)}, u32[]{:S(2)}, u32[]{:S(2)}) collective-permute-start(bf16[128,1152]{1,0:T(8,128)(2,1)S(1)} %pad_maximum_fusion.refs_0_), channel_id=1, source_target_pairs={{0,32},{16,48},{32,0},{48,16},{1,33},{17,49},{33,1},{49,17},{2,34}... | collective-permute-start | bytes 884744 | tf_op jit(solution)/shard_map/ppermute | solution.py:465
  17.1 1.3 collective-permute-start.8
  18.4 1.6 collective-permute-done.6.refs_6_
  20.0 1.1 collective-permute-start.3
  21.1 1.5 collective-permute-start.4
  22.7 0.5 collective-permute-done.5.refs_5_
  23.1 1.5 collective-permute-start.10
  24.6 1.1 collective-permute-start.9
  25.7 0.1 stack.124.info_ref
  25.8 4.8 %collective-permute-done.3.refs_2_ = bf16[128,1152]{1,0:T(8,128)(2,1)S(1)} collective-permute-done((bf16[128,1152]{1,0:T(8,128)(2,1)S(1)}, bf16[128,1152]{1,0:T(8,128)(2,1)S(1)}, u32[]{:S(2)}, u32[]{:S(2)}) %collective-permute-start.3) | collective-permute-done | bytes 294944 | tf_op jit(solution)/shard_map/ppermute | solution.py:465
  30.6 31.8 %attention.1 = bf16[512,1152]{1,0:T(8,128)(2,1)} custom-call(s32[24]{0:T(128)S(1)} %stack.124.info_ref, bf16[128,1152]{1,0:T(8,128)(2,1)S(1)} %pad_maximum_fusion.refs_0_, bf16[128,1152]{1,0:T(8,128)(2,1)S(1)} %collective-permute-done.2.refs_1_, bf16[128,1152]{1,0:T(8,128)(2,1)S(1)} %collective-permute-done.3.refs_2_, ...), custom_call_target="tpu_custom_call" | custom-call | flops 12884901888 | bytes 6291456 | tf_op jit(solution)/shard_map/attention/pallas_call | solution.py:183
  62.4 7.2 %all-to-all-start = ((bf16[16,32,1152]{2,1,0:T(8,128)(2,1)}), bf16[16,32,1152]{2,1,0:T(8,128)(2,1)S(1)}, u32[]{:S(2)}, u32[]{:S(2)}) async-start(bf16[16,32,1152]{2,1,0:T(8,128)(2,1)} %bitcast.33), calls=%async_computation | async-start | bytes 2359296 | tf_op jit(solution)/shard_map/all_to_all | solution.py:474
  69.7 17.5 %all-to-all-done.x_ref = bf16[16,32,1152]{2,1,0:T(8,128)(2,1)S(1)} async-done(((bf16[16,32,1152]{2,1,0:T(8,128)(2,1)}), bf16[16,32,1152]{2,1,0:T(8,128)(2,1)S(1)}, u32[]{:S(2)}, u32[]{:S(2)}) %all-to-all-start) | async-done | bytes 1179680 | tf_op jit(solution)/shard_map/all_to_all | solution.py:474
  87.2 0.9 combine.1
  88.1 0.1 collective-permute-start.12
  88.1 0.8 collective-permute-start.13
  88.9 3.1 %collective-permute-start.14 = (bf16[2,32,512]{2,1,0:T(8,128)(2,1)S(1)}, bf16[2,32,512]{2,1,0:T(8,128)(2,1)S(1)}, u32[]{:S(2)}, u32[]{:S(2)}) collective-permute-start(bf16[2,32,512]{2,1,0:T(8,128)(2,1)S(1)} %combine.1), channel_id=1, source_target_pairs={{0,3},{1,2},{2,1},{3,0},{4,7},{5,6},{6,5},{7,4},{8,11},{9,10},{10,... | collective-permute-start | bytes 196616 | tf_op jit(solution)/shard_map/ppermute | solution.py:481
  92.1 0.8 collective-permute-done.13
  92.9 0.8 collective-permute-done.14
  93.7 0.8 broadcast_in_dim.62
  94.5 6.7 %all-to-all-start.1 = ((bf16[16,32,512]{2,1,0:T(8,128)(2,1)}), bf16[16,32,512]{2,1,0:T(8,128)(2,1)S(1)}, u32[]{:S(2)}, u32[]{:S(2)}) async-start(bf16[16,32,512]{2,1,0:T(8,128)(2,1)} %bitcast.39), calls=%async_computation.1 | async-start | bytes 1048576 | tf_op jit(solution)/shard_map/all_to_all | solution.py:485
  101.3 0.1 eq.88
  101.4 0.1 eq.84
  101.5 0.6 reduce-window.6
  102.1 0.2 slice_reduce_fusion
  102.4 7.8 %all-to-all-done.1 = bf16[16,32,512]{2,1,0:T(8,128)(2,1)S(1)} async-done(((bf16[16,32,512]{2,1,0:T(8,128)(2,1)}), bf16[16,32,512]{2,1,0:T(8,128)(2,1)S(1)}, u32[]{:S(2)}, u32[]{:S(2)}) %all-to-all-start.1) | async-done | bytes 524320 | tf_op jit(solution)/shard_map/all_to_all | solution.py:485
  110.2 0.4 project.1
  110.6 4.4 %collective-permute-start.15 = (bf16[256,512]{1,0:T(8,128)(2,1)S(1)}, bf16[256,512]{1,0:T(8,128)(2,1)S(1)}, u32[]{:S(2)}, u32[]{:S(2)}) collective-permute-start(bf16[256,512]{1,0:T(8,128)(2,1)S(1)} %get-tuple-element.8), channel_id=1, source_target_pairs={{0,8},{8,0},{1,9},{9,1},{2,10},{10,2},{3,11},{11,3},{4,12},{12,4},... | collective-permute-start | bytes 786440 | tf_op jit(solution)/shard_map/ppermute | solution.py:487
  115.1 0.1 fusion.7
  115.3 1.0 collective-permute-done.15
  116.2 0.8 add_convert_fusion
  117.0 3.4 %all-to-all-start.2 = ((bf16[8,32,512]{2,1,0:T(8,128)(2,1)}), bf16[8,32,512]{2,1,0:T(8,128)(2,1)S(1)}, u32[]{:S(2)}, u32[]{:S(2)}) async-start(bf16[8,32,512]{2,1,0:T(8,128)(2,1)} %bitcast.41), calls=%async_computation.2 | async-start | bytes 524288 | tf_op jit(solution)/shard_map/all_to_all | solution.py:489
  120.5 0.2 fusion.4
  120.7 7.1 %all-to-all-done.2 = bf16[8,32,512]{2,1,0:T(8,128)(2,1)S(1)} async-done(((bf16[8,32,512]{2,1,0:T(8,128)(2,1)}), bf16[8,32,512]{2,1,0:T(8,128)(2,1)S(1)}, u32[]{:S(2)}, u32[]{:S(2)}) %all-to-all-start.2) | async-done | bytes 262176 | tf_op jit(solution)/shard_map/all_to_all | solution.py:489
  127.8 1.1 convolution_convert_fusion
  128.9 4.2 %all-to-all-start.3 = ((bf16[16,24,512]{2,1,0:T(8,128)(2,1)}), bf16[16,24,512]{2,1,0:T(8,128)(2,1)S(1)}, u32[]{:S(2)}, u32[]{:S(2)}) async-start(bf16[16,24,512]{2,1,0:T(8,128)(2,1)} %bitcast.43), calls=%async_computation.3 | async-start | bytes 786432 | tf_op jit(solution)/shard_map/all_to_all | solution.py:507
  133.0 0.9 fusion.3
  134.0 0.6 slice.18
  135.2 6.2 %all-to-all-done.3 = bf16[16,24,512]{2,1,0:T(8,128)(2,1)S(1)} async-done(((bf16[16,24,512]{2,1,0:T(8,128)(2,1)}), bf16[16,24,512]{2,1,0:T(8,128)(2,1)S(1)}, u32[]{:S(2)}, u32[]{:S(2)}) %all-to-all-start.3) | async-done | bytes 393248 | tf_op jit(solution)/shard_map/all_to_all | solution.py:507
  141.4 0.6 broadcast_in_dim.65.gain_ref
  142.1 0.1 copy-done.2
  142.2 7.7 %gate_up.1 = bf16[384,3200]{1,0:T(8,128)(2,1)} custom-call(bf16[384,512]{1,0:T(8,128)(2,1)} %bitcast.96, bf16[384,384]{1,0:T(8,128)(2,1)} %copy-done.3, f32[8,512]{1,0:T(8,128)} %broadcast_in_dim.65.gain_ref, bf16[4,512,1536]{2,1,0:T(8,128)(2,1)} %gate_hbm.1, bf16[4,512,1536]{2,1,0:T(8,128)(2,1)} %up_hbm.1), custom_call_target="tpu_custom_call" | custom-call | flops 1207959552 | bytes 14942208 | tf_op jit(solution)/shard_map/gate_up/pallas_call | solution.py:304
  149.9 34.6 %all_to_all.35.x_ref = bf16[8,48,3200]{2,1,0:T(8,128)(2,1)S(1)} all-to-all(bf16[8,48,3200]{2,1,0:T(8,128)(2,1)} %bitcast.91), channel_id=1, replica_groups=mesh['zl'=2,'x'=4,'core'=2,'zh'=2,'yh'=2,'yl'=2] {'zh','yh','yl'}, dimensions={0} | all-to-all | bytes 4915200 | tf_op jit(solution)/shard_map/all_to_all | solution.py:519
  184.5 0.5 activate.1
  185.0 19.3 %all_to_all.36 = bf16[8,48,1536]{2,1,0:T(8,128)(2,1)} all-to-all(bf16[8,48,1536]{2,1,0:T(8,128)(2,1)S(1)} %activate.1), channel_id=1, replica_groups=mesh['zl'=2,'x'=4,'core'=2,'zh'=2,'yh'=2,'yl'=2] {'zh','yh','yl'}, dimensions={0} | all-to-all | bytes 2359296 | tf_op jit(solution)/shard_map/all_to_all | solution.py:521
  204.3 5.6 %down.1 = bf16[384,512]{1,0:T(8,128)(2,1)} custom-call(bf16[384,1536]{1,0:T(8,128)(2,1)} %bitcast.92, bf16[384,384]{1,0:T(8,128)(2,1)} %get-tuple-element.19.back_ref, bf16[4,1536,512]{2,1,0:T(8,128)(2,1)} %down_hbm.1), custom_call_target="tpu_custom_call" | custom-call | flops 603979776 | bytes 6291456 | tf_op jit(solution)/shard_map/down/pallas_call | solution.py:378
  209.9 8.0 %all-to-all-start.6 = ((bf16[16,24,512]{2,1,0:T(8,128)(2,1)}), bf16[16,24,512]{2,1,0:T(8,128)(2,1)S(1)}, u32[]{:S(2)}, u32[]{:S(2)}) async-start(bf16[16,24,512]{2,1,0:T(8,128)(2,1)} %bitcast.95), calls=%async_computation.6 | async-start | bytes 786432 | tf_op jit(solution)/shard_map/all_to_all | solution.py:523
  217.9 0.2 select_reduce_fusion
  218.1 8.0 %all-to-all-done.6 = bf16[16,24,512]{2,1,0:T(8,128)(2,1)S(1)} async-done(((bf16[16,24,512]{2,1,0:T(8,128)(2,1)}), bf16[16,24,512]{2,1,0:T(8,128)(2,1)S(1)}, u32[]{:S(2)}, u32[]{:S(2)}) %all-to-all-start.6) | async-done | bytes 393248 | tf_op jit(solution)/shard_map/all_to_all | solution.py:523
  226.1 0.2 fusion.11
  226.3 0.8 fusion.1
  (58 shorter events, 0.8 us)
Async XLA Ops:
  0.0 2.0 copy-start
  0.0 3.0 %copy-start.9 = (s32[32]{0:T(128)S(1)}, s32[32]{0:T(128)}, u32[]{:S(2)}) copy-start(s32[32]{0:T(128)} %param.17) | copy-start | bytes 388
  0.0 3.3 %copy-start.5 = (s32[32,64]{1,0:T(8,128)S(1)}, s32[32,64]{1,0:T(8,128)}, u32[]{:S(2)}) copy-start(s32[32,64]{1,0:T(8,128)} %param.16) | copy-start | bytes 24580
  4.0 4.5 %collective-permute-start = (bf16[32,1152]{1,0:T(8,128)(2,1)S(1)}, bf16[32,1152]{1,0:T(8,128)(2,1)S(1)}, u32[]{:S(2)}, u32[]{:S(2)}) collective-permute-start(bf16[32,1152]{1,0:T(8,128)(2,1)S(1)} %concatenate.17), channel_id=1, source_target_pairs={{0,8},{8,0},{1,9},{9,1},{2,10},{10,2},{3,11},{11,3},{4,12},{12,4},... | collective-permute-start | bytes 221192 | tf_op jit(solution)/shard_map/ppermute | solution.py:456
  5.5 14.5 %collective-permute-start.6 = (bf16[2,4,128,128]{3,2,1,0:T(8,128)(2,1)S(1)}, bf16[2,4,128,128]{3,2,1,0:T(8,128)(2,1)S(1)}, u32[]{:S(2)}, u32[]{:S(2)}) collective-permute-start(bf16[2,4,128,128]{3,2,1,0:T(8,128)(2,1)S(1)} %pad_maximum_fusion.3), channel_id=1, source_target_pairs={{0,3},{1,2},{2,1},{3,0},{4,7},{5,6},{6,5},{7,4},{8,11},{9,10},{10,... | collective-permute-start | bytes 786440 | tf_op jit(solution)/shard_map/ppermute | solution.py:438
  8.6 5.6 %collective-permute-start.1 = (bf16[64,1152]{1,0:T(8,128)(2,1)S(1)}, bf16[64,1152]{1,0:T(8,128)(2,1)S(1)}, u32[]{:S(2)}, u32[]{:S(2)}) collective-permute-start(bf16[64,1152]{1,0:T(8,128)(2,1)S(1)} %pad_maximum_fusion.5), channel_id=1, source_target_pairs={{0,64},{64,0},{1,65},{65,1},{2,66},{66,2},{3,67},{67,3},{4,68},{68... | collective-permute-start | bytes 442376 | tf_op jit(solution)/shard_map/ppermute | solution.py:458
  10.3 10.8 %collective-permute-start.7 = (bf16[2,4,128,128]{3,2,1,0:T(8,128)(2,1)S(1)}, bf16[2,4,128,128]{3,2,1,0:T(8,128)(2,1)S(1)}, u32[]{:S(2)}, u32[]{:S(2)}) collective-permute-start(bf16[2,4,128,128]{3,2,1,0:T(8,128)(2,1)S(1)} %pad_maximum_fusion.4), channel_id=1, source_target_pairs={{0,2},{1,3},{2,0},{3,1},{4,6},{5,7},{6,4},{7,5},{8,10},{9,11},{10,... | collective-permute-start | bytes 786440 | tf_op jit(solution)/shard_map/ppermute | solution.py:438
  11.3 11.8 %collective-permute-start.5 = (bf16[2,4,128,128]{3,2,1,0:T(8,128)(2,1)S(1)}, bf16[2,4,128,128]{3,2,1,0:T(8,128)(2,1)S(1)}, u32[]{:S(2)}, u32[]{:S(2)}) collective-permute-start(bf16[2,4,128,128]{3,2,1,0:T(8,128)(2,1)S(1)} %pad_maximum_fusion.2), channel_id=1, source_target_pairs={{0,1},{1,0},{2,3},{3,2},{4,5},{5,4},{6,7},{7,6},{8,9},{9,8},{10,11... | collective-permute-start | bytes 786440 | tf_op jit(solution)/shard_map/ppermute | solution.py:438
  14.2 10.4 %collective-permute-start.2 = (bf16[128,1152]{1,0:T(8,128)(2,1)S(1)}, bf16[128,1152]{1,0:T(8,128)(2,1)S(1)}, u32[]{:S(2)}, u32[]{:S(2)}) collective-permute-start(bf16[128,1152]{1,0:T(8,128)(2,1)S(1)} %pad_maximum_fusion.refs_0_), channel_id=1, source_target_pairs={{0,32},{16,48},{32,0},{48,16},{1,33},{17,49},{33,1},{49,17},{2,34}... | collective-permute-start | bytes 884744 | tf_op jit(solution)/shard_map/ppermute | solution.py:465
  17.1 7.5 %collective-permute-start.8 = (bf16[2,4,128,128]{3,2,1,0:T(8,128)(2,1)S(1)}, bf16[2,4,128,128]{3,2,1,0:T(8,128)(2,1)S(1)}, u32[]{:S(2)}, u32[]{:S(2)}) collective-permute-start(bf16[2,4,128,128]{3,2,1,0:T(8,128)(2,1)S(1)} %pad_maximum_fusion.1.refs_4_), channel_id=1, source_target_pairs={{0,8},{8,0},{1,9},{9,1},{2,10},{10,2},{3,11},{11,3},{4,12},{12,4},... | collective-permute-start | bytes 786440 | tf_op jit(solution)/shard_map/ppermute | solution.py:439
  20.0 10.6 %collective-permute-start.3 = (bf16[128,1152]{1,0:T(8,128)(2,1)S(1)}, bf16[128,1152]{1,0:T(8,128)(2,1)S(1)}, u32[]{:S(2)}, u32[]{:S(2)}) collective-permute-start(bf16[128,1152]{1,0:T(8,128)(2,1)S(1)} %pad_maximum_fusion.refs_0_), channel_id=1, source_target_pairs={{0,16},{16,32},{32,48},{48,0},{1,17},{17,33},{33,49},{49,1},{2,18}... | collective-permute-start | bytes 884744 | tf_op jit(solution)/shard_map/ppermute | solution.py:465
  21.1 9.5 %collective-permute-start.4 = (bf16[128,1152]{1,0:T(8,128)(2,1)S(1)}, bf16[128,1152]{1,0:T(8,128)(2,1)S(1)}, u32[]{:S(2)}, u32[]{:S(2)}) collective-permute-start(bf16[128,1152]{1,0:T(8,128)(2,1)S(1)} %pad_maximum_fusion.refs_0_), channel_id=1, source_target_pairs={{0,48},{16,0},{32,16},{48,32},{1,49},{17,1},{33,17},{49,33},{2,50}... | collective-permute-start | bytes 884744 | tf_op jit(solution)/shard_map/ppermute | solution.py:465
  23.1 7.4 %collective-permute-start.10 = (bf16[2,4,128,128]{3,2,1,0:T(8,128)(2,1)S(1)}, bf16[2,4,128,128]{3,2,1,0:T(8,128)(2,1)S(1)}, u32[]{:S(2)}, u32[]{:S(2)}) collective-permute-start(bf16[2,4,128,128]{3,2,1,0:T(8,128)(2,1)S(1)} %collective-permute-done.6.refs_6_), channel_id=1, source_target_pairs={{0,8},{8,0},{1,9},{9,1},{2,10},{10,2},{3,11},{11,3},{4,12},{12,4},... | collective-permute-start | bytes 786440 | tf_op jit(solution)/shard_map/ppermute | solution.py:439
  24.6 6.0 %collective-permute-start.11 = (bf16[2,4,128,128]{3,2,1,0:T(8,128)(2,1)S(1)}, bf16[2,4,128,128]{3,2,1,0:T(8,128)(2,1)S(1)}, u32[]{:S(2)}, u32[]{:S(2)}) collective-permute-start(bf16[2,4,128,128]{3,2,1,0:T(8,128)(2,1)S(1)} %collective-permute-done.7.refs_7_), channel_id=1, source_target_pairs={{0,8},{8,0},{1,9},{9,1},{2,10},{10,2},{3,11},{11,3},{4,12},{12,4},... | collective-permute-start | bytes 786440 | tf_op jit(solution)/shard_map/ppermute | solution.py:439
  24.6 6.0 %collective-permute-start.9 = (bf16[2,4,128,128]{3,2,1,0:T(8,128)(2,1)S(1)}, bf16[2,4,128,128]{3,2,1,0:T(8,128)(2,1)}, u32[]{:S(2)}, u32[]{:S(2)}) collective-permute-start(bf16[2,4,128,128]{3,2,1,0:T(8,128)(2,1)S(1)} %collective-permute-done.5.refs_5_), channel_id=1, source_target_pairs={{0,8},{8,0},{1,9},{9,1},{2,10},{10,2},{3,11},{11,3},{4,12},{12,4},... | collective-permute-start | bytes 786440 | tf_op jit(solution)/shard_map/ppermute | solution.py:439
  62.4 24.7 %all-to-all-start = ((bf16[16,32,1152]{2,1,0:T(8,128)(2,1)}), bf16[16,32,1152]{2,1,0:T(8,128)(2,1)S(1)}, u32[]{:S(2)}, u32[]{:S(2)}) async-start(bf16[16,32,1152]{2,1,0:T(8,128)(2,1)} %bitcast.33), calls=%async_computation | async-start | bytes 2359296 | tf_op jit(solution)/shard_map/all_to_all | solution.py:474
  69.7 31.6 %copy-start.6 = (s32[32,8]{0,1:T(8,128)S(1)}, s32[32,8]{0,1:T(8,128)}, u32[]{:S(2)}) copy-start(s32[32,8]{0,1:T(8,128)} %param.21) | copy-start | bytes 3076
  69.7 40.5 %copy-start.1 = (bf16[512,512]{1,0:T(8,128)(2,1)S(1)}, bf16[512,512]{1,0:T(8,128)(2,1)}, u32[]{:S(2)}) copy-start(bf16[512,512]{1,0:T(8,128)(2,1)} %weight_ref.1) | copy-start | bytes 1572868
  88.1 4.0 %collective-permute-start.12 = (bf16[2,32,512]{2,1,0:T(8,128)(2,1)S(1)}, bf16[2,32,512]{2,1,0:T(8,128)(2,1)S(1)}, u32[]{:S(2)}, u32[]{:S(2)}) collective-permute-start(bf16[2,32,512]{2,1,0:T(8,128)(2,1)S(1)} %combine.1), channel_id=1, source_target_pairs={{0,1},{1,0},{2,3},{3,2},{4,5},{5,4},{6,7},{7,6},{8,9},{9,8},{10,11... | collective-permute-start | bytes 196616 | tf_op jit(solution)/shard_map/ppermute | solution.py:481
  88.1 4.7 %collective-permute-start.13 = (bf16[2,32,512]{2,1,0:T(8,128)(2,1)S(1)}, bf16[2,32,512]{2,1,0:T(8,128)(2,1)S(1)}, u32[]{:S(2)}, u32[]{:S(2)}) collective-permute-start(bf16[2,32,512]{2,1,0:T(8,128)(2,1)S(1)} %combine.1), channel_id=1, source_target_pairs={{0,2},{1,3},{2,0},{3,1},{4,6},{5,7},{6,4},{7,5},{8,10},{9,11},{10,... | collective-permute-start | bytes 196616 | tf_op jit(solution)/shard_map/ppermute | solution.py:481
  88.9 4.7 %collective-permute-start.14 = (bf16[2,32,512]{2,1,0:T(8,128)(2,1)S(1)}, bf16[2,32,512]{2,1,0:T(8,128)(2,1)S(1)}, u32[]{:S(2)}, u32[]{:S(2)}) collective-permute-start(bf16[2,32,512]{2,1,0:T(8,128)(2,1)S(1)} %combine.1), channel_id=1, source_target_pairs={{0,3},{1,2},{2,1},{3,0},{4,7},{5,6},{6,5},{7,4},{8,11},{9,10},{10,... | collective-permute-start | bytes 196616 | tf_op jit(solution)/shard_map/ppermute | solution.py:481
  93.7 34.2 %copy-start.4 = (bf16[32,512]{1,0:T(8,128)(2,1)S(1)}, bf16[32,512]{1,0:T(8,128)(2,1)}, u32[]{:S(2)}) copy-start(bf16[32,512]{1,0:T(8,128)(2,1)} %param.19) | copy-start | bytes 98308
  94.5 15.7 %all-to-all-start.1 = ((bf16[16,32,512]{2,1,0:T(8,128)(2,1)}), bf16[16,32,512]{2,1,0:T(8,128)(2,1)S(1)}, u32[]{:S(2)}, u32[]{:S(2)}) async-start(bf16[16,32,512]{2,1,0:T(8,128)(2,1)} %bitcast.39), calls=%async_computation.1 | async-start | bytes 1048576 | tf_op jit(solution)/shard_map/all_to_all | solution.py:485
  110.2 25.0 %copy-start.8 = (f32[512]{0:T(512)S(1)}, f32[512]{0:T(512)}, u32[]{:S(2)}) copy-start(f32[512]{0:T(512)} %param.20) | copy-start | bytes 6148
  110.6 5.6 %collective-permute-start.15 = (bf16[256,512]{1,0:T(8,128)(2,1)S(1)}, bf16[256,512]{1,0:T(8,128)(2,1)S(1)}, u32[]{:S(2)}, u32[]{:S(2)}) collective-permute-start(bf16[256,512]{1,0:T(8,128)(2,1)S(1)} %get-tuple-element.8), channel_id=1, source_target_pairs={{0,8},{8,0},{1,9},{9,1},{2,10},{10,2},{3,11},{11,3},{4,12},{12,4},... | collective-permute-start | bytes 786440 | tf_op jit(solution)/shard_map/ppermute | solution.py:487
  117.0 10.8 %all-to-all-start.2 = ((bf16[8,32,512]{2,1,0:T(8,128)(2,1)}), bf16[8,32,512]{2,1,0:T(8,128)(2,1)S(1)}, u32[]{:S(2)}, u32[]{:S(2)}) async-start(bf16[8,32,512]{2,1,0:T(8,128)(2,1)} %bitcast.41), calls=%async_computation.2 | async-start | bytes 524288 | tf_op jit(solution)/shard_map/all_to_all | solution.py:489
  128.9 12.5 %all-to-all-start.3 = ((bf16[16,24,512]{2,1,0:T(8,128)(2,1)}), bf16[16,24,512]{2,1,0:T(8,128)(2,1)S(1)}, u32[]{:S(2)}, u32[]{:S(2)}) async-start(bf16[16,24,512]{2,1,0:T(8,128)(2,1)} %bitcast.43), calls=%async_computation.3 | async-start | bytes 786432 | tf_op jit(solution)/shard_map/all_to_all | solution.py:507
  134.0 8.1 %copy-start.3 = (bf16[384,384]{1,0:T(8,128)(2,1)}, bf16[384,384]{1,0:T(8,128)(2,1)S(1)}, u32[]{:S(2)}) copy-start(bf16[384,384]{1,0:T(8,128)(2,1)S(1)} %get-tuple-element.20.perm_ref) | copy-start | bytes 884740
  141.4 0.8 copy-start.2
  204.3 13.6 %copy-start.7 = (f32[32,8]{0,1:T(8,128)S(1)}, f32[32,8]{0,1:T(8,128)}, u32[]{:S(2)}) copy-start(f32[32,8]{0,1:T(8,128)} %param.22) | copy-start | bytes 3076
  209.9 16.3 %all-to-all-start.6 = ((bf16[16,24,512]{2,1,0:T(8,128)(2,1)}), bf16[16,24,512]{2,1,0:T(8,128)(2,1)S(1)}, u32[]{:S(2)}, u32[]{:S(2)}) async-start(bf16[16,24,512]{2,1,0:T(8,128)(2,1)} %bitcast.95), calls=%async_computation.6 | async-start | bytes 786432 | tf_op jit(solution)/shard_map/all_to_all | solution.py:523

commit v7 on v6

--- a/solution.py
+++ b/solution.py
@@ -474,12 +474,8 @@
     partial = lax.all_to_all(partial.reshape(n_blk, rows, width + LANES), group_axes, 0, 0)
     attended = combine(partial, heads)
 
-    gathered = jnp.zeros((KEY_VALUE_HEADS,) + attended.shape, attended.dtype)
-    gathered = lax.dynamic_update_index_in_dim(gathered, attended, kv_head, 0)
-    for step in range(1, KEY_VALUE_HEADS):
-        pairs = [(i, i ^ step) for i in range(KEY_VALUE_HEADS)]
-        piece = lax.ppermute(attended, ("yh", "yl"), pairs)
-        gathered = lax.dynamic_update_index_in_dim(gathered, piece, kv_head ^ step, 0)
+    gathered = jnp.broadcast_to(attended[None], (KEY_VALUE_HEADS,) + attended.shape)
+    gathered = lax.all_to_all(gathered, ("yh", "yl"), 0, 0)
     gathered = gathered.reshape(n_blk // 2, 1, rows, -1)
     gathered = jnp.broadcast_to(gathered, (n_blk // 2, 2) + gathered.shape[2:])
     gathered = lax.all_to_all(gathered.reshape((n_blk,) + gathered.shape[2:]), group_axes, 0, 0)

time: 228 us -> 227 us (level)
  blocking collectives: 53.9 us -> 86.6 us
  waiting for transfers between devices: 58.5 us -> 39.4 us
  starting transfers between devices: 54.7 us -> 40.9 us
    all_to_all x0 -> x2, blocking collectives: none -> 32.4 us  [the longest x1 24.5 us: per_device(): lax.all_to_all(partial.reshape(n_blk, rows, width + LANES), group_axes, 0...]
    all_to_all x1 -> x0, waiting for transfers between devices: 17.5 us -> none  [per_device(): lax.all_to_all(partial.reshape(n_blk, rows, width + LANES), group_axes, 0...]
    all_to_all x1 -> x0, starting transfers between devices: 7.22 us -> none  [per_device(): lax.all_to_all(partial.reshape(n_blk, rows, width + LANES), group_axes, 0...]
    ppermute x3 -> x0, starting transfers between devices: 3.93 us -> none  [per_device(): piece = lax.ppermute(attended, ('yh', 'yl'), pairs)]
    all_to_all x1, starting transfers between devices: 6.71 us -> 3.85 us  [per_device(): lax.all_to_all(gathered.reshape((n_blk,) + gathered.shape[2:]), group_axe...]
  transfers between devices with their start and end apart: 21 -> 17, of which waited for: 12 -> 9; matrix products, arithmetic and copies ran while one was open for 2% -> 2% of each run, Pallas kernels for 0% -> 0%
where the time goes in v7:
time: 227 us; the launch traced here: 226 us
  blocking collectives  86.6 us (38%)
  Pallas kernels  45.9 us (20%)
  starting transfers between devices  40.9 us (18%)
  waiting for transfers between devices  39.4 us (17%)
  local copies, waits for them, and re-layouts  6.36 us (3%)
  other arithmetic  3.03 us (1%)
    all_to_all x1, blocking collectives, per_device(): lax.all_to_all(sums.reshape(n_narrow, slots // n_narrow, -1), NARROW, 0, 0)  34.7 us
    pallas_call x1, Pallas kernels, attention(): pl.pallas_call(functools.partial(attention_kernel, heads), in_specs=[pl.B...  30.8 us
    all_to_all x1, blocking collectives, per_device(): lax.all_to_all(partial.reshape(n_blk, rows, width + LANES), group_axes, 0...  24.5 us
    all_to_all x1, blocking collectives, per_device(): activated = lax.all_to_all(activated, NARROW, 0, 0).reshape(slots, -1)  19.4 us
    all_to_all x1, waiting for transfers between devices, per_device(): lax.all_to_all(expert_out.reshape(n_blk, exp_dev * CAP, -1), BLK, 0, 0)  8 us
    all_to_all x1, blocking collectives, per_device(): gathered = lax.all_to_all(gathered, ('yh', 'yl'), 0, 0)  7.92 us
    all_to_all x1, waiting for transfers between devices, per_device(): lax.all_to_all(gathered.reshape((n_blk,) + gathered.shape[2:]), group_axe...  7.84 us
    pallas_call x1, Pallas kernels, gate_up(): pl.pallas_call(gate_up_kernel, in_specs=[vmem] * 3 + [anywhere] * 2, out_...  7.72 us
  transfers between devices with their start and end apart: 17, of which 9 were waited for; matrix products, arithmetic and copies ran while one was open for 2% of the time, Pallas kernels for 0%

profile of v7, /device:TPU:1, one launch (start us, length us, event | category | flops | bytes accessed | tf_op | source)
XLA Modules:
  0.0 225.8 jit_solution(4789937487588607990)
XLA Ops:
  0.0 1.4 dynamic-slice_bitcast_fusion
  1.5 0.6 slice.16
  2.1 0.1 reshape.146
  2.1 0.9 dynamic-slice_reduce_fusion.1
  3.1 0.1 copy.38
  3.2 0.1 copy.39
  4.0 0.1 concatenate.17
  4.1 1.5 collective-permute-start
  5.5 2.9 %collective-permute-start.6 = (bf16[2,4,128,128]{3,2,1,0:T(8,128)(2,1)S(1)}, bf16[2,4,128,128]{3,2,1,0:T(8,128)(2,1)S(1)}, u32[]{:S(2)}, u32[]{:S(2)}) collective-permute-start(bf16[2,4,128,128]{3,2,1,0:T(8,128)(2,1)S(1)} %pad_maximum_fusion.3), channel_id=1, source_target_pairs={{0,3},{1,2},{2,1},{3,0},{4,7},{5,6},{6,5},{7,4},{8,11},{9,10},{10,... | collective-permute-start | bytes 786440 | tf_op jit(solution)/shard_map/ppermute | solution.py:438
  8.5 0.1 concatenate.16
  8.6 1.7 collective-permute-start.1
  10.4 0.9 collective-permute-start.7
  11.3 0.5 collective-permute-start.5
  11.8 2.4 %collective-permute-done.1 = bf16[64,1152]{1,0:T(8,128)(2,1)S(1)} collective-permute-done((bf16[64,1152]{1,0:T(8,128)(2,1)S(1)}, bf16[64,1152]{1,0:T(8,128)(2,1)S(1)}, u32[]{:S(2)}, u32[]{:S(2)}) %collective-permute-start.1) | collective-permute-done | bytes 147488 | tf_op jit(solution)/shard_map/ppermute | solution.py:458
  14.2 2.8 %collective-permute-start.2 = (bf16[128,1152]{1,0:T(8,128)(2,1)S(1)}, bf16[128,1152]{1,0:T(8,128)(2,1)S(1)}, u32[]{:S(2)}, u32[]{:S(2)}) collective-permute-start(bf16[128,1152]{1,0:T(8,128)(2,1)S(1)} %pad_maximum_fusion.refs_0_), channel_id=1, source_target_pairs={{0,32},{16,48},{32,0},{48,16},{1,33},{17,49},{33,1},{49,17},{2,34}... | collective-permute-start | bytes 884744 | tf_op jit(solution)/shard_map/ppermute | solution.py:465
  17.1 1.3 collective-permute-start.8
  18.4 1.6 collective-permute-done.6.refs_6_
  20.0 1.1 collective-permute-start.3
  21.1 1.5 collective-permute-start.4
  22.7 0.5 collective-permute-done.5.refs_5_
  23.2 1.5 collective-permute-start.10
  24.6 0.0 collective-permute-start.11
  24.6 1.1 collective-permute-start.9
  25.7 0.1 stack.124.info_ref
  25.8 4.8 %collective-permute-done.3.refs_2_ = bf16[128,1152]{1,0:T(8,128)(2,1)S(1)} collective-permute-done((bf16[128,1152]{1,0:T(8,128)(2,1)S(1)}, bf16[128,1152]{1,0:T(8,128)(2,1)S(1)}, u32[]{:S(2)}, u32[]{:S(2)}) %collective-permute-start.3) | collective-permute-done | bytes 294944 | tf_op jit(solution)/shard_map/ppermute | solution.py:465
  30.6 30.8 %attention.1 = bf16[512,1152]{1,0:T(8,128)(2,1)S(1)} custom-call(s32[24]{0:T(128)S(1)} %stack.124.info_ref, bf16[128,1152]{1,0:T(8,128)(2,1)S(1)} %pad_maximum_fusion.refs_0_, bf16[128,1152]{1,0:T(8,128)(2,1)S(1)} %collective-permute-done.2.refs_1_, bf16[128,1152]{1,0:T(8,128)(2,1)S(1)} %collective-permute-done.3.refs_2_, ...), custom_call_target="tpu_custom_call" | custom-call | flops 12884901888 | bytes 6291456 | tf_op jit(solution)/shard_map/attention/pallas_call | solution.py:183
  61.4 24.5 %all_to_all.40.x_ref = bf16[16,32,1152]{2,1,0:T(8,128)(2,1)S(1)} all-to-all(bf16[16,32,1152]{2,1,0:T(8,128)(2,1)S(1)} %bitcast.83), channel_id=1, replica_groups=mesh['zl'=2,'x'=4,'core'=2,'zh'=2,'yh'=2,'yl'=2] {'zl','x','zh'}, dimensions={0} | all-to-all | bytes 2359296 | tf_op jit(solution)/shard_map/all_to_all | solution.py:474
  85.9 0.9 combine.1
  86.8 7.9 %all_to_all.41 = bf16[4,2,32,512]{3,2,1,0:T(8,128)(2,1)S(1)} all-to-all(bf16[4,2,32,512]{3,2,1,0:T(8,128)(2,1)S(1)} %broadcast_in_dim.26), channel_id=1, replica_groups=mesh['zl'=2,'x'=4,'core'=2,'zh'=2,'yh'=2,'yl'=2] {'yh','yl'}, dimensions={0} | all-to-all | bytes 524288 | tf_op jit(solution)/shard_map/all_to_all | solution.py:478
  94.8 0.9 broadcast_in_dim.48
  95.6 3.8 %all-to-all-start.2 = ((bf16[16,32,512]{2,1,0:T(8,128)(2,1)}), bf16[16,32,512]{2,1,0:T(8,128)(2,1)S(1)}, u32[]{:S(2)}, u32[]{:S(2)}) async-start(bf16[16,32,512]{2,1,0:T(8,128)(2,1)} %bitcast.35), calls=%async_computation.2 | async-start | bytes 1048576 | tf_op jit(solution)/shard_map/all_to_all | solution.py:481
  99.5 0.1 copy.42
  99.5 0.1 eq.88
  99.6 0.1 eq.84
  99.7 0.6 reduce-window.6
  100.4 0.2 slice_reduce_fusion
  100.6 7.8 %all-to-all-done.2 = bf16[16,32,512]{2,1,0:T(8,128)(2,1)S(1)} async-done(((bf16[16,32,512]{2,1,0:T(8,128)(2,1)}), bf16[16,32,512]{2,1,0:T(8,128)(2,1)S(1)}, u32[]{:S(2)}, u32[]{:S(2)}) %all-to-all-start.2) | async-done | bytes 524320 | tf_op jit(solution)/shard_map/all_to_all | solution.py:481
  108.4 0.4 project.1
  108.9 5.0 %collective-permute-start.12 = (bf16[256,512]{1,0:T(8,128)(2,1)S(1)}, bf16[256,512]{1,0:T(8,128)(2,1)S(1)}, u32[]{:S(2)}, u32[]{:S(2)}) collective-permute-start(bf16[256,512]{1,0:T(8,128)(2,1)S(1)} %get-tuple-element.8), channel_id=1, source_target_pairs={{0,8},{8,0},{1,9},{9,1},{2,10},{10,2},{3,11},{11,3},{4,12},{12,4},... | collective-permute-start | bytes 786440 | tf_op jit(solution)/shard_map/ppermute | solution.py:483
  113.8 0.1 fusion.7
  113.9 0.1 reduce_sum.31
  114.0 1.0 collective-permute-done.12
  115.0 0.8 add_convert_fusion
  115.8 3.4 %all-to-all-start.3 = ((bf16[8,32,512]{2,1,0:T(8,128)(2,1)}), bf16[8,32,512]{2,1,0:T(8,128)(2,1)S(1)}, u32[]{:S(2)}, u32[]{:S(2)}) async-start(bf16[8,32,512]{2,1,0:T(8,128)(2,1)} %bitcast.37), calls=%async_computation.3 | async-start | bytes 524288 | tf_op jit(solution)/shard_map/all_to_all | solution.py:485
  119.2 0.2 fusion.4
  119.4 7.1 %all-to-all-done.3 = bf16[8,32,512]{2,1,0:T(8,128)(2,1)S(1)} async-done(((bf16[8,32,512]{2,1,0:T(8,128)(2,1)}), bf16[8,32,512]{2,1,0:T(8,128)(2,1)S(1)}, u32[]{:S(2)}, u32[]{:S(2)}) %all-to-all-start.3) | async-done | bytes 262176 | tf_op jit(solution)/shard_map/all_to_all | solution.py:485
  126.6 1.1 convolution_convert_fusion
  127.6 4.2 %all-to-all-start.4 = ((bf16[16,24,512]{2,1,0:T(8,128)(2,1)}), bf16[16,24,512]{2,1,0:T(8,128)(2,1)S(1)}, u32[]{:S(2)}, u32[]{:S(2)}) async-start(bf16[16,24,512]{2,1,0:T(8,128)(2,1)} %bitcast.39), calls=%async_computation.4 | async-start | bytes 786432 | tf_op jit(solution)/shard_map/all_to_all | solution.py:503
  131.8 0.9 fusion.3
  132.7 0.6 slice.18
  134.0 6.2 %all-to-all-done.4 = bf16[16,24,512]{2,1,0:T(8,128)(2,1)S(1)} async-done(((bf16[16,24,512]{2,1,0:T(8,128)(2,1)}), bf16[16,24,512]{2,1,0:T(8,128)(2,1)S(1)}, u32[]{:S(2)}, u32[]{:S(2)}) %all-to-all-start.4) | async-done | bytes 393248 | tf_op jit(solution)/shard_map/all_to_all | solution.py:503
  140.2 0.6 broadcast_in_dim.51.gain_ref
  140.8 0.1 copy-done.2
  140.9 7.7 %gate_up.1 = bf16[384,3200]{1,0:T(8,128)(2,1)} custom-call(bf16[384,512]{1,0:T(8,128)(2,1)} %bitcast.89, bf16[384,384]{1,0:T(8,128)(2,1)} %copy-done.3, f32[8,512]{1,0:T(8,128)} %broadcast_in_dim.51.gain_ref, bf16[4,512,1536]{2,1,0:T(8,128)(2,1)} %gate_hbm.1, bf16[4,512,1536]{2,1,0:T(8,128)(2,1)} %up_hbm.1), custom_call_target="tpu_custom_call" | custom-call | flops 1207959552 | bytes 14942208 | tf_op jit(solution)/shard_map/gate_up/pallas_call | solution.py:304
  148.6 34.7 %all_to_all.42.x_ref = bf16[8,48,3200]{2,1,0:T(8,128)(2,1)S(1)} all-to-all(bf16[8,48,3200]{2,1,0:T(8,128)(2,1)} %bitcast.84), channel_id=1, replica_groups=mesh['zl'=2,'x'=4,'core'=2,'zh'=2,'yh'=2,'yl'=2] {'zh','yh','yl'}, dimensions={0} | all-to-all | bytes 4915200 | tf_op jit(solution)/shard_map/all_to_all | solution.py:515
  183.3 0.5 activate.1
  183.9 19.4 %all_to_all.43 = bf16[8,48,1536]{2,1,0:T(8,128)(2,1)} all-to-all(bf16[8,48,1536]{2,1,0:T(8,128)(2,1)S(1)} %activate.1), channel_id=1, replica_groups=mesh['zl'=2,'x'=4,'core'=2,'zh'=2,'yh'=2,'yl'=2] {'zh','yh','yl'}, dimensions={0} | all-to-all | bytes 2359296 | tf_op jit(solution)/shard_map/all_to_all | solution.py:517
  203.3 5.6 %down.1 = bf16[384,512]{1,0:T(8,128)(2,1)} custom-call(bf16[384,1536]{1,0:T(8,128)(2,1)} %bitcast.85, bf16[384,384]{1,0:T(8,128)(2,1)} %get-tuple-element.19.back_ref, bf16[4,1536,512]{2,1,0:T(8,128)(2,1)} %down_hbm.1), custom_call_target="tpu_custom_call" | custom-call | flops 603979776 | bytes 6291456 | tf_op jit(solution)/shard_map/down/pallas_call | solution.py:378
  208.9 7.7 %all-to-all-start.7 = ((bf16[16,24,512]{2,1,0:T(8,128)(2,1)}), bf16[16,24,512]{2,1,0:T(8,128)(2,1)S(1)}, u32[]{:S(2)}, u32[]{:S(2)}) async-start(bf16[16,24,512]{2,1,0:T(8,128)(2,1)} %bitcast.88), calls=%async_computation.7 | async-start | bytes 786432 | tf_op jit(solution)/shard_map/all_to_all | solution.py:519
  216.6 0.1 copy.46
  216.6 0.2 select_reduce_fusion
  216.8 8.0 %all-to-all-done.7 = bf16[16,24,512]{2,1,0:T(8,128)(2,1)S(1)} async-done(((bf16[16,24,512]{2,1,0:T(8,128)(2,1)}), bf16[16,24,512]{2,1,0:T(8,128)(2,1)S(1)}, u32[]{:S(2)}, u32[]{:S(2)}) %all-to-all-start.7) | async-done | bytes 393248 | tf_op jit(solution)/shard_map/all_to_all | solution.py:519
  224.8 0.2 fusion.11
  225.0 0.8 fusion.1
  (48 shorter events, 0.4 us)
Async XLA Ops:
  0.0 2.0 copy-start
  0.0 3.1 %copy-start.9 = (s32[32]{0:T(128)S(1)}, s32[32]{0:T(128)}, u32[]{:S(2)}) copy-start(s32[32]{0:T(128)} %param.17) | copy-start | bytes 388
  0.0 3.3 %copy-start.5 = (s32[32,64]{1,0:T(8,128)S(1)}, s32[32,64]{1,0:T(8,128)}, u32[]{:S(2)}) copy-start(s32[32,64]{1,0:T(8,128)} %param.16) | copy-start | bytes 24580
  4.1 4.5 %collective-permute-start = (bf16[32,1152]{1,0:T(8,128)(2,1)S(1)}, bf16[32,1152]{1,0:T(8,128)(2,1)S(1)}, u32[]{:S(2)}, u32[]{:S(2)}) collective-permute-start(bf16[32,1152]{1,0:T(8,128)(2,1)S(1)} %concatenate.17), channel_id=1, source_target_pairs={{0,8},{8,0},{1,9},{9,1},{2,10},{10,2},{3,11},{11,3},{4,12},{12,4},... | collective-permute-start | bytes 221192 | tf_op jit(solution)/shard_map/ppermute | solution.py:456
  5.5 14.4 %collective-permute-start.6 = (bf16[2,4,128,128]{3,2,1,0:T(8,128)(2,1)S(1)}, bf16[2,4,128,128]{3,2,1,0:T(8,128)(2,1)S(1)}, u32[]{:S(2)}, u32[]{:S(2)}) collective-permute-start(bf16[2,4,128,128]{3,2,1,0:T(8,128)(2,1)S(1)} %pad_maximum_fusion.3), channel_id=1, source_target_pairs={{0,3},{1,2},{2,1},{3,0},{4,7},{5,6},{6,5},{7,4},{8,11},{9,10},{10,... | collective-permute-start | bytes 786440 | tf_op jit(solution)/shard_map/ppermute | solution.py:438
  8.6 5.6 %collective-permute-start.1 = (bf16[64,1152]{1,0:T(8,128)(2,1)S(1)}, bf16[64,1152]{1,0:T(8,128)(2,1)S(1)}, u32[]{:S(2)}, u32[]{:S(2)}) collective-permute-start(bf16[64,1152]{1,0:T(8,128)(2,1)S(1)} %pad_maximum_fusion.5), channel_id=1, source_target_pairs={{0,64},{64,0},{1,65},{65,1},{2,66},{66,2},{3,67},{67,3},{4,68},{68... | collective-permute-start | bytes 442376 | tf_op jit(solution)/shard_map/ppermute | solution.py:458
  10.4 10.8 %collective-permute-start.7 = (bf16[2,4,128,128]{3,2,1,0:T(8,128)(2,1)S(1)}, bf16[2,4,128,128]{3,2,1,0:T(8,128)(2,1)S(1)}, u32[]{:S(2)}, u32[]{:S(2)}) collective-permute-start(bf16[2,4,128,128]{3,2,1,0:T(8,128)(2,1)S(1)} %pad_maximum_fusion.4), channel_id=1, source_target_pairs={{0,2},{1,3},{2,0},{3,1},{4,6},{5,7},{6,4},{7,5},{8,10},{9,11},{10,... | collective-permute-start | bytes 786440 | tf_op jit(solution)/shard_map/ppermute | solution.py:438
  11.3 11.8 %collective-permute-start.5 = (bf16[2,4,128,128]{3,2,1,0:T(8,128)(2,1)S(1)}, bf16[2,4,128,128]{3,2,1,0:T(8,128)(2,1)S(1)}, u32[]{:S(2)}, u32[]{:S(2)}) collective-permute-start(bf16[2,4,128,128]{3,2,1,0:T(8,128)(2,1)S(1)} %pad_maximum_fusion.2), channel_id=1, source_target_pairs={{0,1},{1,0},{2,3},{3,2},{4,5},{5,4},{6,7},{7,6},{8,9},{9,8},{10,11... | collective-permute-start | bytes 786440 | tf_op jit(solution)/shard_map/ppermute | solution.py:438
  14.2 10.4 %collective-permute-start.2 = (bf16[128,1152]{1,0:T(8,128)(2,1)S(1)}, bf16[128,1152]{1,0:T(8,128)(2,1)S(1)}, u32[]{:S(2)}, u32[]{:S(2)}) collective-permute-start(bf16[128,1152]{1,0:T(8,128)(2,1)S(1)} %pad_maximum_fusion.refs_0_), channel_id=1, source_target_pairs={{0,32},{16,48},{32,0},{48,16},{1,33},{17,49},{33,1},{49,17},{2,34}... | collective-permute-start | bytes 884744 | tf_op jit(solution)/shard_map/ppermute | solution.py:465
  17.1 7.5 %collective-permute-start.8 = (bf16[2,4,128,128]{3,2,1,0:T(8,128)(2,1)S(1)}, bf16[2,4,128,128]{3,2,1,0:T(8,128)(2,1)S(1)}, u32[]{:S(2)}, u32[]{:S(2)}) collective-permute-start(bf16[2,4,128,128]{3,2,1,0:T(8,128)(2,1)S(1)} %pad_maximum_fusion.1.refs_4_), channel_id=1, source_target_pairs={{0,8},{8,0},{1,9},{9,1},{2,10},{10,2},{3,11},{11,3},{4,12},{12,4},... | collective-permute-start | bytes 786440 | tf_op jit(solution)/shard_map/ppermute | solution.py:439
  20.0 10.6 %collective-permute-start.3 = (bf16[128,1152]{1,0:T(8,128)(2,1)S(1)}, bf16[128,1152]{1,0:T(8,128)(2,1)S(1)}, u32[]{:S(2)}, u32[]{:S(2)}) collective-permute-start(bf16[128,1152]{1,0:T(8,128)(2,1)S(1)} %pad_maximum_fusion.refs_0_), channel_id=1, source_target_pairs={{0,16},{16,32},{32,48},{48,0},{1,17},{17,33},{33,49},{49,1},{2,18}... | collective-permute-start | bytes 884744 | tf_op jit(solution)/shard_map/ppermute | solution.py:465
  21.1 9.5 %collective-permute-start.4 = (bf16[128,1152]{1,0:T(8,128)(2,1)S(1)}, bf16[128,1152]{1,0:T(8,128)(2,1)S(1)}, u32[]{:S(2)}, u32[]{:S(2)}) collective-permute-start(bf16[128,1152]{1,0:T(8,128)(2,1)S(1)} %pad_maximum_fusion.refs_0_), channel_id=1, source_target_pairs={{0,48},{16,0},{32,16},{48,32},{1,49},{17,1},{33,17},{49,33},{2,50}... | collective-permute-start | bytes 884744 | tf_op jit(solution)/shard_map/ppermute | solution.py:465
  23.2 7.4 %collective-permute-start.10 = (bf16[2,4,128,128]{3,2,1,0:T(8,128)(2,1)S(1)}, bf16[2,4,128,128]{3,2,1,0:T(8,128)(2,1)S(1)}, u32[]{:S(2)}, u32[]{:S(2)}) collective-permute-start(bf16[2,4,128,128]{3,2,1,0:T(8,128)(2,1)S(1)} %collective-permute-done.6.refs_6_), channel_id=1, source_target_pairs={{0,8},{8,0},{1,9},{9,1},{2,10},{10,2},{3,11},{11,3},{4,12},{12,4},... | collective-permute-start | bytes 786440 | tf_op jit(solution)/shard_map/ppermute | solution.py:439
  24.6 6.0 %collective-permute-start.11 = (bf16[2,4,128,128]{3,2,1,0:T(8,128)(2,1)S(1)}, bf16[2,4,128,128]{3,2,1,0:T(8,128)(2,1)S(1)}, u32[]{:S(2)}, u32[]{:S(2)}) collective-permute-start(bf16[2,4,128,128]{3,2,1,0:T(8,128)(2,1)S(1)} %collective-permute-done.7.refs_7_), channel_id=1, source_target_pairs={{0,8},{8,0},{1,9},{9,1},{2,10},{10,2},{3,11},{11,3},{4,12},{12,4},... | collective-permute-start | bytes 786440 | tf_op jit(solution)/shard_map/ppermute | solution.py:439
  24.6 6.0 %collective-permute-start.9 = (bf16[2,4,128,128]{3,2,1,0:T(8,128)(2,1)S(1)}, bf16[2,4,128,128]{3,2,1,0:T(8,128)(2,1)}, u32[]{:S(2)}, u32[]{:S(2)}) collective-permute-start(bf16[2,4,128,128]{3,2,1,0:T(8,128)(2,1)S(1)} %collective-permute-done.5.refs_5_), channel_id=1, source_target_pairs={{0,8},{8,0},{1,9},{9,1},{2,10},{10,2},{3,11},{11,3},{4,12},{12,4},... | collective-permute-start | bytes 786440 | tf_op jit(solution)/shard_map/ppermute | solution.py:439
  85.9 13.5 %copy-start.6 = (s32[32,8]{0,1:T(8,128)S(1)}, s32[32,8]{0,1:T(8,128)}, u32[]{:S(2)}) copy-start(s32[32,8]{0,1:T(8,128)} %param.21) | copy-start | bytes 3076
  85.9 22.5 %copy-start.1 = (bf16[512,512]{1,0:T(8,128)(2,1)S(1)}, bf16[512,512]{1,0:T(8,128)(2,1)}, u32[]{:S(2)}) copy-start(bf16[512,512]{1,0:T(8,128)(2,1)} %weight_ref.1) | copy-start | bytes 1572868
  94.8 31.8 %copy-start.4 = (bf16[32,512]{1,0:T(8,128)(2,1)S(1)}, bf16[32,512]{1,0:T(8,128)(2,1)}, u32[]{:S(2)}) copy-start(bf16[32,512]{1,0:T(8,128)(2,1)} %param.19) | copy-start | bytes 98308
  95.6 12.8 %all-to-all-start.2 = ((bf16[16,32,512]{2,1,0:T(8,128)(2,1)}), bf16[16,32,512]{2,1,0:T(8,128)(2,1)S(1)}, u32[]{:S(2)}, u32[]{:S(2)}) async-start(bf16[16,32,512]{2,1,0:T(8,128)(2,1)} %bitcast.35), calls=%async_computation.2 | async-start | bytes 1048576 | tf_op jit(solution)/shard_map/all_to_all | solution.py:481
  108.4 25.5 %copy-start.8 = (f32[512]{0:T(512)S(1)}, f32[512]{0:T(512)}, u32[]{:S(2)}) copy-start(f32[512]{0:T(512)} %param.20) | copy-start | bytes 6148
  108.9 6.1 %collective-permute-start.12 = (bf16[256,512]{1,0:T(8,128)(2,1)S(1)}, bf16[256,512]{1,0:T(8,128)(2,1)S(1)}, u32[]{:S(2)}, u32[]{:S(2)}) collective-permute-start(bf16[256,512]{1,0:T(8,128)(2,1)S(1)} %get-tuple-element.8), channel_id=1, source_target_pairs={{0,8},{8,0},{1,9},{9,1},{2,10},{10,2},{3,11},{11,3},{4,12},{12,4},... | collective-permute-start | bytes 786440 | tf_op jit(solution)/shard_map/ppermute | solution.py:483
  115.8 10.8 %all-to-all-start.3 = ((bf16[8,32,512]{2,1,0:T(8,128)(2,1)}), bf16[8,32,512]{2,1,0:T(8,128)(2,1)S(1)}, u32[]{:S(2)}, u32[]{:S(2)}) async-start(bf16[8,32,512]{2,1,0:T(8,128)(2,1)} %bitcast.37), calls=%async_computation.3 | async-start | bytes 524288 | tf_op jit(solution)/shard_map/all_to_all | solution.py:485
  127.6 12.5 %all-to-all-start.4 = ((bf16[16,24,512]{2,1,0:T(8,128)(2,1)}), bf16[16,24,512]{2,1,0:T(8,128)(2,1)S(1)}, u32[]{:S(2)}, u32[]{:S(2)}) async-start(bf16[16,24,512]{2,1,0:T(8,128)(2,1)} %bitcast.39), calls=%async_computation.4 | async-start | bytes 786432 | tf_op jit(solution)/shard_map/all_to_all | solution.py:503
  132.7 8.1 %copy-start.3 = (bf16[384,384]{1,0:T(8,128)(2,1)}, bf16[384,384]{1,0:T(8,128)(2,1)S(1)}, u32[]{:S(2)}) copy-start(bf16[384,384]{1,0:T(8,128)(2,1)S(1)} %get-tuple-element.20.perm_ref) | copy-start | bytes 884740
  140.2 0.7 copy-start.2
  203.3 13.3 %copy-start.7 = (f32[32,8]{0,1:T(8,128)S(1)}, f32[32,8]{0,1:T(8,128)}, u32[]{:S(2)}) copy-start(f32[32,8]{0,1:T(8,128)} %param.22) | copy-start | bytes 3076
  208.9 16.0 %all-to-all-start.7 = ((bf16[16,24,512]{2,1,0:T(8,128)(2,1)}), bf16[16,24,512]{2,1,0:T(8,128)(2,1)S(1)}, u32[]{:S(2)}, u32[]{:S(2)}) async-start(bf16[16,24,512]{2,1,0:T(8,128)(2,1)} %bitcast.88), calls=%async_computation.7 | async-start | bytes 786432 | tf_op jit(solution)/shard_map/all_to_all | solution.py:519
